TPU v7x, 128 devices: a whole 4x4x4 slice. The times are simulated.
128 devices in a mesh: dp: 16 (over y_lo, z, core), tensor: 8 (over x, y_hi).
Axes of the slice: x: 4, y: 4 (y_hi: 2, y_lo: 2; y = y_hi * 2 + y_lo), z: 4, core: 2. Of those that a mesh axis runs over, the one named last changes fastest.
Arguments:
- query: bfloat16 [4, 2048, 4096], P(None, 'dp', 'tensor'), may hold values from -61 to 61
- new_keys: bfloat16 [4, 2048, 1024], P(None, 'dp', 'tensor'), may hold values from -6 to 6
- new_values: bfloat16 [4, 2048, 1024], P(None, 'dp', 'tensor'), may hold values from -6 to 6
- cache_keys: bfloat16 [2048, 64, 1024], P('dp', None, 'tensor'), may hold values from -3 to 3
- cache_values: bfloat16 [2048, 64, 1024], P('dp', None, 'tensor'), may hold values from -6 to 6
- cache_lengths: int32 [2048], P('dp'), may hold values from 2 to 64, as said below
- residual: bfloat16 [4, 2048, 8192], P(None, 'dp', 'tensor'), may hold values from -6 to 6
- out_weight: bfloat16 [4096, 8192], P('tensor'), may hold values from -0.09375 to 0.09375
- bridge_weight: bfloat16 [8192, 3584], P('tensor'), may hold values from -0.0625 to 0.0625
- text_table: bfloat16 [3584, 76032], P(('dp', 'tensor')), may hold values from -45 to 45
- codec_table: bfloat16 [3584, 8448], P(('dp', 'tensor')), may hold values from -45 to 45
- tokens: int32 [4, 2048], P(None, 'dp'), may hold values from 0 to 76031
- frames: int32 [4, 2048], P(None, 'dp'), may hold values from 0 to 8447
- talk_gain: bfloat16 [3584], replicated, may hold values from 0.099609375 to 1.8984375
Outputs:
- thinker_hidden: bfloat16 [4, 2048, 8192], P(None, 'dp', 'tensor')
- talker_input: bfloat16 [4, 2048, 3584], P(None, ('dp', 'tensor'))
Inputs may be any that keep to these rules, and one draw needn't show every extreme that they name: `cache_lengths`: stream 0 has all 64 positions valid.
All inputs are finite; a program needn't handle non-finite values.
Results may differ from a plain program's by a relative error of at most 0.0035.
Values may be sent and summed in bfloat16 or wider, within the bound.
No kernel may reach another device: no remote copies, remote signals or barrier semaphores. Data moves between devices by JAX's collectives and lax.ppermute only.
A program may use at most 192 MiB of HBM per device.

v0:
```python
import jax
import jax.numpy as jnp
from jax import lax
from jax.sharding import PartitionSpec as P

QH = 32
KVH = 8
HD = 128
CAP = 64


def local(
    query,
    new_keys,
    new_values,
    cache_keys,
    cache_values,
    cache_lengths,
    residual,
    out_weight,
    bridge_weight,
    text_table,
    codec_table,
    tokens,
    frames,
    talk_gain,
):
    steps, streams_here, query_width = query.shape
    width = residual.shape[2]
    group = QH // KVH
    kv_local = new_keys.shape[2] // HD
    scale = 1.0 / HD**0.5
    token_all, frame_all = (
        lax.all_gather(tokens, "dp", axis=1, tiled=True),
        lax.all_gather(frames, "dp", axis=1, tiled=True),
    )
    cached_k = cache_keys.reshape(streams_here, CAP, kv_local, HD)
    cached_v = cache_values.reshape(streams_here, CAP, kv_local, HD)
    fresh_k = new_keys.reshape(steps, streams_here, kv_local, HD)
    fresh_v = new_values.reshape(steps, streams_here, kv_local, HD)
    positions = jnp.arange(CAP, dtype=jnp.int32)
    valid = positions[None, :] < cache_lengths[:, None]
    gain = talk_gain.astype(jnp.float32)
    hidden_rows = []
    talker_rows = []
    for step in range(steps):
        queries = query[step].reshape(streams_here, kv_local, group, HD)
        score_c = (
            jnp.einsum("skgd,spkd->skgp", queries, cached_k, preferred_element_type=jnp.float32)
            * scale
        )
        score_c = jnp.where(valid[:, None, None, :], score_c, -1e30)
        score_n = (
            jnp.einsum(
                "skgd,uskd->skgu", queries, fresh_k[: step + 1], preferred_element_type=jnp.float32
            )
            * scale
        )
        top = jnp.maximum(jnp.max(score_c, axis=-1), jnp.max(score_n, axis=-1))[..., None]
        exp_c = jnp.exp(score_c - top)
        exp_n = jnp.exp(score_n - top)
        total = jnp.sum(exp_c, axis=-1, keepdims=True) + jnp.sum(exp_n, axis=-1, keepdims=True)
        weight_c = (exp_c / total).astype(jnp.bfloat16)
        weight_n = (exp_n / total).astype(jnp.bfloat16)
        attended = jnp.einsum(
            "skgp,spkd->skgd", weight_c, cached_v, preferred_element_type=jnp.float32
        )
        attended = attended + jnp.einsum(
            "skgu,uskd->skgd", weight_n, fresh_v[: step + 1], preferred_element_type=jnp.float32
        )
        attended = attended.astype(jnp.bfloat16).reshape(streams_here, query_width)
        full = lax.psum(jnp.dot(attended, out_weight, preferred_element_type=jnp.float32), "tensor")
        share = lax.dynamic_slice_in_dim(full, lax.axis_index("tensor") * width, width, 1)
        hidden = (residual[step].astype(jnp.float32) + share).astype(jnp.bfloat16)
        bridged = lax.psum_scatter(
            jnp.dot(hidden, bridge_weight, preferred_element_type=jnp.float32),
            "tensor",
            scatter_dimension=0,
            tiled=True,
        )
        text_cols = jnp.take(text_table, token_all[step], axis=1)
        codec_cols = jnp.take(codec_table, frame_all[step], axis=1)
        text_rows, codec_rows = (
            lax.all_to_all(text_cols, ("dp", "tensor"), split_axis=1, concat_axis=0, tiled=True),
            lax.all_to_all(codec_cols, ("dp", "tensor"), split_axis=1, concat_axis=0, tiled=True),
        )
        mixed = bridged + text_rows.T.astype(jnp.float32) + codec_rows.T.astype(jnp.float32)
        normed = mixed * lax.rsqrt(jnp.mean(mixed * mixed, axis=-1, keepdims=True) + 1e-06)
        talker_rows.append((normed * gain).astype(jnp.bfloat16))
        hidden_rows.append(hidden)
    return (jnp.stack(hidden_rows), jnp.stack(talker_rows))


def solution(mesh):
    in_specs = (
        P(None, "dp", "tensor"),
        P(None, "dp", "tensor"),
        P(None, "dp", "tensor"),
        P("dp", None, "tensor"),
        P("dp", None, "tensor"),
        P("dp"),
        P(None, "dp", "tensor"),
        P("tensor", None),
        P("tensor", None),
        P(("dp", "tensor"), None),
        P(("dp", "tensor"), None),
        P(None, "dp"),
        P(None, "dp"),
        P(),
    )
    out_specs = (P(None, "dp", "tensor"), P(None, ("dp", "tensor"), None))
    return jax.shard_map(local, mesh=mesh, in_specs=in_specs, out_specs=out_specs, check_vma=False)
```

profile of v0, /device:TPU:0, one launch (start us, length us, event | category | flops | bytes accessed | tf_op | source)
XLA Modules:
  0.0 1059.0 jit_solution(14642954507678191430)
XLA Ops:
  47.1 6.6 fusion.30
  53.7 663.3 %all-reduce.3.cloned.1.call-done = (f32[128,8192]{1,0:T(8,128)}, f32[128,8192]{1,0:T(8,128)}, f32[128,8192]{1,0:T(8,128)}, f32[128,8192]{1,0:T(8,128)}) async-done(((f32[128,8192]{1,0:T(8,128)}, f32[128,8192]{1,0:T(8,128)}, f32[128,8192]{1,0:T(8,128)}, f32[128,8192]{1,0:T(8,128)}), (f32[128,8192]{1,0:T(8,128)}, f32[128,8192]{1,0:T(8,128)}, f32[128,8192]{1,0:T(8,128)}, ...) | async-done | bytes 16777232 | tf_op jit(solution)/shard_map/psum | solution.py:72
  718.9 5.8 fusion.84
  724.8 15.7 %copy.128 = bf16[28,76032]{0,1:T(8,128)(2,1)} copy(bf16[28,76032]{1,0:T(8,128)(2,1)} %param.27) | data formatting | bytes 8515584 | tf_op args[9]
  740.5 19.1 %all_gather.6 = s32[4,2048]{1,0:T(4,128)S(1)} all-gather(s32[4,128]{1,0:T(4,128)S(1)} %copy-done.22), channel_id=1, replica_groups=mesh['dp'=16,'tensor'=8] {'dp'}, dimensions={1}, use_global_device_ids=true | all-gather | bytes 34816 | tf_op jit(solution)/shard_map/all_gather | solution.py:34
  759.6 14.8 %gather_fusion.6 = bf16[2048,28]{1,0:T(8,128)(2,1)S(1)} fusion(bf16[28,76032]{0,1:T(8,128)(2,1)} %copy.128, s32[2048]{0:T(1024)S(1)} %fusion.64), kind=kCustom, calls=%fused_computation.4.clone | custom fusion | bytes 237568 | tf_op jit(solution)/shard_map/jit(_take)/gather | solution.py:81
  776.0 14.3 %all-to-all-start.6 = ((bf16[128,2,224]{2,1,0:T(2,128)(2,1)}), bf16[128,2,224]{2,1,0:T(2,128)(2,1)S(1)}, u32[]{:S(2)}, u32[]{:S(2)}) async-start(bf16[128,2,224]{2,1,0:T(2,128)(2,1)} %reshape.528), calls=%async_computation.10 | async-start | bytes 262144 | tf_op jit(solution)/shard_map/all_to_all | solution.py:84
  792.3 19.8 %all_gather.7 = s32[4,2048]{1,0:T(4,128)S(1)} all-gather(s32[4,128]{1,0:T(4,128)S(1)} %copy-done.23), channel_id=1, replica_groups=mesh['dp'=16,'tensor'=8] {'dp'}, dimensions={1}, use_global_device_ids=true | all-gather | bytes 34816 | tf_op jit(solution)/shard_map/all_gather | solution.py:35
  818.0 7.5 gather_fusion.7
  827.1 14.7 %gather_fusion.4 = bf16[2048,28]{1,0:T(8,128)(2,1)S(1)} fusion(bf16[28,76032]{0,1:T(8,128)(2,1)} %copy.128, s32[2048]{0:T(1024)S(1)} %fusion.62), kind=kCustom, calls=%fused_computation.3.clone | custom fusion | bytes 237568 | tf_op jit(solution)/shard_map/jit(_take)/gather | solution.py:81
  843.4 7.5 gather_fusion.5
  850.9 14.7 %gather_fusion.2 = bf16[2048,28]{1,0:T(8,128)(2,1)S(1)} fusion(bf16[28,76032]{0,1:T(8,128)(2,1)} %copy.128, s32[2048]{0:T(1024)S(1)} %fusion.60), kind=kCustom, calls=%fused_computation.2.clone | custom fusion | bytes 237568 | tf_op jit(solution)/shard_map/jit(_take)/gather | solution.py:81
  865.6 7.7 gather_fusion.3
  873.3 5.5 fusion.82
  879.9 14.7 %gather_fusion = bf16[2048,28]{1,0:T(8,128)(2,1)S(1)} fusion(bf16[28,76032]{0,1:T(8,128)(2,1)} %copy.128, s32[2048]{0:T(1024)S(1)} %fusion.58), kind=kCustom, calls=%fused_computation.clone | custom fusion | bytes 237568 | tf_op jit(solution)/shard_map/jit(_take)/gather | solution.py:81
  894.6 7.3 all-to-all-start.7
  902.0 10.2 all-to-all-done.7
  931.9 7.5 gather_fusion.1
  941.4 7.7 all-to-all-start.2
  949.2 9.5 all-to-all-done.2
  963.4 5.5 fusion.81
  973.7 6.1 all-to-all-start
  989.2 6.1 all-to-all-start.1
  1034.4 13.6 %reduce-scatter.5.cloned.1.call-done = f32[16,3584]{1,0:T(8,128)} async-done(((f32[128,3584]{1,0:T(8,128)}), f32[16,3584]{1,0:T(8,128)}) %reduce-scatter.5.cloned.1.call-update) | async-done | bytes 229392 | tf_op jit(solution)/shard_map/reduce_scatter | solution.py:75
  (205 shorter events, 138.8 us)
Async XLA Ops:
  7.2 20.3 %copy-start = (bf16[128,64,128]{2,1,0:T(8,128)(2,1)S(1)}, bf16[128,64,128]{2,1,0:T(8,128)(2,1)}, u32[]{:S(2)}) copy-start(bf16[128,64,128]{2,1,0:T(8,128)(2,1)} %param.22) | copy-start | bytes 6291460
  7.2 709.9 %all-reduce.3.cloned.1.call-start = ((), (), s32[]{:S(2)}) async-start(), calls=%async_computation.16 | async-start | bytes 33554432 | tf_op jit(solution)/shard_map/psum | solution.py:72
  12.6 9.7 copy-start.14
  19.4 7.5 copy-start.19
  53.7 663.4 %copy-start.11 = (bf16[4,128,1024]{2,1,0:T(8,128)(2,1)S(1)}, bf16[4,128,1024]{2,1,0:T(8,128)(2,1)}, u32[]{:S(2)}) copy-start(bf16[4,128,1024]{2,1,0:T(8,128)(2,1)} %param.24) | copy-start | bytes 3145732
  53.7 976.8 %reduce-scatter.11.cloned.1.call-start = ((), (), s32[]{:S(2)}) async-start(), calls=%async_computation.15 | async-start | bytes 2064384 | tf_op jit(solution)/shard_map/reduce_scatter | solution.py:75
  718.9 93.1 %copy-start.4 = (bf16[128,1024]{1,0:T(8,128)(2,1)}, bf16[128,1024]{1,0:T(8,128)(2,1)S(1)}, u32[]{:S(2)}) copy-start(bf16[128,1024]{1,0:T(8,128)(2,1)S(1)} %get-tuple-element.10) | copy-start | bytes 786436
  718.9 154.4 %copy-start.6 = (bf16[128,1024]{1,0:T(8,128)(2,1)}, bf16[128,1024]{1,0:T(8,128)(2,1)S(1)}, u32[]{:S(2)}) copy-start(bf16[128,1024]{1,0:T(8,128)(2,1)S(1)} %get-tuple-element.11) | copy-start | bytes 786436
  724.7 15.8 %copy-start.22 = (s32[4,128]{1,0:T(4,128)S(1)}, s32[4,128]{1,0:T(4,128)}, u32[]{:S(2)}) copy-start(s32[4,128]{1,0:T(4,128)} %param.29) | copy-start | bytes 6148
  724.8 65.6 %copy-start.12 = (bf16[28,8448]{1,0:T(8,128)(2,1)S(1)}, bf16[28,8448]{1,0:T(8,128)(2,1)}, u32[]{:S(2)}) copy-start(bf16[28,8448]{1,0:T(8,128)(2,1)} %param.28) | copy-start | bytes 1419268
  740.5 51.8 %copy-start.23 = (s32[4,128]{1,0:T(4,128)S(1)}, s32[4,128]{1,0:T(4,128)}, u32[]{:S(2)}) copy-start(s32[4,128]{1,0:T(4,128)} %param.30) | copy-start | bytes 6148
  776.0 118.7 %all-to-all-start.6 = ((bf16[128,2,224]{2,1,0:T(2,128)(2,1)}), bf16[128,2,224]{2,1,0:T(2,128)(2,1)S(1)}, u32[]{:S(2)}, u32[]{:S(2)}) async-start(bf16[128,2,224]{2,1,0:T(2,128)(2,1)} %reshape.528), calls=%async_computation.10 | async-start | bytes 262144 | tf_op jit(solution)/shard_map/all_to_all | solution.py:84
  790.3 241.4 %reduce-scatter.9.cloned.1.call-start = ((), (), s32[]{:S(2)}) async-start(), calls=%async_computation.14 | async-start | bytes 2064384 | tf_op jit(solution)/shard_map/reduce_scatter | solution.py:75
  817.5 215.4 %reduce-scatter.7.cloned.1.call-start = ((), (), s32[]{:S(2)}) async-start(), calls=%async_computation.13 | async-start | bytes 2064384 | tf_op jit(solution)/shard_map/reduce_scatter | solution.py:75
  894.6 17.6 %all-to-all-start.7 = ((bf16[128,2,224]{2,1,0:T(2,128)(2,1)}), bf16[128,2,224]{2,1,0:T(2,128)(2,1)S(1)}, u32[]{:S(2)}, u32[]{:S(2)}) async-start(bf16[128,2,224]{2,1,0:T(2,128)(2,1)} %reshape.526), calls=%async_computation.11 | async-start | bytes 262144 | tf_op jit(solution)/shard_map/all_to_all | solution.py:85
  912.2 14.4 %all-to-all-start.4 = ((bf16[128,2,224]{2,1,0:T(2,128)(2,1)}), bf16[128,2,224]{2,1,0:T(2,128)(2,1)S(1)}, u32[]{:S(2)}, u32[]{:S(2)}) async-start(bf16[128,2,224]{2,1,0:T(2,128)(2,1)} %reshape.532), calls=%async_computation.7 | async-start | bytes 262144 | tf_op jit(solution)/shard_map/all_to_all | solution.py:84
  926.7 14.7 %all-to-all-start.5 = ((bf16[128,2,224]{2,1,0:T(2,128)(2,1)}), bf16[128,2,224]{2,1,0:T(2,128)(2,1)S(1)}, u32[]{:S(2)}, u32[]{:S(2)}) async-start(bf16[128,2,224]{2,1,0:T(2,128)(2,1)} %reshape.530), calls=%async_computation.8 | async-start | bytes 262144 | tf_op jit(solution)/shard_map/all_to_all | solution.py:85
  941.4 17.3 %all-to-all-start.2 = ((bf16[128,2,224]{2,1,0:T(2,128)(2,1)}), bf16[128,2,224]{2,1,0:T(2,128)(2,1)S(1)}, u32[]{:S(2)}, u32[]{:S(2)}) async-start(bf16[128,2,224]{2,1,0:T(2,128)(2,1)} %reshape.536), calls=%async_computation.4 | async-start | bytes 262144 | tf_op jit(solution)/shard_map/all_to_all | solution.py:84
  958.7 14.4 %all-to-all-start.3 = ((bf16[128,2,224]{2,1,0:T(2,128)(2,1)}), bf16[128,2,224]{2,1,0:T(2,128)(2,1)S(1)}, u32[]{:S(2)}, u32[]{:S(2)}) async-start(bf16[128,2,224]{2,1,0:T(2,128)(2,1)} %reshape.534), calls=%async_computation.5 | async-start | bytes 262144 | tf_op jit(solution)/shard_map/all_to_all | solution.py:85
  963.3 84.7 %reduce-scatter.5.cloned.1.call-start = ((), (), s32[]{:S(2)}) async-start(), calls=%async_computation.12 | async-start | bytes 2064384 | tf_op jit(solution)/shard_map/reduce_scatter | solution.py:75
  963.4 18.0 %copy-start.21 = (bf16[3584]{0:T(1024)(128)(2,1)S(1)}, bf16[3584]{0:T(1024)(128)(2,1)}, u32[]{:S(2)}) copy-start(bf16[3584]{0:T(1024)(128)(2,1)} %param.31) | copy-start | bytes 21508
  973.7 15.5 %all-to-all-start = ((bf16[128,2,224]{2,1,0:T(2,128)(2,1)}), bf16[128,2,224]{2,1,0:T(2,128)(2,1)}, u32[]{:S(2)}, u32[]{:S(2)}) async-start(bf16[128,2,224]{2,1,0:T(2,128)(2,1)} %reshape.540), calls=%async_computation.1 | async-start | bytes 262144 | tf_op jit(solution)/shard_map/all_to_all | solution.py:84
  989.2 37.9 %all-to-all-start.1 = ((bf16[128,2,224]{2,1,0:T(2,128)(2,1)}), bf16[128,2,224]{2,1,0:T(2,128)(2,1)S(1)}, u32[]{:S(2)}, u32[]{:S(2)}) async-start(bf16[128,2,224]{2,1,0:T(2,128)(2,1)} %reshape.538), calls=%async_computation.2 | async-start | bytes 262144 | tf_op jit(solution)/shard_map/all_to_all | solution.py:85
  1029.3 22.8 %copy-start.1 = (bf16[128,64,128]{2,1,0:T(8,128)(2,1)S(1)}, bf16[128,64,128]{2,1,0:T(8,128)(2,1)}, u32[]{:S(2)}) copy-start(bf16[128,64,128]{2,1,0:T(8,128)(2,1)} %param.22) | copy-start | bytes 6291460
  (15 other events, 60.4 us)
Sparse Core Ops, SparseCore 0:
  53.8 663.1 all-reduce.2
  724.9 82.9 reduce-scatter.10
  817.7 73.4 reduce-scatter.8
  894.8 75.5 reduce-scatter.6
  974.0 73.9 reduce-scatter.4
where the time goes:
time: 1070 us; the launch traced here: 1060 us
  waiting for transfers between devices  711 us (66%)
  local copies, waits for them, and re-layouts  158 us (15%)
  matrix products  57.5 us (5%)
  starting transfers between devices  56.7 us (5%)
  blocking collectives  38.8 us (4%)
  other arithmetic  21.9 us (2%)
  between operations  15 us (1%)
    psum x1, waiting for transfers between devices, local(): lax.psum(jnp.dot(attended, out_weight, preferred_element_type=jnp.float32...  663 us
    gather x4, local copies, waits for them, and re-layouts, local(): text_cols = jnp.take(text_table, token_all[step], axis=1)  58.9 us
    unnamed x72, local copies, waits for them, and re-layouts  38.4 us
    all_to_all x4, starting transfers between devices, local(): lax.all_to_all(text_cols, ('dp', 'tensor'), split_axis=1, concat_axis=0,...  32.9 us
    gather x4, local copies, waits for them, and re-layouts, local(): codec_cols = jnp.take(codec_table, frame_all[step], axis=1)  30.1 us
    all_to_all x4, starting transfers between devices, local(): lax.all_to_all(codec_cols, ('dp', 'tensor'), split_axis=1, concat_axis=0,...  23.2 us
    dot_general x4, matrix products, local(): jnp.dot(hidden, bridge_weight, preferred_element_type=jnp.float32)  22.3 us
  transfers between devices with their start and end apart: 13, of which 8 were waited for; matrix products, arithmetic and copies ran while one was open for 17% of the time, Pallas kernels for 0%

commit v1 on v0

v1 whole, which is shorter than its diff:
```python
import functools

import jax
import jax.numpy as jnp
from jax import lax
from jax.experimental import pallas as pl
from jax.experimental.pallas import tpu as pltpu
from jax.sharding import PartitionSpec as P

QH = 32
KVH = 8
HD = 128
CAP = 64
GROUP = QH // KVH
STEPS = 4
SB = 16
LANES = 128
FPAD = 32
BF16 = jnp.bfloat16
F32 = jnp.float32
BOTH = ("dp", "tensor")
MIB = 1 << 20


def iota(shape, dim):
    return lax.broadcasted_iota(jnp.int32, shape, dim)


def attention_kernel(key_ref, q_ref, ck_ref, cv_ref, nk_ref, nv_ref, out_ref):
    rows = STEPS * GROUP * SB
    scale = 1.0 / HD**0.5
    queries = jnp.concatenate(
        [q_ref[t, :, h * HD : (h + 1) * HD] for t in range(STEPS) for h in range(GROUP)], axis=0
    )
    cached_k = ck_ref[...].reshape(SB * CAP, HD)
    cached_v = cv_ref[...].reshape(SB * CAP, HD)
    fresh_k = nk_ref[...].reshape(STEPS * SB, HD)
    fresh_v = nv_ref[...].reshape(STEPS * SB, HD)
    contract = (((1,), (1,)), ((), ()))
    score_c = lax.dot_general(queries, cached_k, contract, preferred_element_type=F32) * scale
    score_n = lax.dot_general(queries, fresh_k, contract, preferred_element_type=F32) * scale
    own = iota((rows, 1), 0) % SB
    score_c = jnp.where(own == key_ref[0], score_c, -1e30)
    row, col = iota((rows, STEPS * SB), 0), iota((rows, STEPS * SB), 1)
    seen = (row % SB == col % SB) & (col // SB <= row // (GROUP * SB))
    score_n = jnp.where(seen, score_n, -1e30)
    top = jnp.maximum(
        jnp.max(score_c, axis=-1, keepdims=True), jnp.max(score_n, axis=-1, keepdims=True)
    )
    exp_c = jnp.exp(score_c - top)
    exp_n = jnp.exp(score_n - top)
    total = jnp.sum(exp_c, axis=-1, keepdims=True) + jnp.sum(exp_n, axis=-1, keepdims=True)
    inverse = 1.0 / total
    weight_c = (exp_c * inverse).astype(BF16)
    weight_n = (exp_n * inverse).astype(BF16)
    attended = jnp.dot(weight_c, cached_v, preferred_element_type=F32)
    attended = attended + jnp.dot(weight_n, fresh_v, preferred_element_type=F32)
    attended = attended.astype(BF16)
    for t in range(STEPS):
        for h in range(GROUP):
            at = (t * GROUP + h) * SB
            out_ref[t, :, h * HD : (h + 1) * HD] = attended[at : at + SB]


def attention(query, new_keys, new_values, cache_keys, cache_values, cache_lengths):
    steps, streams, width = query.shape
    blocks = streams // SB
    position = jnp.arange(CAP, dtype=jnp.int32)[None, :]
    own = (jnp.arange(streams, dtype=jnp.int32) % SB)[:, None]
    keys = jnp.where(position < cache_lengths[:, None], own, -1).reshape(blocks, 1, SB * CAP)
    fresh = pl.BlockSpec((steps, SB, HD), lambda i: (0, i, 0))
    cached = pl.BlockSpec((SB, CAP, HD), lambda i: (i, 0, 0))
    heads = pl.BlockSpec((steps, SB, width), lambda i: (0, i, 0))
    return pl.pallas_call(
        attention_kernel,
        grid=(blocks,),
        in_specs=[
            pl.BlockSpec((1, 1, SB * CAP), lambda i: (i, 0, 0)),
            heads,
            cached,
            cached,
            fresh,
            fresh,
        ],
        out_specs=heads,
        out_shape=jax.ShapeDtypeStruct(query.shape, BF16),
        compiler_params=pltpu.CompilerParams(vmem_limit_bytes=32 * MIB),
        cost_estimate=pl.CostEstimate(
            flops=2 * 2 * 2048 * 1024 * 128 * 2, bytes_accessed=6 * MIB, transcendentals=2 * MIB
        ),
        name="attention",
    )(keys, query, cache_keys, cache_values, new_keys, new_values)


def embed_kernel(code_ref, text_ref, codec_ref, out_ref, text_s, codec_s):
    feats = text_ref.shape[0]

    def unpack(src, dst):
        def body(b, _):
            at = pl.multiple_of(b * LANES, LANES)
            block = src[:, pl.ds(at, LANES)].astype(F32)
            dst[b] = jnp.concatenate([block, jnp.zeros((FPAD - feats, LANES), F32)], axis=0)
            return 0

        lax.fori_loop(0, dst.shape[0], body, 0)

    unpack(text_ref, text_s)
    unpack(codec_ref, codec_s)
    lane = iota((FPAD, LANES), 1)

    def owner(o, _):
        acc = jnp.zeros((FPAD, LANES), F32)
        for j in range(LANES):
            code = code_ref[o, j]
            table = text_s if j < LANES // 2 else codec_s
            found = table[lax.shift_right_logical(code, 7)]
            found = pltpu.roll(found, code & (LANES - 1), 1)
            acc = jnp.where(lane == j, found, acc)
        out_ref[o] = acc.astype(BF16)
        return 0

    lax.fori_loop(0, out_ref.shape[0], owner, 0)


def embed(codes, text_table, codec_table):
    owners = codes.shape[0]
    vmem = pl.BlockSpec(memory_space=pltpu.VMEM)
    return pl.pallas_call(
        embed_kernel,
        in_specs=[pl.BlockSpec(memory_space=pltpu.SMEM), vmem, vmem],
        out_specs=vmem,
        out_shape=jax.ShapeDtypeStruct((owners, FPAD, LANES), BF16),
        scratch_shapes=[
            pltpu.VMEM((text_table.shape[1] // LANES, FPAD, LANES), F32),
            pltpu.VMEM((codec_table.shape[1] // LANES, FPAD, LANES), F32),
        ],
        compiler_params=pltpu.CompilerParams(vmem_limit_bytes=40 * MIB),
        cost_estimate=pl.CostEstimate(flops=40 * 1000 * 1000, bytes_accessed=100 * MIB, transcendentals=0),
        name="embed",
    )(codes, text_table, codec_table)


def project_kernel(a_ref, w_ref, res_ref, bridge_ref, hidden_ref, part_ref, acc, kept, *, owners):
    i = pl.program_id(0)

    @pl.when(i < owners)
    def _():
        w = w_ref[...].reshape(a_ref.shape[2], w_ref.shape[3])
        prod = jnp.dot(a_ref[0], w, preferred_element_type=F32)

        @pl.when(i == 0)
        def _():
            acc[...] = prod

        @pl.when(i > 0)
        def _():
            acc[...] += prod

    @pl.when(i == owners - 1)
    def _():
        hidden = (res_ref[...].astype(F32) + acc[...]).astype(BF16)
        kept[...] = hidden
        hidden_ref[...] = hidden

    @pl.when(i >= owners)
    def _():
        part = jnp.dot(kept[...], bridge_ref[...], preferred_element_type=F32).astype(BF16)
        per = part_ref.shape[2]
        width = part_ref.shape[3]
        part_ref[...] = (
            part.reshape(STEPS, owners, per, width).transpose(1, 0, 2, 3)
        )


def project(attended, weight, residual, bridge):
    owners, rows, depth = attended.shape
    parts, width = weight.shape[0], weight.shape[3]
    talk = bridge.shape[1]
    cols = 512
    first = lambda i: jnp.minimum(i, owners - 1)
    later = lambda i: jnp.maximum(i - owners, 0)
    whole = pl.BlockSpec((rows, width), lambda i: (0, 0))
    return pl.pallas_call(
        functools.partial(project_kernel, owners=owners),
        grid=(owners + talk // cols,),
        in_specs=[
            pl.BlockSpec((1, rows, depth), lambda i: (first(i), 0, 0)),
            pl.BlockSpec((parts, 1, depth // parts, width), lambda i: (0, first(i), 0, 0)),
            whole,
            pl.BlockSpec((width, cols), lambda i: (0, later(i))),
        ],
        out_specs=[
            whole,
            pl.BlockSpec((owners, STEPS, rows // STEPS // owners, cols), lambda i: (0, 0, 0, later(i))),
        ],
        out_shape=[
            jax.ShapeDtypeStruct((rows, width), BF16),
            jax.ShapeDtypeStruct((owners, STEPS, rows // STEPS // owners, talk), BF16),
        ],
        scratch_shapes=[pltpu.VMEM((rows, width), F32), pltpu.VMEM((rows, width), BF16)],
        compiler_params=pltpu.CompilerParams(vmem_limit_bytes=48 * MIB),
        cost_estimate=pl.CostEstimate(flops=8 * 10**9, bytes_accessed=24 * MIB, transcendentals=0),
        name="project",
    )(attended, weight, residual, bridge)


def finish_kernel(part_ref, emb_ref, gain_ref, out_ref, pick, mixed, square, *, feats):
    i = pl.program_id(0)
    sources, rows, cols = part_ref.shape
    depth = emb_ref.shape[0] * FPAD
    half = LANES // 2

    @pl.when(i == 0)
    def _():
        row = iota((depth, 1), 0)
        target = jnp.where(row % FPAD < feats, row // FPAD * feats + row % FPAD, -1)
        pick[...] = jnp.where(iota((depth, cols), 1) == target, 1.0, 0.0).astype(BF16)
        square[...] = jnp.zeros_like(square)

    total = part_ref[0].astype(F32)
    for s in range(1, sources):
        total = total + part_ref[s].astype(F32)
    found = lax.dot_general(
        emb_ref[...].reshape(depth, LANES),
        pick[...],
        (((0,), (0,)), ((), ())),
        preferred_element_type=F32,
    )
    total = total + found[:half] + found[half:]
    mixed[i] = total
    square[...] += jnp.sum(total * total, axis=-1, keepdims=True)

    @pl.when(i == pl.num_programs(0) - 1)
    def _():
        blocks = mixed.shape[0]
        factor = lax.rsqrt(square[...] * (1.0 / (blocks * cols)) + 1e-06)
        for b in range(blocks):
            gain = gain_ref[:, b * cols : (b + 1) * cols].astype(F32)
            out_ref[:, b * cols : (b + 1) * cols] = (mixed[b] * factor * gain).astype(BF16)


def finish(parts, emb, gain):
    sources, rows, talk = parts.shape
    feats = talk // emb.shape[0]
    blocks = 4
    cols = talk // blocks
    return pl.pallas_call(
        functools.partial(finish_kernel, feats=feats),
        grid=(blocks,),
        in_specs=[
            pl.BlockSpec((sources, rows, cols), lambda i: (0, 0, i)),
            pl.BlockSpec((emb.shape[0] // blocks, FPAD, LANES), lambda i: (i, 0, 0)),
            pl.BlockSpec((1, talk), lambda i: (0, 0)),
        ],
        out_specs=pl.BlockSpec((rows, talk), lambda i: (0, 0)),
        out_shape=jax.ShapeDtypeStruct((rows, talk), BF16),
        scratch_shapes=[
            pltpu.VMEM((emb.shape[0] // blocks * FPAD, cols), BF16),
            pltpu.VMEM((blocks, rows, cols), F32),
            pltpu.VMEM((rows, 1), F32),
        ],
        compiler_params=pltpu.CompilerParams(vmem_limit_bytes=32 * MIB),
        name="finish",
    )(parts, emb, gain)


def local(
    query,
    new_keys,
    new_values,
    cache_keys,
    cache_values,
    cache_lengths,
    residual,
    out_weight,
    bridge_weight,
    text_table,
    codec_table,
    tokens,
    frames,
    talk_gain,
):
    steps, streams, depth = query.shape
    width = residual.shape[2]
    talk = bridge_weight.shape[1]
    tensor = out_weight.shape[1] // width
    dp = lax.axis_size("dp")
    rows = steps * streams
    per = streams // tensor

    share = lax.dynamic_slice_in_dim(out_weight, lax.axis_index("dp") * (depth // dp), depth // dp, 0)
    share = share.reshape(depth // dp, tensor, width).transpose(1, 0, 2)
    share = lax.all_to_all(share, "tensor", 0, 0, tiled=True)
    weight = lax.all_gather(share, "dp")

    def by_owner(ids):
        return ids.reshape(steps, tensor, per).transpose(1, 0, 2).reshape(tensor, steps * per)

    ids = jnp.concatenate([by_owner(tokens), by_owner(frames)], axis=1)
    lane = jnp.arange(LANES, dtype=jnp.int32)[None, :]
    codes = (ids // LANES) * LANES + (lane - ids) % LANES
    codes = lax.all_gather(codes, "dp", axis=0, tiled=True)
    emb = embed(codes, text_table, codec_table)
    emb = lax.all_to_all(emb, BOTH, 0, 0, tiled=True)

    attended = attention(query, new_keys, new_values, cache_keys, cache_values, cache_lengths)
    attended = attended.reshape(rows, depth)
    attended = lax.all_to_all(
        jnp.broadcast_to(attended[None], (tensor, rows, depth)), "tensor", 0, 0, tiled=True
    )
    hidden, parts = project(attended, weight, residual.reshape(rows, width), bridge_weight)
    parts = lax.all_to_all(
        parts.reshape(tensor, steps * per, talk), "tensor", 0, 0, tiled=True
    )
    talker = finish(parts, emb, talk_gain.reshape(1, talk))
    return hidden.reshape(steps, streams, width), talker.reshape(steps, per, talk)


def solution(mesh):
    in_specs = (
        P(None, "dp", "tensor"),
        P(None, "dp", "tensor"),
        P(None, "dp", "tensor"),
        P("dp", None, "tensor"),
        P("dp", None, "tensor"),
        P("dp"),
        P(None, "dp", "tensor"),
        P("tensor", None),
        P("tensor", None),
        P(("dp", "tensor"), None),
        P(("dp", "tensor"), None),
        P(None, "dp"),
        P(None, "dp"),
        P(),
    )
    out_specs = (P(None, "dp", "tensor"), P(None, ("dp", "tensor"), None))
    return jax.shard_map(local, mesh=mesh, in_specs=in_specs, out_specs=out_specs, check_vma=False)
```

time: 1070 us -> 270 us (0.25)
  waiting for transfers between devices: 711 us -> 52.9 us
  local copies, waits for them, and re-layouts: 158 us -> 10.9 us
  Pallas kernels: 0 us -> 83.4 us
  matrix products: 57.5 us -> 0 us
  blocking collectives: 38.8 us -> 87.8 us
  starting transfers between devices: 56.7 us -> 20.2 us
  other arithmetic: 21.9 us -> 0.14 us
    psum x1 -> x0, waiting for transfers between devices: 663 us -> none  [local(): lax.psum(jnp.dot(attended, out_weight, preferred_element_type=jnp.float32...]
    gather x8 -> x0, local copies, waits for them, and re-layouts: 89 us -> none  [the longest x4 58.9 us: local(): text_cols = jnp.take(text_table, token_all[step], axis=1)]
    pallas_call x0 -> x4, Pallas kernels: none -> 83.4 us  [the longest x1 51.4 us: embed(): pl.pallas_call(embed_kernel, in_specs=[pl.BlockSpec(memory_space=pltpu.SM...]
    dot_general x23 -> x0, matrix products: 57.5 us -> none  [the longest x4 22.3 us: local(): jnp.dot(hidden, bridge_weight, preferred_element_type=jnp.float32)]
    all_to_all x8 -> x3, starting transfers between devices: 56.1 us -> 20.2 us  [the longest x1 9.13 us: local(): emb = lax.all_to_all(emb, BOTH, 0, 0, tiled=True)]
    unnamed x72 -> x27, local copies, waits for them, and re-layouts: 38.4 us -> 6.19 us
    all_gather x2 -> x1, blocking collectives: 38.8 us -> 69.6 us  [local(): codes = lax.all_gather(codes, 'dp', axis=0, tiled=True)]
    convert_element_type x16 -> x0, local copies, waits for them, and re-layouts: 27.8 us -> none  [the longest x8 14.4 us: local(): text_rows.T.astype(jnp.float32)]
  transfers between devices with their start and end apart: 13 -> 4, of which waited for: 8 -> 1; matrix products, arithmetic and copies ran while one was open for 17% -> 1% of each run, Pallas kernels for 0% -> 29%
where the time goes in v1:
time: 270 us
  blocking collectives  87.8 us (33%)
  Pallas kernels  83.4 us (31%)
  waiting for transfers between devices  52.9 us (20%)
  starting transfers between devices  20.2 us (7%)
  between operations  14.2 us (5%)
  local copies, waits for them, and re-layouts  10.9 us (4%)
    all_gather x1, blocking collectives, local(): codes = lax.all_gather(codes, 'dp', axis=0, tiled=True)  69.6 us
    all_to_all x1, waiting for transfers between devices, local(): lax.all_to_all(parts.reshape(tensor, steps * per, talk), 'tensor', 0, 0,...  52.9 us
    pallas_call x1, Pallas kernels, embed(): pl.pallas_call(embed_kernel, in_specs=[pl.BlockSpec(memory_space=pltpu.SM...  51.4 us
    pallas_call x1, Pallas kernels, project(): pl.pallas_call(functools.partial(project_kernel, owners=owners), grid=(ow...  18.9 us
    all_to_all x1, blocking collectives, local(): share = lax.all_to_all(share, 'tensor', 0, 0, tiled=True)  18.2 us
    all_to_all x1, starting transfers between devices, local(): emb = lax.all_to_all(emb, BOTH, 0, 0, tiled=True)  9.13 us
    pallas_call x1, Pallas kernels, attention(): pl.pallas_call(attention_kernel, grid=(blocks,), in_specs=[pl.BlockSpec((...  7.66 us
    all_to_all x1, starting transfers between devices, local(): lax.all_to_all(parts.reshape(tensor, steps * per, talk), 'tensor', 0, 0,...  6.29 us
  transfers between devices with their start and end apart: 4, of which 1 were waited for; matrix products, arithmetic and copies ran while one was open for 1% of the time, Pallas kernels for 29%

profile of v1, /device:TPU:0, one launch (start us, length us, event | category | flops | bytes accessed | tf_op | source)
XLA Modules:
  0.0 269.5 jit_solution(9742632140478797247)
XLA Ops:
  7.3 1.2 constant_dynamic-slice_fusion
  8.5 0.3 copy.27
  8.8 0.3 copy.24
  9.1 18.2 %all_to_all.20 = bf16[8,32,1024]{2,1,0:T(8,128)(2,1)} all-to-all(bf16[8,32,1024]{2,1,0:T(8,128)(2,1)S(1)} %copy.24), channel_id=1, replica_groups=mesh['dp'=16,'tensor'=8] {'tensor'}, dimensions={0} | all-to-all | bytes 1048576 | tf_op jit(solution)/shard_map/all_to_all | solution.py:293
  27.4 0.1 broadcast_in_dim.26
  27.5 0.1 lt.46
  27.6 0.1 lt.48
  27.9 1.6 copy-done.4
  29.5 7.7 %attention.1 = bf16[4,128,512]{2,1,0:T(8,128)(2,1)S(1)} custom-call(s32[8,1,1024]{2,1,0:T(1,128)S(1)} %compare_select_fusion.key_ref, bf16[4,128,512]{2,1,0:T(8,128)(2,1)S(1)} %copy-done.6, bf16[128,64,128]{2,1,0:T(8,128)(2,1)S(1)} %copy-done.3, bf16[128,64,128]{2,1,0:T(8,128)(2,1)S(1)} %copy-done.4, bf16[4,128,128]{2,1,0:T(8,128)(2,1)S(1)} %copy-done.7, ...), custom_call_target="tpu_custom_call" | custom-call | flops 2147483648 | bytes 6291456 | tf_op jit(solution)/shard_map/attention/pallas_call | solution.py:74
  37.2 2.3 broadcast_in_dim.29
  39.5 4.7 %all-to-all-start = ((bf16[8,512,512]{2,1,0:T(8,128)(2,1)}), bf16[8,512,512]{2,1,0:T(8,128)(2,1)}, u32[]{:S(2)}, u32[]{:S(2)}) async-start(bf16[8,512,512]{2,1,0:T(8,128)(2,1)} %broadcast_in_dim.29), calls=%async_computation | async-start | bytes 8388608 | tf_op jit(solution)/shard_map/all_to_all | solution.py:308
  44.3 0.1 reshape.106
  44.4 0.1 reshape.107
  44.5 0.1 reshape.109
  44.6 0.1 fusion.2
  44.7 69.6 %all_gather.11.code_ref = s32[128,128]{1,0:T(8,128)S(1)} all-gather(s32[8,128]{1,0:T(8,128)S(1)} %fusion.2), channel_id=1, replica_groups=mesh['dp'=16,'tensor'=8] {'dp'}, dimensions={0}, use_global_device_ids=true | all-gather | bytes 69632 | tf_op jit(solution)/shard_map/all_gather | solution.py:302
  114.3 2.5 copy-done
  116.8 51.4 %embed.1 = bf16[128,32,128]{2,1,0:T(8,128)(2,1)} custom-call(s32[128,128]{1,0:T(8,128)S(1)} %all_gather.11.code_ref, bf16[28,76032]{1,0:T(8,128)(2,1)S(1)} %copy-done, bf16[28,8448]{1,0:T(8,128)(2,1)S(1)} %copy-done.2), custom_call_target="tpu_custom_call" | custom-call | flops 40000000 | bytes 104857600 | tf_op jit(solution)/shard_map/embed/pallas_call | solution.py:128
  168.2 9.1 %all-to-all-start.3 = ((bf16[128,32,128]{2,1,0:T(8,128)(2,1)}), bf16[128,32,128]{2,1,0:T(8,128)(2,1)S(1)}, u32[]{:S(2)}, u32[]{:S(2)}) async-start(bf16[128,32,128]{2,1,0:T(8,128)(2,1)} %embed.1), calls=%async_computation.3 | async-start | bytes 2097152 | tf_op jit(solution)/shard_map/all_to_all | solution.py:304
  177.4 18.9 %project.1 = (bf16[512,1024]{1,0:T(8,128)(2,1)}, bf16[8,4,16,3584]{3,2,1,0:T(8,128)(2,1)S(1)}) custom-call(bf16[8,512,512]{2,1,0:T(8,128)(2,1)} %all-to-all-done.a_ref, bf16[16,8,32,1024]{3,2,1,0:T(8,128)(2,1)} %bitcast.24, bf16[512,1024]{1,0:T(8,128)(2,1)S(1)} %bitcast.18, bf16[1024,3584]{1,0:T(8,128)(2,1)} %bridge_ref.1), custom_call_target="tpu_custom_call" | custom-call | flops 8000000000 | bytes 25165824 | tf_op jit(solution)/shard_map/project/pallas_call | solution.py:183
  196.2 1.8 copy-done.1
  198.0 6.3 %all-to-all-start.2 = ((bf16[8,64,3584]{2,1,0:T(8,128)(2,1)}), bf16[8,64,3584]{2,1,0:T(8,128)(2,1)}, u32[]{:S(2)}, u32[]{:S(2)}) async-start(bf16[8,64,3584]{2,1,0:T(8,128)(2,1)} %bitcast.16), calls=%async_computation.2 | async-start | bytes 7340032 | tf_op jit(solution)/shard_map/all_to_all | solution.py:312
  204.3 52.9 %all-to-all-done.2.part_ref = bf16[8,64,3584]{2,1,0:T(8,128)(2,1)} async-done(((bf16[8,64,3584]{2,1,0:T(8,128)(2,1)}), bf16[8,64,3584]{2,1,0:T(8,128)(2,1)}, u32[]{:S(2)}, u32[]{:S(2)}) %all-to-all-start.2) | async-done | bytes 3670048 | tf_op jit(solution)/shard_map/all_to_all | solution.py:312
  257.2 5.5 %finish.1 = bf16[64,3584]{1,0:T(8,128)(2,1)} custom-call(bf16[8,64,3584]{2,1,0:T(8,128)(2,1)} %all-to-all-done.2.part_ref, bf16[128,32,128]{2,1,0:T(8,128)(2,1)S(1)} %all-to-all-done.3.emb_ref, bf16[1,3584]{1,0:T(2,128)(2,1)S(1)} %reshape.110.gain_ref), custom_call_target="tpu_custom_call" | custom-call | tf_op jit(solution)/shard_map/finish/pallas_call | solution.py:247
  (38 shorter events, 0.5 us)
Async XLA Ops:
  7.2 20.3 %copy-start.12 = (s32[128]{0:T(128)S(1)}, s32[128]{0:T(128)}, u32[]{:S(2)}) copy-start(s32[128]{0:T(128)} %param.19) | copy-start | bytes 1540
  7.2 20.7 %copy-start.6 = (bf16[4,128,512]{2,1,0:T(8,128)(2,1)S(1)}, bf16[4,128,512]{2,1,0:T(8,128)(2,1)}, u32[]{:S(2)}) copy-start(bf16[4,128,512]{2,1,0:T(8,128)(2,1)} %q_ref.1) | copy-start | bytes 1572868
  7.2 20.7 %copy-start.7 = (bf16[4,128,128]{2,1,0:T(8,128)(2,1)S(1)}, bf16[4,128,128]{2,1,0:T(8,128)(2,1)}, u32[]{:S(2)}) copy-start(bf16[4,128,128]{2,1,0:T(8,128)(2,1)} %nk_ref.1) | copy-start | bytes 393220
  7.2 20.7 %copy-start.8 = (bf16[4,128,128]{2,1,0:T(8,128)(2,1)S(1)}, bf16[4,128,128]{2,1,0:T(8,128)(2,1)}, u32[]{:S(2)}) copy-start(bf16[4,128,128]{2,1,0:T(8,128)(2,1)} %nv_ref.1) | copy-start | bytes 393220
  7.2 20.7 %copy-start.3 = (bf16[128,64,128]{2,1,0:T(8,128)(2,1)S(1)}, bf16[128,64,128]{2,1,0:T(8,128)(2,1)}, u32[]{:S(2)}) copy-start(bf16[128,64,128]{2,1,0:T(8,128)(2,1)} %ck_ref.1) | copy-start | bytes 6291460
  7.2 170.1 %all-gather.3.cloned.1.call-start = ((), (), s32[]{:S(2)}) async-start(), calls=%async_computation.4 | async-start | bytes 8912896 | tf_op jit(solution)/shard_map/all_gather | solution.py:294
  27.9 1.6 copy-start.4
  39.5 4.8 %copy-start.10 = (s32[4,128]{1,0:T(4,128)S(1)}, s32[4,128]{1,0:T(4,128)}, u32[]{:S(2)}) copy-start(s32[4,128]{1,0:T(4,128)} %param.25) | copy-start | bytes 6148
  39.5 4.9 %copy-start.11 = (s32[4,128]{1,0:T(4,128)S(1)}, s32[4,128]{1,0:T(4,128)}, u32[]{:S(2)}) copy-start(s32[4,128]{1,0:T(4,128)} %param.26) | copy-start | bytes 6148
  39.5 74.8 %copy-start.2 = (bf16[28,8448]{1,0:T(8,128)(2,1)S(1)}, bf16[28,8448]{1,0:T(8,128)(2,1)}, u32[]{:S(2)}) copy-start(bf16[28,8448]{1,0:T(8,128)(2,1)} %codec_ref.1) | copy-start | bytes 1419268
  39.5 128.7 %all-to-all-start = ((bf16[8,512,512]{2,1,0:T(8,128)(2,1)}), bf16[8,512,512]{2,1,0:T(8,128)(2,1)}, u32[]{:S(2)}, u32[]{:S(2)}) async-start(bf16[8,512,512]{2,1,0:T(8,128)(2,1)} %broadcast_in_dim.29), calls=%async_computation | async-start | bytes 8388608 | tf_op jit(solution)/shard_map/all_to_all | solution.py:308
  114.3 2.5 copy-start
  116.8 60.5 %copy-start.5 = (bf16[4,128,1024]{2,1,0:T(8,128)(2,1)S(1)}, bf16[4,128,1024]{2,1,0:T(8,128)(2,1)}, u32[]{:S(2)}) copy-start(bf16[4,128,1024]{2,1,0:T(8,128)(2,1)} %param.20) | copy-start | bytes 3145732
  168.2 29.8 %all-to-all-start.3 = ((bf16[128,32,128]{2,1,0:T(8,128)(2,1)}), bf16[128,32,128]{2,1,0:T(8,128)(2,1)S(1)}, u32[]{:S(2)}, u32[]{:S(2)}) async-start(bf16[128,32,128]{2,1,0:T(8,128)(2,1)} %embed.1), calls=%async_computation.3 | async-start | bytes 2097152 | tf_op jit(solution)/shard_map/all_to_all | solution.py:304
  196.2 1.8 copy-start.1
  198.0 6.3 %copy-start.9 = (bf16[3584]{0:T(1024)(128)(2,1)S(1)}, bf16[3584]{0:T(1024)(128)(2,1)}, u32[]{:S(2)}) copy-start(bf16[3584]{0:T(1024)(128)(2,1)} %param.27) | copy-start | bytes 21508
  198.0 59.2 %all-to-all-start.2 = ((bf16[8,64,3584]{2,1,0:T(8,128)(2,1)}), bf16[8,64,3584]{2,1,0:T(8,128)(2,1)}, u32[]{:S(2)}, u32[]{:S(2)}) async-start(bf16[8,64,3584]{2,1,0:T(8,128)(2,1)} %bitcast.16), calls=%async_computation.2 | async-start | bytes 7340032 | tf_op jit(solution)/shard_map/all_to_all | solution.py:312
Sparse Core Ops, SparseCore 0:
  27.4 95.7 all-gather.2

commit v2 on v1

--- a/solution.py
+++ b/solution.py
@@ -16,6 +16,7 @@
 SB = 16
 LANES = 128
 FPAD = 32
+PACK = LANES // FPAD
 BF16 = jnp.bfloat16
 F32 = jnp.float32
 BOTH = ("dp", "tensor")
@@ -92,141 +93,185 @@
     )(keys, query, cache_keys, cache_values, new_keys, new_values)
 
 
+def turn_kernel(text_ref, codec_ref, text_out, codec_out):
+    feats = text_ref.shape[0]
+    pad = jnp.zeros((FPAD - feats, LANES), F32)
+
+    def turn(src, dst):
+        blocks = src.shape[1] // LANES
+
+        def rows(first, count):
+            parts = []
+            for k in range(count):
+                at = pl.multiple_of((first + k) * LANES, LANES)
+                parts += [src[:, pl.ds(at, LANES)].astype(F32), pad]
+            if count < PACK:
+                parts.append(jnp.zeros(((PACK - count) * FPAD, LANES), F32))
+            return jnp.concatenate(parts, axis=0).T
+
+        def body(g, _):
+            dst[pl.ds(pl.multiple_of(g * LANES, LANES), LANES), :] = rows(g * PACK, PACK)
+            return 0
+
+        whole = blocks // PACK
+        lax.fori_loop(0, whole, body, 0, unroll=4)
+        if blocks % PACK:
+            dst[whole * LANES : (whole + 1) * LANES, :] = rows(whole * PACK, blocks % PACK)
+
+    turn(text_ref, text_out)
+    turn(codec_ref, codec_out)
+
+
+def turn_tables(text_table, codec_table):
+    vmem = pl.BlockSpec(memory_space=pltpu.VMEM)
+    rows = lambda table: pl.cdiv(table.shape[1], PACK * LANES) * LANES
+    return pl.pallas_call(
+        turn_kernel,
+        in_specs=[vmem, vmem],
+        out_specs=[vmem, vmem],
+        out_shape=[jax.ShapeDtypeStruct((rows(t), LANES), F32) for t in (text_table, codec_table)],
+        compiler_params=pltpu.CompilerParams(vmem_limit_bytes=40 * MIB),
+        cost_estimate=pl.CostEstimate(flops=0, bytes_accessed=16 * MIB, transcendentals=0),
+        name="turn_tables",
+    )(text_table, codec_table)
+
+
 def embed_kernel(code_ref, text_ref, codec_ref, out_ref, text_s, codec_s):
-    feats = text_ref.shape[0]
-
-    def unpack(src, dst):
-        def body(b, _):
-            at = pl.multiple_of(b * LANES, LANES)
-            block = src[:, pl.ds(at, LANES)].astype(F32)
-            dst[b] = jnp.concatenate([block, jnp.zeros((FPAD - feats, LANES), F32)], axis=0)
-            return 0
-
-        lax.fori_loop(0, dst.shape[0], body, 0)
-
-    unpack(text_ref, text_s)
-    unpack(codec_ref, codec_s)
-    lane = iota((FPAD, LANES), 1)
+    half = code_ref.shape[1] // 2
+    slot = iota((1, LANES), 1) // FPAD
+    lane = iota((half // 2, LANES), 1)
+
+    def look(table, code):
+        row = table[pl.ds(lax.shift_right_logical(code, 2), 1), :]
+        return jnp.where(slot == (code & (PACK - 1)), row, 0.0)
+
+    def spread(x):
+        x = x + pltpu.roll(x, 64, 1)
+        return x + pltpu.roll(x, 32, 1)
 
     def owner(o, _):
-        acc = jnp.zeros((FPAD, LANES), F32)
-        for j in range(LANES):
-            code = code_ref[o, j]
-            table = text_s if j < LANES // 2 else codec_s
-            found = table[lax.shift_right_logical(code, 7)]
-            found = pltpu.roll(found, code & (LANES - 1), 1)
-            acc = jnp.where(lane == j, found, acc)
-        out_ref[o] = acc.astype(BF16)
+        for r in range(half):
+            text_s[r : r + 1, :] = look(text_ref, code_ref[o, r])
+            codec_s[r : r + 1, :] = look(codec_ref, code_ref[o, half + r])
+        text, codec = spread(text_s[...]), spread(codec_s[...])
+        low = jnp.where(lane < FPAD, text[: half // 2], codec[: half // 2])
+        high = jnp.where(lane < 3 * FPAD, text[half // 2 :], codec[half // 2 :])
+        out_ref[o] = jnp.where(lane < 2 * FPAD, low, high).astype(BF16)
         return 0
 
     lax.fori_loop(0, out_ref.shape[0], owner, 0)
 
 
-def embed(codes, text_table, codec_table):
+def embed(codes, text_rows, codec_rows):
     owners = codes.shape[0]
     vmem = pl.BlockSpec(memory_space=pltpu.VMEM)
     return pl.pallas_call(
         embed_kernel,
         in_specs=[pl.BlockSpec(memory_space=pltpu.SMEM), vmem, vmem],
         out_specs=vmem,
-        out_shape=jax.ShapeDtypeStruct((owners, FPAD, LANES), BF16),
-        scratch_shapes=[
-            pltpu.VMEM((text_table.shape[1] // LANES, FPAD, LANES), F32),
-            pltpu.VMEM((codec_table.shape[1] // LANES, FPAD, LANES), F32),
-        ],
+        out_shape=jax.ShapeDtypeStruct((owners, codes.shape[1] // 4, LANES), BF16),
+        scratch_shapes=[pltpu.VMEM((codes.shape[1] // 2, LANES), F32)] * 2,
         compiler_params=pltpu.CompilerParams(vmem_limit_bytes=40 * MIB),
-        cost_estimate=pl.CostEstimate(flops=40 * 1000 * 1000, bytes_accessed=100 * MIB, transcendentals=0),
+        cost_estimate=pl.CostEstimate(flops=0, bytes_accessed=owners * 256 * 1024, transcendentals=0),
         name="embed",
-    )(codes, text_table, codec_table)
-
-
-def project_kernel(a_ref, w_ref, res_ref, bridge_ref, hidden_ref, part_ref, acc, kept, *, owners):
+    )(codes, text_rows, codec_rows)
+
+
+def project_kernel(order_ref, *refs, owners):
+    del order_ref
+    a_refs = refs[:owners]
+    w_ref, res_ref, bridge_ref, hidden_ref, part_ref, acc, kept = refs[owners:]
     i = pl.program_id(0)
-
-    @pl.when(i < owners)
-    def _():
-        w = w_ref[...].reshape(a_ref.shape[2], w_ref.shape[3])
-        prod = jnp.dot(a_ref[0], w, preferred_element_type=F32)
-
-        @pl.when(i == 0)
-        def _():
-            acc[...] = prod
-
-        @pl.when(i > 0)
-        def _():
-            acc[...] += prod
-
-    @pl.when(i == owners - 1)
-    def _():
-        hidden = (res_ref[...].astype(F32) + acc[...]).astype(BF16)
-        kept[...] = hidden
-        hidden_ref[...] = hidden
+    depth = a_refs[0].shape[1]
+
+    for k in range(owners):
+
+        @pl.when(i == k)
+        def _(k=k):
+            w = w_ref[...].reshape(depth, w_ref.shape[3])
+            prod = jnp.dot(a_refs[k][...], w, preferred_element_type=F32)
+            if k == 0:
+                acc[...] = res_ref[...].astype(F32) + prod
+            elif k < owners - 1:
+                acc[...] += prod
+            else:
+                hidden = (acc[...] + prod).astype(BF16)
+                kept[...] = hidden
+                hidden_ref[...] = hidden
 
     @pl.when(i >= owners)
     def _():
-        part = jnp.dot(kept[...], bridge_ref[...], preferred_element_type=F32).astype(BF16)
+        at = pl.multiple_of((i - owners) * part_ref.shape[3], part_ref.shape[3])
+        bridge = bridge_ref[:, pl.ds(at, part_ref.shape[3])]
+        part = jnp.dot(kept[...], bridge, preferred_element_type=F32).astype(BF16)
         per = part_ref.shape[2]
         width = part_ref.shape[3]
-        part_ref[...] = (
-            part.reshape(STEPS, owners, per, width).transpose(1, 0, 2, 3)
-        )
-
-
-def project(attended, weight, residual, bridge):
-    owners, rows, depth = attended.shape
+        part_ref[...] = part.reshape(STEPS, owners, per, width).transpose(1, 0, 2, 3)
+
+
+def project(attended, order, weight, residual, bridge):
+    owners = len(attended)
+    rows, depth = attended[0].shape
     parts, width = weight.shape[0], weight.shape[3]
     talk = bridge.shape[1]
     cols = 512
     first = lambda i: jnp.minimum(i, owners - 1)
     later = lambda i: jnp.maximum(i - owners, 0)
-    whole = pl.BlockSpec((rows, width), lambda i: (0, 0))
+    vmem = pl.BlockSpec(memory_space=pltpu.VMEM)
+    per = rows // STEPS // owners
     return pl.pallas_call(
         functools.partial(project_kernel, owners=owners),
-        grid=(owners + talk // cols,),
-        in_specs=[
-            pl.BlockSpec((1, rows, depth), lambda i: (first(i), 0, 0)),
-            pl.BlockSpec((parts, 1, depth // parts, width), lambda i: (0, first(i), 0, 0)),
-            whole,
-            pl.BlockSpec((width, cols), lambda i: (0, later(i))),
-        ],
-        out_specs=[
-            whole,
-            pl.BlockSpec((owners, STEPS, rows // STEPS // owners, cols), lambda i: (0, 0, 0, later(i))),
-        ],
+        grid_spec=pltpu.PrefetchScalarGridSpec(
+            num_scalar_prefetch=1,
+            grid=(owners + talk // cols,),
+            in_specs=[vmem] * owners
+            + [
+                pl.BlockSpec((parts, 1, depth // parts, width), lambda i, o: (0, o[first(i)], 0, 0)),
+                vmem,
+                vmem,
+            ],
+            out_specs=[
+                pl.BlockSpec((rows, width), lambda i, o: (0, 0)),
+                pl.BlockSpec((owners, STEPS, per, cols), lambda i, o: (0, 0, 0, later(i))),
+            ],
+            scratch_shapes=[pltpu.VMEM((rows, width), F32), pltpu.VMEM((rows, width), BF16)],
+        ),
         out_shape=[
             jax.ShapeDtypeStruct((rows, width), BF16),
-            jax.ShapeDtypeStruct((owners, STEPS, rows // STEPS // owners, talk), BF16),
+            jax.ShapeDtypeStruct((owners, STEPS, per, talk), BF16),
         ],
-        scratch_shapes=[pltpu.VMEM((rows, width), F32), pltpu.VMEM((rows, width), BF16)],
-        compiler_params=pltpu.CompilerParams(vmem_limit_bytes=48 * MIB),
+        compiler_params=pltpu.CompilerParams(vmem_limit_bytes=52 * MIB),
         cost_estimate=pl.CostEstimate(flops=8 * 10**9, bytes_accessed=24 * MIB, transcendentals=0),
         name="project",
-    )(attended, weight, residual, bridge)
-
-
-def finish_kernel(part_ref, emb_ref, gain_ref, out_ref, pick, mixed, square, *, feats):
+    )(order, *attended, weight, residual, bridge)
+
+
+def finish_kernel(part_ref, emb_ref, gain_ref, out_ref, mixed, square, *, feats):
     i = pl.program_id(0)
     sources, rows, cols = part_ref.shape
-    depth = emb_ref.shape[0] * FPAD
-    half = LANES // 2
+    holders, half, _ = emb_ref.shape
 
     @pl.when(i == 0)
     def _():
-        row = iota((depth, 1), 0)
-        target = jnp.where(row % FPAD < feats, row // FPAD * feats + row % FPAD, -1)
-        pick[...] = jnp.where(iota((depth, cols), 1) == target, 1.0, 0.0).astype(BF16)
         square[...] = jnp.zeros_like(square)
 
+    lane = iota((half, LANES), 1)
+    found = [[jnp.zeros((half, LANES), F32)] * (cols // LANES) for _ in range(2)]
+    for h in range(holders):
+        both = emb_ref[h].astype(F32)
+        both = both + pltpu.roll(both, LANES - FPAD, 1)
+        tile, at = divmod(h * feats, LANES)
+        end = at + feats
+        for k in range(2):
+            moved = pltpu.roll(both, (at - k * LANES // 2) % LANES, 1)
+            inside = (lane >= at) & (lane < end)
+            found[k][tile] = jnp.where(inside, moved, found[k][tile])
+            if end > LANES:
+                found[k][tile + 1] = jnp.where(lane < end - LANES, moved, found[k][tile + 1])
     total = part_ref[0].astype(F32)
     for s in range(1, sources):
         total = total + part_ref[s].astype(F32)
-    found = lax.dot_general(
-        emb_ref[...].reshape(depth, LANES),
-        pick[...],
-        (((0,), (0,)), ((), ())),
-        preferred_element_type=F32,
-    )
-    total = total + found[:half] + found[half:]
+    total = total + jnp.concatenate([jnp.concatenate(f, axis=1) for f in found], axis=0)
     mixed[i] = total
     square[...] += jnp.sum(total * total, axis=-1, keepdims=True)
 
@@ -249,19 +294,37 @@
         grid=(blocks,),
         in_specs=[
             pl.BlockSpec((sources, rows, cols), lambda i: (0, 0, i)),
-            pl.BlockSpec((emb.shape[0] // blocks, FPAD, LANES), lambda i: (i, 0, 0)),
+            pl.BlockSpec((emb.shape[0] // blocks,) + emb.shape[1:], lambda i: (i, 0, 0)),
             pl.BlockSpec((1, talk), lambda i: (0, 0)),
         ],
         out_specs=pl.BlockSpec((rows, talk), lambda i: (0, 0)),
         out_shape=jax.ShapeDtypeStruct((rows, talk), BF16),
         scratch_shapes=[
-            pltpu.VMEM((emb.shape[0] // blocks * FPAD, cols), BF16),
             pltpu.VMEM((blocks, rows, cols), F32),
             pltpu.VMEM((rows, 1), F32),
         ],
         compiler_params=pltpu.CompilerParams(vmem_limit_bytes=32 * MIB),
         name="finish",
     )(parts, emb, gain)
+
+
+def gather_tensor(own):
+    size = lax.axis_size("tensor")
+    send = lambda x, pairs: lax.ppermute(x, "tensor", pairs)
+    up = [(i, (i + 2) % size) for i in range(size)]
+    down = [(i, (i - 2) % size) for i in range(size)]
+    across = [(i, i ^ 1) for i in range(size)]
+    half = own.shape[0] // 2
+    from_up, from_down, beside = send(own, up), send(own, down), send(own, across)
+    far = jnp.concatenate([send(from_up[:half], up), send(from_down[half:], down)], axis=0)
+    beside_up, beside_down = send(beside, up), send(beside, down)
+    beside_far = send(far, across)
+    me = lax.axis_index("tensor")
+    x, y = me // 2, me % 2
+    spot = lambda k, other: (x + k) % (size // 2) * 2 + (y + other) % 2
+    order = [spot(k, other) for k in (0, 3, 1, 2) for other in (0, 1)]
+    arrays = [own, beside, from_up, beside_up, from_down, beside_down, far, beside_far]
+    return arrays, jnp.stack(order).astype(jnp.int32)
 
 
 def local(
@@ -290,25 +353,28 @@
 
     share = lax.dynamic_slice_in_dim(out_weight, lax.axis_index("dp") * (depth // dp), depth // dp, 0)
     share = share.reshape(depth // dp, tensor, width).transpose(1, 0, 2)
+
+    def by_owner(ids):
+        ids = ids.reshape(steps, tensor, per).transpose(1, 0, 2).reshape(tensor, steps * per)
+        block, lane = ids // LANES, ids % LANES
+        return (block // PACK * LANES + lane) * PACK + block % PACK
+
+    codes = jnp.concatenate([by_owner(tokens), by_owner(frames)], axis=1)
+    codes = lax.all_to_all(jnp.broadcast_to(codes[None], (dp,) + codes.shape), "dp", 0, 0, tiled=True)
+    codes = codes.reshape(dp * tensor, codes.shape[2])
     share = lax.all_to_all(share, "tensor", 0, 0, tiled=True)
     weight = lax.all_gather(share, "dp")
-
-    def by_owner(ids):
-        return ids.reshape(steps, tensor, per).transpose(1, 0, 2).reshape(tensor, steps * per)
-
-    ids = jnp.concatenate([by_owner(tokens), by_owner(frames)], axis=1)
-    lane = jnp.arange(LANES, dtype=jnp.int32)[None, :]
-    codes = (ids // LANES) * LANES + (lane - ids) % LANES
-    codes = lax.all_gather(codes, "dp", axis=0, tiled=True)
-    emb = embed(codes, text_table, codec_table)
-    emb = lax.all_to_all(emb, BOTH, 0, 0, tiled=True)
+    text_rows, codec_rows = turn_tables(text_table, codec_table)
 
     attended = attention(query, new_keys, new_values, cache_keys, cache_values, cache_lengths)
-    attended = attended.reshape(rows, depth)
-    attended = lax.all_to_all(
-        jnp.broadcast_to(attended[None], (tensor, rows, depth)), "tensor", 0, 0, tiled=True
-    )
-    hidden, parts = project(attended, weight, residual.reshape(rows, width), bridge_weight)
+    attended, codes, share = lax.optimization_barrier((attended, codes, share))
+    attended, order = gather_tensor(attended.reshape(rows, depth))
+    chunks = 4
+    emb = [
+        embed(c, text_rows, codec_rows) for c in jnp.split(codes, chunks, axis=0)
+    ]
+    emb = lax.all_to_all(jnp.concatenate(emb, axis=0), BOTH, 0, 0, tiled=True)
+    hidden, parts = project(attended, order, weight, residual.reshape(rows, width), bridge_weight)
     parts = lax.all_to_all(
         parts.reshape(tensor, steps * per, talk), "tensor", 0, 0, tiled=True
     )

time: 270 us -> 240 us (0.89)
  blocking collectives: 87.8 us -> 18.2 us
  starting transfers between devices: 20.2 us -> 32 us
  waiting for transfers between devices: 52.9 us -> 64.3 us
  local copies, waits for them, and re-layouts: 10.9 us -> 18.1 us
  Pallas kernels: 83.4 us -> 90 us
    all_gather x1 -> x0, blocking collectives: 69.6 us -> none  [local(): codes = lax.all_gather(codes, 'dp', axis=0, tiled=True)]
    ppermute x0 -> x8, starting transfers between devices: none -> 13.5 us  [gather_tensor(): send = lambda x, pairs: lax.ppermute(x, 'tensor', pairs)]
    ppermute x0 -> x8, waiting for transfers between devices: none -> 11.4 us  [gather_tensor(): send = lambda x, pairs: lax.ppermute(x, 'tensor', pairs)]
    pallas_call x1 -> x2, Pallas kernels: 18.9 us -> 28 us  [the longest x1 19.8 us: project(): pl.pallas_call(functools.partial(project_kernel, owners=owners), grid_spe...]
    pallas_call x1 -> x4, Pallas kernels: 51.4 us -> 45.6 us  [embed(): pl.pallas_call(embed_kernel, in_specs=[pl.BlockSpec(memory_space=pltpu.SM...]
    unnamed x27 -> x26, local copies, waits for them, and re-layouts: 6.19 us -> 9.76 us
    pallas_call x1, Pallas kernels: 5.46 us -> 8.72 us  [finish(): pl.pallas_call(functools.partial(finish_kernel, feats=feats), grid=(block...]
  transfers between devices with their start and end apart: 4 -> 12, of which waited for: 1 -> 3; matrix products, arithmetic and copies ran while one was open for 1% -> 4% of each run, Pallas kernels for 29% -> 34%
where the time goes in v2:
time: 240 us; the launch traced here: 239 us
  Pallas kernels  90 us (38%)
  waiting for transfers between devices  64.3 us (27%)
  starting transfers between devices  32 us (13%)
  blocking collectives  18.2 us (8%)
  local copies, waits for them, and re-layouts  18.1 us (8%)
  between operations  14.4 us (6%)
    all_to_all x1, waiting for transfers between devices, local(): lax.all_to_all(parts.reshape(tensor, steps * per, talk), 'tensor', 0, 0,...  52.9 us
    pallas_call x4, Pallas kernels, embed(): pl.pallas_call(embed_kernel, in_specs=[pl.BlockSpec(memory_space=pltpu.SM...  45.6 us
    pallas_call x1, Pallas kernels, project(): pl.pallas_call(functools.partial(project_kernel, owners=owners), grid_spe...  19.8 us
    all_to_all x1, blocking collectives, local(): share = lax.all_to_all(share, 'tensor', 0, 0, tiled=True)  18.2 us
    ppermute x8, starting transfers between devices, gather_tensor(): send = lambda x, pairs: lax.ppermute(x, 'tensor', pairs)  13.5 us
    ppermute x8, waiting for transfers between devices, gather_tensor(): send = lambda x, pairs: lax.ppermute(x, 'tensor', pairs)  11.4 us
    unnamed x26, local copies, waits for them, and re-layouts  9.76 us
    pallas_call x1, Pallas kernels, finish(): pl.pallas_call(functools.partial(finish_kernel, feats=feats), grid=(block...  8.72 us
  transfers between devices with their start and end apart: 12, of which 3 were waited for; matrix products, arithmetic and copies ran while one was open for 4% of the time, Pallas kernels for 34%

profile of v2, /device:TPU:0, one launch (start us, length us, event | category | flops | bytes accessed | tf_op | source)
XLA Modules:
  0.0 239.1 jit_solution(15711543227620422694)
XLA Ops:
  7.3 1.2 constant_dynamic-slice_fusion
  9.1 18.2 %all_to_all.20 = bf16[8,32,1024]{2,1,0:T(8,128)(2,1)} all-to-all(bf16[8,32,1024]{2,1,0:T(8,128)(2,1)S(1)} %copy.24), channel_id=1, replica_groups=mesh['dp'=16,'tensor'=8] {'tensor'}, dimensions={0} | all-to-all | bytes 1048576 | tf_op jit(solution)/shard_map/all_to_all | solution.py:365
  29.7 5.5 %all-to-all-start = ((s32[16,8,128]{2,1,0:T(8,128)}), s32[16,8,128]{2,1,0:T(8,128)S(1)}, u32[]{:S(2)}, u32[]{:S(2)}) async-start(s32[16,8,128]{2,1,0:T(8,128)} %broadcast_in_dim.26), calls=%async_computation | async-start | bytes 131072 | tf_op jit(solution)/shard_map/all_to_all | solution.py:363
  36.1 1.3 lt.115
  39.8 1.6 copy-done.4
  41.4 7.7 %attention.1 = bf16[4,128,512]{2,1,0:T(8,128)(2,1)S(1)} custom-call(s32[8,1,1024]{2,1,0:T(1,128)S(1)} %compare_select_fusion.key_ref, bf16[4,128,512]{2,1,0:T(8,128)(2,1)S(1)} %copy-done.5, bf16[128,64,128]{2,1,0:T(8,128)(2,1)S(1)} %copy-done.3, bf16[128,64,128]{2,1,0:T(8,128)(2,1)S(1)} %copy-done.4, bf16[4,128,128]{2,1,0:T(8,128)(2,1)S(1)} %copy-done.8, ...), custom_call_target="tpu_custom_call" | custom-call | flops 2147483648 | bytes 6291456 | tf_op jit(solution)/shard_map/attention/pallas_call | solution.py:75
  50.1 3.0 %collective-permute-start.3 = (bf16[512,512]{1,0:T(8,128)(2,1)}, bf16[512,512]{1,0:T(8,128)(2,1)S(1)}, u32[]{:S(2)}, u32[]{:S(2)}) collective-permute-start(bf16[512,512]{1,0:T(8,128)(2,1)} %bitcast.26), channel_id=1, source_target_pairs={{0,6},{1,7},{2,0},{3,1},{4,2},{5,3},{6,4},{7,5},{8,14},{9,15},{10,... | collective-permute-start | bytes 1572872 | tf_op jit(solution)/shard_map/ppermute | solution.py:313
  53.1 1.8 collective-permute-start
  55.0 10.6 %collective-permute-done.1.refs_2_ = bf16[512,512]{1,0:T(8,128)(2,1)S(1)} collective-permute-done((bf16[512,512]{1,0:T(8,128)(2,1)}, bf16[512,512]{1,0:T(8,128)(2,1)S(1)}, u32[]{:S(2)}, u32[]{:S(2)}) %collective-permute-start.1) | collective-permute-done | bytes 524320 | tf_op jit(solution)/shard_map/ppermute | solution.py:313
  65.7 3.3 %collective-permute-start.6 = (bf16[256,512]{1,0:T(8,128)(2,1)S(1)}, bf16[256,512]{1,0:T(8,128)(2,1)S(1)}, u32[]{:S(2)}, u32[]{:S(2)}) collective-permute-start(bf16[256,512]{1,0:T(8,128)(2,1)S(1)} %slice.9), channel_id=1, source_target_pairs={{0,6},{1,7},{2,0},{3,1},{4,2},{5,3},{6,4},{7,5},{8,14},{9,15},{10,... | collective-permute-start | bytes 786440 | tf_op jit(solution)/shard_map/ppermute | solution.py:313
  69.0 2.5 %copy-done.1 = bf16[28,76032]{1,0:T(8,128)(2,1)S(1)} copy-done((bf16[28,76032]{1,0:T(8,128)(2,1)S(1)}, bf16[28,76032]{1,0:T(8,128)(2,1)}, u32[]{:S(2)}) %copy-start.1) | copy-done | bytes 4257816
  71.5 8.3 %turn_tables.1 = (f32[19072,128]{1,0:T(8,128)}, f32[2176,128]{1,0:T(8,128)S(1)}) custom-call(bf16[28,76032]{1,0:T(8,128)(2,1)S(1)} %copy-done.1, bf16[28,8448]{1,0:T(8,128)(2,1)S(1)} %copy-done.2), custom_call_target="tpu_custom_call" | custom-call | bytes 16777216 | tf_op jit(solution)/shard_map/turn_tables/pallas_call | solution.py:128
  80.5 3.2 %collective-permute-start.4 = (bf16[512,512]{1,0:T(8,128)(2,1)S(1)}, bf16[512,512]{1,0:T(8,128)(2,1)}, u32[]{:S(2)}, u32[]{:S(2)}) collective-permute-start(bf16[512,512]{1,0:T(8,128)(2,1)S(1)} %collective-permute-done.refs_1_), channel_id=1, source_target_pairs={{0,6},{1,7},{2,0},{3,1},{4,2},{5,3},{6,4},{7,5},{8,14},{9,15},{10,... | collective-permute-start | bytes 1572872 | tf_op jit(solution)/shard_map/ppermute | solution.py:313
  85.2 1.8 collective-permute-start.7
  87.0 3.8 %copy-done = f32[19072,128]{1,0:T(8,128)S(1)} copy-done((f32[19072,128]{1,0:T(8,128)S(1)}, f32[19072,128]{1,0:T(8,128)}, u32[]{:S(2)}) %copy-start) | copy-done | bytes 9764888
  90.9 11.4 %embed.4 = bf16[32,32,128]{2,1,0:T(8,128)(2,1)S(1)} custom-call(s32[32,128]{1,0:T(8,128)S(1)} %get-tuple-element.14.code_ref, f32[19072,128]{1,0:T(8,128)S(1)} %copy-done, f32[2176,128]{1,0:T(8,128)S(1)} %get-tuple-element.13.codec_ref), custom_call_target="tpu_custom_call" | custom-call | bytes 8388608 | tf_op jit(solution)/shard_map/embed/pallas_call | solution.py:168
  102.3 11.4 %embed.5 = bf16[32,32,128]{2,1,0:T(8,128)(2,1)S(1)} custom-call(s32[32,128]{1,0:T(8,128)S(1)} %get-tuple-element.17.code_ref, f32[19072,128]{1,0:T(8,128)S(1)} %copy-done, f32[2176,128]{1,0:T(8,128)S(1)} %get-tuple-element.13.codec_ref), custom_call_target="tpu_custom_call" | custom-call | bytes 8388608 | tf_op jit(solution)/shard_map/embed/pallas_call | solution.py:168
  113.7 11.4 %embed.6 = bf16[32,32,128]{2,1,0:T(8,128)(2,1)S(1)} custom-call(s32[32,128]{1,0:T(8,128)S(1)} %get-tuple-element.16.code_ref, f32[19072,128]{1,0:T(8,128)S(1)} %copy-done, f32[2176,128]{1,0:T(8,128)S(1)} %get-tuple-element.13.codec_ref), custom_call_target="tpu_custom_call" | custom-call | bytes 8388608 | tf_op jit(solution)/shard_map/embed/pallas_call | solution.py:168
  125.1 11.4 %embed.7 = bf16[32,32,128]{2,1,0:T(8,128)(2,1)S(1)} custom-call(s32[32,128]{1,0:T(8,128)S(1)} %get-tuple-element.15.code_ref, f32[19072,128]{1,0:T(8,128)S(1)} %copy-done, f32[2176,128]{1,0:T(8,128)S(1)} %get-tuple-element.13.codec_ref), custom_call_target="tpu_custom_call" | custom-call | bytes 8388608 | tf_op jit(solution)/shard_map/embed/pallas_call | solution.py:168
  137.6 6.8 %all-to-all-start.3 = ((bf16[128,32,128]{2,1,0:T(8,128)(2,1)}), bf16[128,32,128]{2,1,0:T(8,128)(2,1)S(1)}, u32[]{:S(2)}, u32[]{:S(2)}) async-start(bf16[128,32,128]{2,1,0:T(8,128)(2,1)} %pad_maximum_fusion), calls=%async_computation.3 | async-start | bytes 2097152 | tf_op jit(solution)/shard_map/all_to_all | solution.py:376
  144.6 19.8 %project.1 = (bf16[512,1024]{1,0:T(8,128)(2,1)}, bf16[8,4,16,3584]{3,2,1,0:T(8,128)(2,1)}) custom-call(s32[8]{0:T(128)S(1)} %stack.35.order_ref, bf16[512,512]{1,0:T(8,128)(2,1)S(1)} %bitcast.28, bf16[512,512]{1,0:T(8,128)(2,1)S(1)} %collective-permute-done.refs_1_, bf16[512,512]{1,0:T(8,128)(2,1)S(1)} %collective-permute-done.1.refs_2_, ...), custom_call_target="tpu_custom_call" | custom-call | flops 8000000000 | bytes 25165824 | tf_op jit(solution)/shard_map/project/pallas_call | solution.py:222
  164.4 6.2 %all-to-all-start.2 = ((bf16[8,64,3584]{2,1,0:T(8,128)(2,1)}), bf16[8,64,3584]{2,1,0:T(8,128)(2,1)}, u32[]{:S(2)}, u32[]{:S(2)}) async-start(bf16[8,64,3584]{2,1,0:T(8,128)(2,1)} %bitcast.29), calls=%async_computation.2 | async-start | bytes 7340032 | tf_op jit(solution)/shard_map/all_to_all | solution.py:378
  170.6 52.9 %all-to-all-done.2.part_ref = bf16[8,64,3584]{2,1,0:T(8,128)(2,1)} async-done(((bf16[8,64,3584]{2,1,0:T(8,128)(2,1)}), bf16[8,64,3584]{2,1,0:T(8,128)(2,1)}, u32[]{:S(2)}, u32[]{:S(2)}) %all-to-all-start.2) | async-done | bytes 3670048 | tf_op jit(solution)/shard_map/all_to_all | solution.py:378
  223.5 8.7 %finish.1 = bf16[64,3584]{1,0:T(8,128)(2,1)} custom-call(bf16[8,64,3584]{2,1,0:T(8,128)(2,1)} %all-to-all-done.2.part_ref, bf16[128,32,128]{2,1,0:T(8,128)(2,1)S(1)} %all-to-all-done.3.emb_ref, bf16[1,3584]{1,0:T(2,128)(2,1)S(1)} %reshape.118.gain_ref), custom_call_target="tpu_custom_call" | custom-call | tf_op jit(solution)/shard_map/finish/pallas_call | solution.py:292
  (63 shorter events, 10.9 us)
Async XLA Ops:
  7.2 32.6 %copy-start.5 = (bf16[4,128,512]{2,1,0:T(8,128)(2,1)S(1)}, bf16[4,128,512]{2,1,0:T(8,128)(2,1)}, u32[]{:S(2)}) copy-start(bf16[4,128,512]{2,1,0:T(8,128)(2,1)} %q_ref.1) | copy-start | bytes 1572868
  7.2 32.6 %copy-start.8 = (bf16[4,128,128]{2,1,0:T(8,128)(2,1)S(1)}, bf16[4,128,128]{2,1,0:T(8,128)(2,1)}, u32[]{:S(2)}) copy-start(bf16[4,128,128]{2,1,0:T(8,128)(2,1)} %nk_ref.1) | copy-start | bytes 393220
  7.2 32.6 %copy-start.9 = (bf16[4,128,128]{2,1,0:T(8,128)(2,1)S(1)}, bf16[4,128,128]{2,1,0:T(8,128)(2,1)}, u32[]{:S(2)}) copy-start(bf16[4,128,128]{2,1,0:T(8,128)(2,1)} %nv_ref.1) | copy-start | bytes 393220
  7.2 32.6 %copy-start.3 = (bf16[128,64,128]{2,1,0:T(8,128)(2,1)S(1)}, bf16[128,64,128]{2,1,0:T(8,128)(2,1)}, u32[]{:S(2)}) copy-start(bf16[128,64,128]{2,1,0:T(8,128)(2,1)} %ck_ref.1) | copy-start | bytes 6291460
  7.2 137.4 %all-gather.3.cloned.1.call-start = ((), (), s32[]{:S(2)}) async-start(), calls=%async_computation.4 | async-start | bytes 8912896 | tf_op jit(solution)/shard_map/all_gather | solution.py:366
  28.9 40.1 %copy-start.2 = (bf16[28,8448]{1,0:T(8,128)(2,1)S(1)}, bf16[28,8448]{1,0:T(8,128)(2,1)}, u32[]{:S(2)}) copy-start(bf16[28,8448]{1,0:T(8,128)(2,1)} %codec_ref.1) | copy-start | bytes 1419268
  29.7 20.2 %all-to-all-start = ((s32[16,8,128]{2,1,0:T(8,128)}), s32[16,8,128]{2,1,0:T(8,128)S(1)}, u32[]{:S(2)}, u32[]{:S(2)}) async-start(s32[16,8,128]{2,1,0:T(8,128)} %broadcast_in_dim.26), calls=%async_computation | async-start | bytes 131072 | tf_op jit(solution)/shard_map/all_to_all | solution.py:363
  39.8 1.6 copy-start.4
  49.1 0.8 copy-start.6
  49.9 15.7 %collective-permute-start.1 = (bf16[512,512]{1,0:T(8,128)(2,1)}, bf16[512,512]{1,0:T(8,128)(2,1)S(1)}, u32[]{:S(2)}, u32[]{:S(2)}) collective-permute-start(bf16[512,512]{1,0:T(8,128)(2,1)} %bitcast.25), channel_id=1, source_target_pairs={{0,2},{1,3},{2,4},{3,5},{4,6},{5,7},{6,0},{7,1},{8,10},{9,11},{10,... | collective-permute-start | bytes 1572872 | tf_op jit(solution)/shard_map/ppermute | solution.py:313
  50.1 15.5 %collective-permute-start.3 = (bf16[512,512]{1,0:T(8,128)(2,1)}, bf16[512,512]{1,0:T(8,128)(2,1)S(1)}, u32[]{:S(2)}, u32[]{:S(2)}) collective-permute-start(bf16[512,512]{1,0:T(8,128)(2,1)} %bitcast.26), channel_id=1, source_target_pairs={{0,6},{1,7},{2,0},{3,1},{4,2},{5,3},{6,4},{7,5},{8,14},{9,15},{10,... | collective-permute-start | bytes 1572872 | tf_op jit(solution)/shard_map/ppermute | solution.py:313
  53.1 27.3 %collective-permute-start = (bf16[512,512]{1,0:T(8,128)(2,1)}, bf16[512,512]{1,0:T(8,128)(2,1)S(1)}, u32[]{:S(2)}, u32[]{:S(2)}) collective-permute-start(bf16[512,512]{1,0:T(8,128)(2,1)} %bitcast.27), channel_id=1, source_target_pairs={{0,1},{1,0},{2,3},{3,2},{4,5},{5,4},{6,7},{7,6},{8,9},{9,8},{10,11... | collective-permute-start | bytes 1572872 | tf_op jit(solution)/shard_map/ppermute | solution.py:313
  65.6 18.1 %collective-permute-start.5 = (bf16[256,512]{1,0:T(8,128)(2,1)S(1)}, bf16[256,512]{1,0:T(8,128)(2,1)S(1)}, u32[]{:S(2)}, u32[]{:S(2)}) collective-permute-start(bf16[256,512]{1,0:T(8,128)(2,1)S(1)} %slice.8), channel_id=1, source_target_pairs={{0,2},{1,3},{2,4},{3,5},{4,6},{5,7},{6,0},{7,1},{8,10},{9,11},{10,... | collective-permute-start | bytes 786440 | tf_op jit(solution)/shard_map/ppermute | solution.py:313
  65.7 36.6 %copy-start.10 = (bf16[512,512]{1,0:T(8,128)(2,1)}, bf16[512,512]{1,0:T(8,128)(2,1)S(1)}, u32[]{:S(2)}) copy-start(bf16[512,512]{1,0:T(8,128)(2,1)S(1)} %collective-permute-done.3.refs_4_) | copy-start | bytes 1572868
  65.7 18.7 %collective-permute-start.6 = (bf16[256,512]{1,0:T(8,128)(2,1)S(1)}, bf16[256,512]{1,0:T(8,128)(2,1)S(1)}, u32[]{:S(2)}, u32[]{:S(2)}) collective-permute-start(bf16[256,512]{1,0:T(8,128)(2,1)S(1)} %slice.9), channel_id=1, source_target_pairs={{0,6},{1,7},{2,0},{3,1},{4,2},{5,3},{6,4},{7,5},{8,14},{9,15},{10,... | collective-permute-start | bytes 786440 | tf_op jit(solution)/shard_map/ppermute | solution.py:313
  69.0 2.5 %copy-start.1 = (bf16[28,76032]{1,0:T(8,128)(2,1)S(1)}, bf16[28,76032]{1,0:T(8,128)(2,1)}, u32[]{:S(2)}) copy-start(bf16[28,76032]{1,0:T(8,128)(2,1)} %text_ref.1) | copy-start | bytes 12773380
  80.5 64.1 %collective-permute-start.2 = (bf16[512,512]{1,0:T(8,128)(2,1)S(1)}, bf16[512,512]{1,0:T(8,128)(2,1)}, u32[]{:S(2)}, u32[]{:S(2)}) collective-permute-start(bf16[512,512]{1,0:T(8,128)(2,1)S(1)} %collective-permute-done.refs_1_), channel_id=1, source_target_pairs={{0,2},{1,3},{2,4},{3,5},{4,6},{5,7},{6,0},{7,1},{8,10},{9,11},{10,... | collective-permute-start | bytes 1572872 | tf_op jit(solution)/shard_map/ppermute | solution.py:313
  80.5 64.1 %collective-permute-start.4 = (bf16[512,512]{1,0:T(8,128)(2,1)S(1)}, bf16[512,512]{1,0:T(8,128)(2,1)}, u32[]{:S(2)}, u32[]{:S(2)}) collective-permute-start(bf16[512,512]{1,0:T(8,128)(2,1)S(1)} %collective-permute-done.refs_1_), channel_id=1, source_target_pairs={{0,6},{1,7},{2,0},{3,1},{4,2},{5,3},{6,4},{7,5},{8,14},{9,15},{10,... | collective-permute-start | bytes 1572872 | tf_op jit(solution)/shard_map/ppermute | solution.py:313
  85.2 59.4 %collective-permute-start.7 = (bf16[512,512]{1,0:T(8,128)(2,1)}, bf16[512,512]{1,0:T(8,128)(2,1)}, u32[]{:S(2)}, u32[]{:S(2)}) collective-permute-start(bf16[512,512]{1,0:T(8,128)(2,1)} %constant_dynamic-update-slice_fusion.refs_6_), channel_id=1, source_target_pairs={{0,1},{1,0},{2,3},{3,2},{4,5},{5,4},{6,7},{7,6},{8,9},{9,8},{10,11... | collective-permute-start | bytes 1572872 | tf_op jit(solution)/shard_map/ppermute | solution.py:313
  87.0 3.8 %copy-start = (f32[19072,128]{1,0:T(8,128)S(1)}, f32[19072,128]{1,0:T(8,128)}, u32[]{:S(2)}) copy-start(f32[19072,128]{1,0:T(8,128)} %get-tuple-element.12.text_ref) | copy-start | bytes 29294596
  125.1 19.5 %copy-start.7 = (bf16[4,128,512]{2,1,0:T(8,128)(2,1)S(1)}, bf16[4,128,512]{2,1,0:T(8,128)(2,1)}, u32[]{:S(2)}) copy-start(bf16[4,128,512]{2,1,0:T(8,128)(2,1)} %copy-done.6) | copy-start | bytes 1572868
  137.6 26.8 %all-to-all-start.3 = ((bf16[128,32,128]{2,1,0:T(8,128)(2,1)}), bf16[128,32,128]{2,1,0:T(8,128)(2,1)S(1)}, u32[]{:S(2)}, u32[]{:S(2)}) async-start(bf16[128,32,128]{2,1,0:T(8,128)(2,1)} %pad_maximum_fusion), calls=%async_computation.3 | async-start | bytes 2097152 | tf_op jit(solution)/shard_map/all_to_all | solution.py:376
  164.4 6.2 %copy-start.11 = (bf16[3584]{0:T(1024)(128)(2,1)S(1)}, bf16[3584]{0:T(1024)(128)(2,1)}, u32[]{:S(2)}) copy-start(bf16[3584]{0:T(1024)(128)(2,1)} %param.27) | copy-start | bytes 21508
  164.4 59.1 %all-to-all-start.2 = ((bf16[8,64,3584]{2,1,0:T(8,128)(2,1)}), bf16[8,64,3584]{2,1,0:T(8,128)(2,1)}, u32[]{:S(2)}, u32[]{:S(2)}) async-start(bf16[8,64,3584]{2,1,0:T(8,128)(2,1)} %bitcast.29), calls=%async_computation.2 | async-start | bytes 7340032 | tf_op jit(solution)/shard_map/all_to_all | solution.py:378
Sparse Core Ops, SparseCore 0:
  27.4 63.1 all-gather.2

commit v3 on v0

v3 whole, which is shorter than its diff:
```python
import functools

import jax
import jax.numpy as jnp
from jax import lax
from jax.experimental import pallas as pl
from jax.experimental.pallas import tpu as pltpu
from jax.sharding import PartitionSpec as P

QH = 32
KVH = 8
HD = 128
CAP = 64
GROUP = QH // KVH
STEPS = 4
SB = 16
LANES = 128
FPAD = 32
PACK = LANES // FPAD
BF16 = jnp.bfloat16
F32 = jnp.float32
BOTH = ("dp", "tensor")
MIB = 1 << 20


def iota(shape, dim):
    return lax.broadcasted_iota(jnp.int32, shape, dim)


def attention_kernel(len_ref, q_ref, ck_ref, cv_ref, nk_ref, nv_ref, out_ref):
    rows = STEPS * GROUP * SB
    scale = 1.0 / HD**0.5
    queries = jnp.concatenate(
        [q_ref[t, :, h * HD : (h + 1) * HD] for t in range(STEPS) for h in range(GROUP)], axis=0
    )
    cached_k = ck_ref[...].reshape(SB * CAP, HD)
    cached_v = cv_ref[...].reshape(SB * CAP, HD)
    fresh_k = nk_ref[...].reshape(STEPS * SB, HD)
    fresh_v = nv_ref[...].reshape(STEPS * SB, HD)
    contract = (((1,), (1,)), ((), ()))
    score_c = lax.dot_general(queries, cached_k, contract, preferred_element_type=F32) * scale
    score_n = lax.dot_general(queries, fresh_k, contract, preferred_element_type=F32) * scale
    own = iota((rows, 1), 0) % SB
    start = own * CAP
    stop = start + jnp.concatenate([len_ref[:, :1]] * (STEPS * GROUP), axis=0)
    spot = iota((rows, SB * CAP), 1)
    score_c = jnp.where((spot >= start) & (spot < stop), score_c, -1e30)
    row, col = iota((rows, STEPS * SB), 0), iota((rows, STEPS * SB), 1)
    seen = (row % SB == col % SB) & (col // SB <= row // (GROUP * SB))
    score_n = jnp.where(seen, score_n, -1e30)
    top = jnp.maximum(
        jnp.max(score_c, axis=-1, keepdims=True), jnp.max(score_n, axis=-1, keepdims=True)
    )
    exp_c = jnp.exp(score_c - top)
    exp_n = jnp.exp(score_n - top)
    total = jnp.sum(exp_c, axis=-1, keepdims=True) + jnp.sum(exp_n, axis=-1, keepdims=True)
    inverse = 1.0 / total
    weight_c = (exp_c * inverse).astype(BF16)
    weight_n = (exp_n * inverse).astype(BF16)
    attended = jnp.dot(weight_c, cached_v, preferred_element_type=F32)
    attended = attended + jnp.dot(weight_n, fresh_v, preferred_element_type=F32)
    attended = attended.astype(BF16)
    for t in range(STEPS):
        for h in range(GROUP):
            at = (t * GROUP + h) * SB
            out_ref[0, t, :, h * HD : (h + 1) * HD] = attended[at : at + SB]


def attention(query, new_keys, new_values, cache_keys, cache_values, cache_lengths):
    steps, streams, width = query.shape
    blocks = streams // SB
    lengths = jnp.broadcast_to(cache_lengths[:, None], (streams, LANES))
    fresh = pl.BlockSpec((steps, SB, HD), lambda i: (0, i, 0))
    cached = pl.BlockSpec((SB, CAP, HD), lambda i: (i, 0, 0))
    return pl.pallas_call(
        attention_kernel,
        grid=(blocks,),
        in_specs=[
            pl.BlockSpec((SB, LANES), lambda i: (i, 0)),
            pl.BlockSpec((steps, SB, width), lambda i: (0, i, 0)),
            cached,
            cached,
            fresh,
            fresh,
        ],
        out_specs=pl.BlockSpec((1, steps, SB, width), lambda i: (i, 0, 0, 0)),
        out_shape=jax.ShapeDtypeStruct((blocks, steps, SB, width), BF16),
        compiler_params=pltpu.CompilerParams(vmem_limit_bytes=32 * MIB),
        cost_estimate=pl.CostEstimate(flops=8 * 10**9, bytes_accessed=6 * MIB, transcendentals=0),
        name="attention",
    )(lengths, query, cache_keys, cache_values, new_keys, new_values)


def look_kernel(shift_ref, id_ref, table_ref, *refs, group):
    other_ref = refs[0] if len(refs) == 4 else None
    out_ref, turned, found = refs[-3:]
    feats, entries = table_ref.shape
    owners = out_ref.shape[0]
    rows = 2 * out_ref.shape[1]
    per = rows // STEPS
    batch = found.shape[0] // rows
    pad = jnp.zeros((FPAD - feats, LANES), BF16)
    slot = iota((LANES, LANES), 1) // FPAD

    def turn(first, count):
        parts = []
        for k in range(count):
            at = pl.multiple_of((first + k) * LANES, LANES)
            parts += [table_ref[:, pl.ds(at, LANES)], pad]
        if count < PACK:
            parts.append(jnp.zeros(((PACK - count) * FPAD, LANES), BF16))
        packed = jnp.concatenate(parts, axis=0).T.astype(F32)
        for k in range(count):
            at = pl.multiple_of((first + k) * LANES, LANES)
            turned[pl.ds(at, LANES), :] = jnp.where(slot == k, packed, 0.0)

    def turn_units(i, _):
        for u in range(4):
            turn((i * 4 + u) * PACK, PACK)
        return 0

    blocks = entries // LANES
    loops = blocks // (4 * PACK)
    lax.fori_loop(0, loops, turn_units, 0)
    for first in range(loops * 4 * PACK, blocks, PACK):
        turn(first, min(PACK, blocks - first))

    place = (iota((LANES, LANES), 1) - shift_ref[0]) & (LANES - 1)
    row = iota((LANES, LANES), 0)
    move = (row % FPAD == place % FPAD) & (place // FPAD % 2 == group)
    move = jnp.where(move, 1.0, 0.0).astype(BF16)
    place = (iota((rows // 2, LANES), 1) - shift_ref[0]) & (LANES - 1)

    def look(i, _):
        def find(j, _):
            o = i * batch + j
            base = o // (LANES // per) * (STEPS * LANES) + o % (LANES // per) * per
            to = pl.multiple_of(j * rows, rows)
            for t in range(STEPS):
                for s in range(per):
                    at = id_ref[base + (t * LANES + s)]
                    found[pl.ds(to + (t * per + s), 1), :] = turned[pl.ds(at, 1), :]
            return 0

        lax.fori_loop(0, batch, find, 0)
        moved = jnp.dot(found[...].astype(BF16), move, preferred_element_type=F32)
        for j in range(batch):
            a = moved[j * rows : j * rows + rows // 2]
            b = moved[j * rows + rows // 2 : (j + 1) * rows]
            both = jnp.where(place < 2 * FPAD, a, b)
            if other_ref is not None:
                both = both + other_ref[i * batch + j].astype(F32)
            out_ref[i * batch + j] = both.astype(BF16)
        return 0

    lax.fori_loop(0, owners // batch, look, 0)


def look_up(ids, table, shift, owners, group, *other):
    groups, _, streams = ids.shape
    rows = streams * STEPS // owners
    vmem = pl.BlockSpec(memory_space=pltpu.VMEM)
    smem = pl.BlockSpec(memory_space=pltpu.SMEM)
    return pl.pallas_call(
        functools.partial(look_kernel, group=group),
        in_specs=[smem, smem, vmem] + [vmem] * len(other),
        out_specs=vmem,
        out_shape=jax.ShapeDtypeStruct((groups * owners, rows // 2, LANES), BF16),
        scratch_shapes=[
            pltpu.VMEM((table.shape[1], LANES), F32),
            pltpu.VMEM((8 * rows, LANES), F32),
        ],
        compiler_params=pltpu.CompilerParams(vmem_limit_bytes=(table.shape[1] // 2048 + 14) * MIB),
        cost_estimate=pl.CostEstimate(
            flops=0, bytes_accessed=(20 + table.shape[1] // 3000) * MIB, transcendentals=0
        ),
        name="look_up",
    )(shift, ids.reshape(-1), table, *other)


def project_kernel(order_ref, subs_ref, *refs, owners):
    a_refs = refs[:owners]
    *w_refs, res_ref, bridge_ref, hidden_ref, part_ref, a_all, w_all = refs[owners:]
    depth = a_refs[0].shape[1]
    cols = w_all.shape[2]
    for k in range(owners):
        at = pl.multiple_of(order_ref[k] * depth, depth)
        a_all[:, pl.ds(at, depth)] = a_refs[k][...]

    def columns(n, _):
        here = pl.ds(pl.multiple_of(n * cols, cols), cols)
        sub = 0
        for w_ref in w_refs:
            for k in range(w_ref.shape[1]):
                size = w_ref.shape[2]
                at = pl.multiple_of(subs_ref[sub] * size, size)
                w_all[:, pl.ds(at, size), :] = w_ref[:, k, :, here]
                sub += 1
        w = w_all[...].reshape(owners * depth, cols)
        prod = jnp.dot(a_all[...], w, preferred_element_type=F32)
        hidden_ref[:, here] = (res_ref[:, here].astype(F32) + prod).astype(BF16)
        return 0

    lax.fori_loop(0, hidden_ref.shape[1] // cols, columns, 0)
    wide = 512

    def bridge(n, _):
        here = pl.ds(pl.multiple_of(n * wide, wide), wide)
        part = jnp.dot(hidden_ref[...], bridge_ref[:, here], preferred_element_type=F32)
        part_ref[:, here] = part.astype(BF16)
        return 0

    lax.fori_loop(0, part_ref.shape[1] // wide, bridge, 0)


def project(attended, order, weights, subs, residual, bridge):
    owners = len(attended)
    rows, depth = attended[0].shape
    vmem = pl.BlockSpec(memory_space=pltpu.VMEM)
    smem = pl.BlockSpec(memory_space=pltpu.SMEM)
    return pl.pallas_call(
        functools.partial(project_kernel, owners=owners),
        in_specs=[smem, smem] + [vmem] * (owners + len(weights) + 2),
        out_specs=[vmem, vmem],
        out_shape=[
            jax.ShapeDtypeStruct(residual.shape, BF16),
            jax.ShapeDtypeStruct((rows, bridge.shape[1]), BF16),
        ],
        scratch_shapes=[
            pltpu.VMEM((rows, owners * depth), BF16),
            pltpu.VMEM((owners, depth, 256), BF16),
        ],
        compiler_params=pltpu.CompilerParams(vmem_limit_bytes=48 * MIB),
        cost_estimate=pl.CostEstimate(flops=12 * 10**9, bytes_accessed=24 * MIB, transcendentals=0),
        name="project",
    )(order, subs, *attended, *weights, residual, bridge)


def place_kernel(emb_ref, out_ref, *, feats):
    holders, half, _ = emb_ref.shape
    lane = iota((half, LANES), 1)
    for tile in range(holders * feats // LANES):
        start = tile * LANES
        found = [jnp.zeros((half, LANES), F32) for _ in range(PACK)]
        for h in range(start // feats, min((start + LANES - 1) // feats, holders - 1) + 1):
            row = emb_ref[h].astype(F32)
            low, high = max(h * feats - start, 0), min((h + 1) * feats - start, LANES)
            for g in range(PACK):
                spot = (lane - g * FPAD) & (LANES - 1)
                found[g] = jnp.where((spot >= low) & (spot < high), row, found[g])
        a = found[0] + pltpu.roll(found[1], LANES - FPAD, 1)
        b = found[2] + pltpu.roll(found[3], LANES - FPAD, 1)
        b = pltpu.roll(b, LANES // 2, 1)
        out_ref[:half, start : start + LANES] = a
        out_ref[half:, start : start + LANES] = b


def place(emb, talk):
    holders, half, _ = emb.shape
    blocks = 4
    return pl.pallas_call(
        functools.partial(place_kernel, feats=talk // holders),
        grid=(blocks,),
        in_specs=[pl.BlockSpec((holders // blocks, half, LANES), lambda i: (i, 0, 0))],
        out_specs=pl.BlockSpec((2 * half, talk // blocks), lambda i: (0, i)),
        out_shape=jax.ShapeDtypeStruct((2 * half, talk), F32),
        cost_estimate=pl.CostEstimate(flops=0, bytes_accessed=8 * MIB, transcendentals=0),
        name="place",
    )(emb)


def finish_kernel(part_ref, emb_ref, gain_ref, out_ref, mixed):
    sources, rows, talk = part_ref.shape
    square = jnp.zeros((rows, LANES), F32)
    for c in range(talk // LANES):
        cols = slice(c * LANES, (c + 1) * LANES)
        total = part_ref[0, :, cols].astype(F32)
        for s in range(1, sources):
            total = total + part_ref[s, :, cols].astype(F32)
        total = total + emb_ref[:, cols]
        mixed[:, cols] = total
        square = square + total * total
    mean = jnp.sum(square, axis=-1, keepdims=True) * (1.0 / talk)
    factor = lax.rsqrt(mean + 1e-06)
    for c in range(talk // LANES):
        cols = slice(c * LANES, (c + 1) * LANES)
        gain = gain_ref[:, cols].astype(F32)
        out_ref[:, cols] = (mixed[:, cols] * factor * gain).astype(BF16)


def finish(parts, emb, gain):
    _, rows, talk = parts.shape
    vmem = pl.BlockSpec(memory_space=pltpu.VMEM)
    return pl.pallas_call(
        finish_kernel,
        in_specs=[vmem, vmem, vmem],
        out_specs=vmem,
        out_shape=jax.ShapeDtypeStruct((rows, talk), BF16),
        scratch_shapes=[pltpu.VMEM((rows, talk), F32)],
        compiler_params=pltpu.CompilerParams(vmem_limit_bytes=32 * MIB),
        cost_estimate=pl.CostEstimate(flops=0, bytes_accessed=8 * MIB, transcendentals=0),
        name="finish",
    )(parts, emb, gain)


def tensor_pairs():
    size = lax.axis_size("tensor")
    up = [(i, (i + 2) % size) for i in range(size)]
    down = [(i, (i - 2) % size) for i in range(size)]
    return up, down, [(i, i ^ 1) for i in range(size)]


def send(x, pairs):
    return lax.ppermute(x, "tensor", pairs)


def gather_first(own):
    up, down, across = tensor_pairs()
    return send(own, up), send(own, down), send(own, across)


def gather_second(own, first):
    up, down, _ = tensor_pairs()
    from_up, from_down, beside = first
    half = own.shape[0] // 2
    far = jnp.concatenate([send(from_up[:half], up), send(from_down[half:], down)], axis=0)
    return [own, beside, from_up, send(beside, up), from_down, send(beside, down), far]


def gather_third(second):
    size = lax.axis_size("tensor")
    arrays = second + [send(second[-1], tensor_pairs()[2])]
    me = lax.axis_index("tensor")
    x, y = me // 2, me % 2
    spot = lambda k, other: (x + k) % (size // 2) * 2 + (y + other) % 2
    order = [spot(k, other) for k in (0, 3, 1, 2) for other in (0, 1)]
    return arrays, jnp.stack(order).astype(jnp.int32)


def share_kernel(subs_ref, w_ref, out_ref, sems):
    owners, parts, size, width = out_ref.shape
    copies = []
    for k in range(parts):
        rows = pl.ds(pl.multiple_of(subs_ref[k] * size, size), size)
        for t in range(owners):
            copies.append(
                pltpu.make_async_copy(
                    w_ref.at[rows, t * width : (t + 1) * width], out_ref.at[t, k], sems.at[t, k]
                )
            )
    for copy in copies:
        copy.start()
    for copy in copies:
        copy.wait()


def share_rows(out_weight, subs, size, width):
    owners = out_weight.shape[1] // width
    return pl.pallas_call(
        share_kernel,
        in_specs=[pl.BlockSpec(memory_space=pltpu.SMEM), pl.BlockSpec(memory_space=pl.ANY)],
        out_specs=pl.BlockSpec(memory_space=pltpu.VMEM),
        out_shape=jax.ShapeDtypeStruct((owners, subs.shape[0], size, width), BF16),
        scratch_shapes=[pltpu.SemaphoreType.DMA((owners, subs.shape[0]))],
        compiler_params=pltpu.CompilerParams(vmem_limit_bytes=16 * MIB),
        cost_estimate=pl.CostEstimate(flops=0, bytes_accessed=4 * MIB, transcendentals=0),
        name="share_rows",
    )(subs, out_weight)


def weight_first(out_weight, width):
    depth = out_weight.shape[0]
    tensor = out_weight.shape[1] // width
    size = depth // 8
    me = lax.axis_index("dp")
    core, odd = me % 2, me // 2 % 2
    sub_a, sub_b = core * 4 + odd, core * 4 + 3 - odd
    pair = jnp.stack([sub_a, sub_b]).astype(jnp.int32)
    share = lax.all_to_all(share_rows(out_weight, pair, size, width), "tensor", 0, 0, tiled=True)

    own = [sub_a, sub_b, core * 4 + 1 - odd, core * 4 + 2 + odd]
    return share, jnp.stack(own + [(k + 4) % 8 for k in own]).astype(jnp.int32)


def weight_second(share):
    count = lax.axis_size("dp")
    turn = lambda i, by: i // 8 * 8 + (i + 2 * by) % 8
    z_of = lambda i: i // 2 % 4
    pairs_a = [(i, turn(i, -1 if z_of(i) % 2 else 1)) for i in range(count)]
    pairs_b = [(i, turn(i, 1 if z_of(i) % 2 else -1)) for i in range(count)]
    beside_a = lax.ppermute(share[:, :1], "dp", pairs_a)
    beside_b = lax.ppermute(share[:, 1:], "dp", pairs_b)
    return [share, beside_a, beside_b]


def weight_third(weights):
    cores = [(i, i ^ 1) for i in range(lax.axis_size("dp"))]
    return weights + [lax.ppermute(x, "dp", cores) for x in weights]


def local(
    query,
    new_keys,
    new_values,
    cache_keys,
    cache_values,
    cache_lengths,
    residual,
    out_weight,
    bridge_weight,
    text_table,
    codec_table,
    tokens,
    frames,
    talk_gain,
):
    steps, streams, depth = query.shape
    width = residual.shape[2]
    talk = bridge_weight.shape[1]
    tensor = out_weight.shape[1] // width
    dp = lax.axis_size("dp")
    rows = steps * streams
    per = streams // tensor

    share, subs = weight_first(out_weight, width)
    ids = jnp.concatenate([tokens, frames], axis=0)
    ids = lax.all_to_all(jnp.broadcast_to(ids[None], (dp,) + ids.shape), "dp", 0, 0, tiled=True)
    feats = text_table.shape[0]
    shift = (lax.axis_index("dp") * tensor + lax.axis_index("tensor")) * feats % LANES
    shift = shift[None].astype(jnp.int32)

    attended = attention(query, new_keys, new_values, cache_keys, cache_values, cache_lengths)
    attended = attended.reshape(rows, depth)
    first = gather_first(attended)
    codec = look_up(ids[:, steps:], codec_table, shift, tensor, 1)
    first, codec, share = lax.optimization_barrier((first, codec, share))
    second = gather_second(attended, first)
    weights = weight_second(share)
    emb = look_up(ids[:, :steps], text_table, shift, tensor, 0, codec)
    second, weights, emb = lax.optimization_barrier((second, weights, emb))
    attended, order = gather_third(second)
    weights = weight_third(weights)
    emb = lax.all_to_all(emb, BOTH, 0, 0, tiled=True)
    mine = residual.reshape(steps, tensor, per, width).transpose(1, 0, 2, 3).reshape(rows, width)
    hidden, parts = project(attended, order, weights, subs, mine, bridge_weight)
    parts = lax.all_to_all(parts.reshape(tensor, steps * per, talk), "tensor", 0, 0, tiled=True)
    talker = finish(parts, place(emb, talk), talk_gain.reshape(1, talk))
    hidden = hidden.reshape(tensor, steps, per, width).transpose(1, 0, 2, 3)
    return hidden.reshape(steps, streams, width), talker.reshape(steps, per, talk)


def solution(mesh):
    in_specs = (
        P(None, "dp", "tensor"),
        P(None, "dp", "tensor"),
        P(None, "dp", "tensor"),
        P("dp", None, "tensor"),
        P("dp", None, "tensor"),
        P("dp"),
        P(None, "dp", "tensor"),
        P("tensor", None),
        P("tensor", None),
        P(("dp", "tensor"), None),
        P(("dp", "tensor"), None),
        P(None, "dp"),
        P(None, "dp"),
        P(),
    )
    out_specs = (P(None, "dp", "tensor"), P(None, ("dp", "tensor"), None))
    return jax.shard_map(local, mesh=mesh, in_specs=in_specs, out_specs=out_specs, check_vma=False)
```

time: 1070 us -> 205 us (0.19)
  waiting for transfers between devices: 711 us -> 67.7 us
  local copies, waits for them, and re-layouts: 158 us -> 15.5 us
  Pallas kernels: 0 us -> 68.4 us
  matrix products: 57.5 us -> 0 us
  blocking collectives: 38.8 us -> 0 us
  other arithmetic: 21.9 us -> 0.82 us
  between operations: 15 us -> 0.9 us
    psum x1 -> x0, waiting for transfers between devices: 663 us -> none  [local(): lax.psum(jnp.dot(attended, out_weight, preferred_element_type=jnp.float32...]
    gather x8 -> x0, local copies, waits for them, and re-layouts: 89 us -> none  [the longest x4 58.9 us: local(): text_cols = jnp.take(text_table, token_all[step], axis=1)]
    pallas_call x0 -> x7, Pallas kernels: none -> 68.4 us  [the longest x2 30.6 us: look_up(): pl.pallas_call(functools.partial(look_kernel, group=group), in_specs=[sme...]
    dot_general x23 -> x0, matrix products: 57.5 us -> none  [the longest x4 22.3 us: local(): jnp.dot(hidden, bridge_weight, preferred_element_type=jnp.float32)]
    all_gather x2 -> x0, blocking collectives: 38.8 us -> none  [the longest x1 19.8 us: local(): lax.all_gather(frames, 'dp', axis=1, tiled=True)]
    unnamed x72 -> x28, local copies, waits for them, and re-layouts: 38.4 us -> 9.51 us
    convert_element_type x16 -> x0, local copies, waits for them, and re-layouts: 27.8 us -> none  [the longest x8 14.4 us: local(): text_rows.T.astype(jnp.float32)]
    ppermute x0 -> x13, waiting for transfers between devices: none -> 22.9 us  [the longest x8 22.9 us: send(): return lax.ppermute(x, 'tensor', pairs)]
  transfers between devices with their start and end apart: 13 -> 17, of which waited for: 8 -> 7; matrix products, arithmetic and copies ran while one was open for 17% -> 2% of each run, Pallas kernels for 0% -> 32%
where the time goes in v3:
time: 205 us; the launch traced here: 204 us
  Pallas kernels  68.4 us (33%)
  waiting for transfers between devices  67.7 us (33%)
  starting transfers between devices  50.3 us (25%)
  local copies, waits for them, and re-layouts  15.5 us (8%)
    all_to_all x1, waiting for transfers between devices, local(): lax.all_to_all(parts.reshape(tensor, steps * per, talk), 'tensor', 0, 0,...  44.7 us
    pallas_call x2, Pallas kernels, look_up(): pl.pallas_call(functools.partial(look_kernel, group=group), in_specs=[sme...  30.6 us
    ppermute x8, waiting for transfers between devices, send(): return lax.ppermute(x, 'tensor', pairs)  22.9 us
    pallas_call x1, Pallas kernels, project(): pl.pallas_call(functools.partial(project_kernel, owners=owners), in_specs...  19.3 us
    all_to_all x1, starting transfers between devices, local(): lax.all_to_all(parts.reshape(tensor, steps * per, talk), 'tensor', 0, 0,...  14.1 us
    ppermute x8, starting transfers between devices, send(): return lax.ppermute(x, 'tensor', pairs)  10.5 us
    unnamed x28, local copies, waits for them, and re-layouts  9.51 us
    pallas_call x1, Pallas kernels, attention(): pl.pallas_call(attention_kernel, grid=(blocks,), in_specs=[pl.BlockSpec((...  8.87 us
  transfers between devices with their start and end apart: 17, of which 7 were waited for; matrix products, arithmetic and copies ran while one was open for 2% of the time, Pallas kernels for 32%

profile of v3, /device:TPU:0, one launch (start us, length us, event | category | flops | bytes accessed | tf_op | source)
XLA Modules:
  0.0 203.8 jit_solution(13489498612556968330)
XLA Ops:
  2.0 6.5 %all-to-all-start = ((s32[16,8,128]{2,1,0:T(8,128)}), s32[16,8,128]{2,1,0:T(8,128)S(1)}, u32[]{:S(2)}, u32[]{:S(2)}) async-start(s32[16,8,128]{2,1,0:T(8,128)} %broadcast_in_dim.8), calls=%async_computation | async-start | bytes 131072 | tf_op jit(solution)/shard_map/all_to_all | solution.py:427
  8.6 3.4 %copy-done = bf16[512,8192]{1,0:T(8,128)(2,1)S(1)} copy-done((bf16[512,8192]{1,0:T(8,128)(2,1)S(1)}, bf16[512,8192]{1,0:T(8,128)(2,1)}, u32[]{:S(2)}) %copy-start) | copy-done | bytes 8388632
  12.0 2.4 %share_rows.1 = bf16[8,2,64,1024]{3,2,1,0:T(8,128)(2,1)} custom-call(s32[2]{0:T(128)S(1)} %pad_add_fusion.1.subs_ref, bf16[512,8192]{1,0:T(8,128)(2,1)S(1)} %copy-done), custom_call_target="tpu_custom_call" | custom-call | bytes 4194304 | tf_op jit(solution)/shard_map/share_rows/pallas_call | solution.py:359
  14.7 6.8 %all-to-all-start.1 = ((bf16[8,2,64,1024]{3,2,1,0:T(8,128)(2,1)}), bf16[8,2,64,1024]{3,2,1,0:T(8,128)(2,1)}, u32[]{:S(2)}, u32[]{:S(2)}) async-start(bf16[8,2,64,1024]{3,2,1,0:T(8,128)(2,1)} %share_rows.1), calls=%async_computation.1 | async-start | bytes 4194304 | tf_op jit(solution)/shard_map/all_to_all | solution.py:379
  24.7 8.9 %attention.1 = bf16[8,4,16,512]{3,2,1,0:T(8,128)(2,1)S(1)} custom-call(s32[128,128]{1,0:T(8,128)S(1)} %broadcast_in_dim.6.len_ref, bf16[4,128,512]{2,1,0:T(8,128)(2,1)S(1)} %copy-done.5, bf16[128,64,128]{2,1,0:T(8,128)(2,1)S(1)} %copy-done.3, bf16[128,64,128]{2,1,0:T(8,128)(2,1)S(1)} %copy-done.4, bf16[4,128,128]{2,1,0:T(8,128)(2,1)S(1)} %copy-done.10, ...), custom_call_target="tpu_custom_call" | custom-call | flops 8000000000 | bytes 6291456 | tf_op jit(solution)/shard_map/attention/pallas_call | solution.py:75
  33.6 3.6 %collective-permute-start.2 = (bf16[512,512]{1,0:T(8,128)(2,1)S(1)}, bf16[512,512]{1,0:T(8,128)(2,1)}, u32[]{:S(2)}, u32[]{:S(2)}) collective-permute-start(bf16[512,512]{1,0:T(8,128)(2,1)S(1)} %bitcast.33), channel_id=1, source_target_pairs={{0,1},{1,0},{2,3},{3,2},{4,5},{5,4},{6,7},{7,6},{8,9},{9,8},{10,11... | collective-permute-start | bytes 1572872 | tf_op jit(solution)/shard_map/ppermute | solution.py:314
  37.2 2.7 %collective-permute-start.1 = (bf16[512,512]{1,0:T(8,128)(2,1)S(1)}, bf16[512,512]{1,0:T(8,128)(2,1)S(1)}, u32[]{:S(2)}, u32[]{:S(2)}) collective-permute-start(bf16[512,512]{1,0:T(8,128)(2,1)S(1)} %bitcast.34), channel_id=1, source_target_pairs={{0,6},{1,7},{2,0},{3,1},{4,2},{5,3},{6,4},{7,5},{8,14},{9,15},{10,... | collective-permute-start | bytes 1572872 | tf_op jit(solution)/shard_map/ppermute | solution.py:314
  39.9 12.0 %look_up.2.refs_0_ = bf16[128,32,128]{2,1,0:T(8,128)(2,1)S(1)} custom-call(s32[1]{0:T(128)} %bitcast.17.shift_ref, s32[8192]{0:T(1024)S(1)} %bitcast.32, bf16[28,8448]{1,0:T(8,128)(2,1)S(1)} %copy-done.2), custom_call_target="tpu_custom_call" | custom-call | bytes 23068672 | tf_op jit(solution)/shard_map/look_up/pallas_call | solution.py:164
  52.0 7.9 %collective-permute-done.2.refs_1_ = bf16[512,512]{1,0:T(8,128)(2,1)} collective-permute-done((bf16[512,512]{1,0:T(8,128)(2,1)S(1)}, bf16[512,512]{1,0:T(8,128)(2,1)}, u32[]{:S(2)}, u32[]{:S(2)}) %collective-permute-start.2) | collective-permute-done | bytes 524320 | tf_op jit(solution)/shard_map/ppermute | solution.py:314
  59.8 2.0 collective-permute-done.1.refs_4_
  61.9 2.5 %collective-permute-done.refs_2_ = bf16[512,512]{1,0:T(8,128)(2,1)S(1)} collective-permute-done((bf16[512,512]{1,0:T(8,128)(2,1)S(1)}, bf16[512,512]{1,0:T(8,128)(2,1)S(1)}, u32[]{:S(2)}, u32[]{:S(2)}) %collective-permute-start) | collective-permute-done | bytes 524320 | tf_op jit(solution)/shard_map/ppermute | solution.py:314
  64.3 1.7 fusion
  66.1 2.9 %collective-permute-start.8 = (bf16[8,1,64,1024]{3,2,1,0:T(8,128)(2,1)S(1)}, bf16[8,1,64,1024]{3,2,1,0:T(8,128)(2,1)}, u32[]{:S(2)}, u32[]{:S(2)}) collective-permute-start(bf16[8,1,64,1024]{3,2,1,0:T(8,128)(2,1)S(1)} %get-tuple-element.38), channel_id=1, source_target_pairs={{0,48},{8,56},{16,32},{24,40},{32,16},{40,24},{48,0},{56,8},{64,11... | collective-permute-start | bytes 3145736 | tf_op jit(solution)/shard_map/ppermute | solution.py:392
  70.2 1.9 collective-permute-start.3
  72.2 6.5 %collective-permute-done.6 = bf16[256,512]{1,0:T(8,128)(2,1)S(1)} collective-permute-done((bf16[256,512]{1,0:T(8,128)(2,1)S(1)}, bf16[256,512]{1,0:T(8,128)(2,1)S(1)}, u32[]{:S(2)}, u32[]{:S(2)}) %collective-permute-start.6) | collective-permute-done | bytes 262176 | tf_op jit(solution)/shard_map/ppermute | solution.py:314
  78.6 18.5 %look_up.3 = bf16[128,32,128]{2,1,0:T(8,128)(2,1)} custom-call(s32[1]{0:T(128)} %bitcast.17.shift_ref, s32[8192]{0:T(1024)S(1)} %bitcast.31, bf16[28,76032]{1,0:T(8,128)(2,1)} %table_ref.3, bf16[128,32,128]{2,1,0:T(8,128)(2,1)S(1)} %look_up.2.refs_0_), custom_call_target="tpu_custom_call" | custom-call | bytes 47185920 | tf_op jit(solution)/shard_map/look_up/pallas_call | solution.py:164
  100.1 2.3 %copy.16 = bf16[4,8,16,1024]{3,2,0,1:T(8,128)(2,1)} copy(bf16[4,8,16,1024]{3,2,1,0:T(8,128)(2,1)} %bitcast.38) | data formatting | bytes 2097152 | tf_op jit(solution)/shard_map/reshape | solution.py:444
  102.5 8.7 %all-to-all-start.3 = ((bf16[128,32,128]{2,1,0:T(8,128)(2,1)}), bf16[128,32,128]{2,1,0:T(8,128)(2,1)}, u32[]{:S(2)}, u32[]{:S(2)}) async-start(bf16[128,32,128]{2,1,0:T(8,128)(2,1)} %look_up.3), calls=%async_computation.3 | async-start | bytes 2097152 | tf_op jit(solution)/shard_map/all_to_all | solution.py:443
  111.2 4.0 %collective-permute-done.9.refs_7_ = bf16[512,512]{1,0:T(8,128)(2,1)} collective-permute-done((bf16[512,512]{1,0:T(8,128)(2,1)S(1)}, bf16[512,512]{1,0:T(8,128)(2,1)}, u32[]{:S(2)}, u32[]{:S(2)}) %collective-permute-start.9) | collective-permute-done | bytes 524320 | tf_op jit(solution)/shard_map/ppermute | solution.py:314
  117.4 19.3 %project.1 = (bf16[512,1024]{1,0:T(8,128)(2,1)S(1)}, bf16[512,3584]{1,0:T(8,128)(2,1)}) custom-call(s32[8]{0:T(128)S(1)} %stack.67.order_ref, s32[8]{0:T(128)S(1)} %stack.76.subs_ref, bf16[512,512]{1,0:T(8,128)(2,1)S(1)} %bitcast.36, bf16[512,512]{1,0:T(8,128)(2,1)} %collective-permute-done.2.refs_1_, bf16[512,512]{1,0:T(8,128)(2,1)S(1)} %collective-permute-done.refs_2_, ...), custom_call_target="tpu_custom_call" | custom-call | flops 12000000000 | bytes 25165824 | tf_op jit(solution)/shard_map/project/pallas_call | solution.py:221
  136.7 14.1 %all-to-all-start.2 = ((bf16[8,64,3584]{2,1,0:T(8,128)(2,1)}), bf16[8,64,3584]{2,1,0:T(8,128)(2,1)}, u32[]{:S(2)}, u32[]{:S(2)}) async-start(bf16[8,64,3584]{2,1,0:T(8,128)(2,1)} %bitcast.37), calls=%async_computation.2 | async-start | bytes 7340032 | tf_op jit(solution)/shard_map/all_to_all | solution.py:446
  150.8 3.8 %place.1.emb_ref = f32[64,3584]{1,0:T(8,128)} custom-call(bf16[128,32,128]{2,1,0:T(8,128)(2,1)} %all-to-all-done.3.emb_ref), custom_call_target="tpu_custom_call" | custom-call | bytes 8388608 | tf_op jit(solution)/shard_map/place/pallas_call | solution.py:261
  155.7 44.7 %all-to-all-done.2.part_ref = bf16[8,64,3584]{2,1,0:T(8,128)(2,1)} async-done(((bf16[8,64,3584]{2,1,0:T(8,128)(2,1)}), bf16[8,64,3584]{2,1,0:T(8,128)(2,1)}, u32[]{:S(2)}, u32[]{:S(2)}) %all-to-all-start.2) | async-done | bytes 3670048 | tf_op jit(solution)/shard_map/all_to_all | solution.py:446
  200.3 3.5 %finish.1 = bf16[64,3584]{1,0:T(8,128)(2,1)} custom-call(bf16[8,64,3584]{2,1,0:T(8,128)(2,1)} %all-to-all-done.2.part_ref, f32[64,3584]{1,0:T(8,128)S(1)} %copy-done.1, bf16[1,3584]{1,0:T(2,128)(2,1)S(1)} %reshape.44.gain_ref), custom_call_target="tpu_custom_call" | custom-call | bytes 8388608 | tf_op jit(solution)/shard_map/finish/pallas_call | solution.py:294
  (59 shorter events, 12.3 us)
Async XLA Ops:
  2.0 12.7 %all-to-all-start = ((s32[16,8,128]{2,1,0:T(8,128)}), s32[16,8,128]{2,1,0:T(8,128)S(1)}, u32[]{:S(2)}, u32[]{:S(2)}) async-start(s32[16,8,128]{2,1,0:T(8,128)} %broadcast_in_dim.8), calls=%async_computation | async-start | bytes 131072 | tf_op jit(solution)/shard_map/all_to_all | solution.py:427
  14.4 7.0 %copy-start.13 = (s32[128]{0:T(128)S(1)}, s32[128]{0:T(128)}, u32[]{:S(2)}) copy-start(s32[128]{0:T(128)} %param.19) | copy-start | bytes 1540
  14.4 7.1 %copy-start.5 = (bf16[4,128,512]{2,1,0:T(8,128)(2,1)S(1)}, bf16[4,128,512]{2,1,0:T(8,128)(2,1)}, u32[]{:S(2)}) copy-start(bf16[4,128,512]{2,1,0:T(8,128)(2,1)} %q_ref.1) | copy-start | bytes 1572868
  14.4 7.1 %copy-start.10 = (bf16[4,128,128]{2,1,0:T(8,128)(2,1)S(1)}, bf16[4,128,128]{2,1,0:T(8,128)(2,1)}, u32[]{:S(2)}) copy-start(bf16[4,128,128]{2,1,0:T(8,128)(2,1)} %nk_ref.1) | copy-start | bytes 393220
  14.5 7.1 %copy-start.11 = (bf16[4,128,128]{2,1,0:T(8,128)(2,1)S(1)}, bf16[4,128,128]{2,1,0:T(8,128)(2,1)}, u32[]{:S(2)}) copy-start(bf16[4,128,128]{2,1,0:T(8,128)(2,1)} %nv_ref.1) | copy-start | bytes 393220
  14.7 49.7 %all-to-all-start.1 = ((bf16[8,2,64,1024]{3,2,1,0:T(8,128)(2,1)}), bf16[8,2,64,1024]{3,2,1,0:T(8,128)(2,1)}, u32[]{:S(2)}, u32[]{:S(2)}) async-start(bf16[8,2,64,1024]{3,2,1,0:T(8,128)(2,1)} %share_rows.1), calls=%async_computation.1 | async-start | bytes 4194304 | tf_op jit(solution)/shard_map/all_to_all | solution.py:379
  24.7 15.2 %copy-start.2 = (bf16[28,8448]{1,0:T(8,128)(2,1)S(1)}, bf16[28,8448]{1,0:T(8,128)(2,1)}, u32[]{:S(2)}) copy-start(bf16[28,8448]{1,0:T(8,128)(2,1)} %table_ref.2) | copy-start | bytes 1419268
  33.6 26.2 %collective-permute-start.2 = (bf16[512,512]{1,0:T(8,128)(2,1)S(1)}, bf16[512,512]{1,0:T(8,128)(2,1)}, u32[]{:S(2)}, u32[]{:S(2)}) collective-permute-start(bf16[512,512]{1,0:T(8,128)(2,1)S(1)} %bitcast.33), channel_id=1, source_target_pairs={{0,1},{1,0},{2,3},{3,2},{4,5},{5,4},{6,7},{7,6},{8,9},{9,8},{10,11... | collective-permute-start | bytes 1572872 | tf_op jit(solution)/shard_map/ppermute | solution.py:314
  37.2 24.7 %collective-permute-start.1 = (bf16[512,512]{1,0:T(8,128)(2,1)S(1)}, bf16[512,512]{1,0:T(8,128)(2,1)S(1)}, u32[]{:S(2)}, u32[]{:S(2)}) collective-permute-start(bf16[512,512]{1,0:T(8,128)(2,1)S(1)} %bitcast.34), channel_id=1, source_target_pairs={{0,6},{1,7},{2,0},{3,1},{4,2},{5,3},{6,4},{7,5},{8,14},{9,15},{10,... | collective-permute-start | bytes 1572872 | tf_op jit(solution)/shard_map/ppermute | solution.py:314
  39.9 24.5 %collective-permute-start = (bf16[512,512]{1,0:T(8,128)(2,1)S(1)}, bf16[512,512]{1,0:T(8,128)(2,1)S(1)}, u32[]{:S(2)}, u32[]{:S(2)}) collective-permute-start(bf16[512,512]{1,0:T(8,128)(2,1)S(1)} %bitcast.35), channel_id=1, source_target_pairs={{0,2},{1,3},{2,4},{3,5},{4,6},{5,7},{6,0},{7,1},{8,10},{9,11},{10,... | collective-permute-start | bytes 1572872 | tf_op jit(solution)/shard_map/ppermute | solution.py:314
  66.1 32.0 %collective-permute-start.8 = (bf16[8,1,64,1024]{3,2,1,0:T(8,128)(2,1)S(1)}, bf16[8,1,64,1024]{3,2,1,0:T(8,128)(2,1)}, u32[]{:S(2)}, u32[]{:S(2)}) collective-permute-start(bf16[8,1,64,1024]{3,2,1,0:T(8,128)(2,1)S(1)} %get-tuple-element.38), channel_id=1, source_target_pairs={{0,48},{8,56},{16,32},{24,40},{32,16},{40,24},{48,0},{56,8},{64,11... | collective-permute-start | bytes 3145736 | tf_op jit(solution)/shard_map/ppermute | solution.py:392
  69.0 29.0 %collective-permute-start.7 = (bf16[8,1,64,1024]{3,2,1,0:T(8,128)(2,1)S(1)}, bf16[8,1,64,1024]{3,2,1,0:T(8,128)(2,1)}, u32[]{:S(2)}, u32[]{:S(2)}) collective-permute-start(bf16[8,1,64,1024]{3,2,1,0:T(8,128)(2,1)S(1)} %get-tuple-element.39), channel_id=1, source_target_pairs={{0,16},{8,24},{16,0},{24,8},{32,48},{40,56},{48,32},{56,40},{64,80... | collective-permute-start | bytes 3145736 | tf_op jit(solution)/shard_map/ppermute | solution.py:391
  69.3 9.3 %collective-permute-start.6 = (bf16[256,512]{1,0:T(8,128)(2,1)S(1)}, bf16[256,512]{1,0:T(8,128)(2,1)S(1)}, u32[]{:S(2)}, u32[]{:S(2)}) collective-permute-start(bf16[256,512]{1,0:T(8,128)(2,1)S(1)} %slice.20), channel_id=1, source_target_pairs={{0,6},{1,7},{2,0},{3,1},{4,2},{5,3},{6,4},{7,5},{8,14},{9,15},{10,... | collective-permute-start | bytes 786440 | tf_op jit(solution)/shard_map/ppermute | solution.py:314
  70.1 27.1 %collective-permute-start.4 = (bf16[512,512]{1,0:T(8,128)(2,1)}, bf16[512,512]{1,0:T(8,128)(2,1)S(1)}, u32[]{:S(2)}, u32[]{:S(2)}) collective-permute-start(bf16[512,512]{1,0:T(8,128)(2,1)} %collective-permute-done.2.refs_1_), channel_id=1, source_target_pairs={{0,6},{1,7},{2,0},{3,1},{4,2},{5,3},{6,4},{7,5},{8,14},{9,15},{10,... | collective-permute-start | bytes 1572872 | tf_op jit(solution)/shard_map/ppermute | solution.py:314
  70.2 27.0 %collective-permute-start.3 = (bf16[512,512]{1,0:T(8,128)(2,1)}, bf16[512,512]{1,0:T(8,128)(2,1)S(1)}, u32[]{:S(2)}, u32[]{:S(2)}) collective-permute-start(bf16[512,512]{1,0:T(8,128)(2,1)} %collective-permute-done.2.refs_1_), channel_id=1, source_target_pairs={{0,2},{1,3},{2,4},{3,5},{4,6},{5,7},{6,0},{7,1},{8,10},{9,11},{10,... | collective-permute-start | bytes 1572872 | tf_op jit(solution)/shard_map/ppermute | solution.py:314
  78.6 18.5 %collective-permute-start.5 = (bf16[256,512]{1,0:T(8,128)(2,1)S(1)}, bf16[256,512]{1,0:T(8,128)(2,1)S(1)}, u32[]{:S(2)}, u32[]{:S(2)}) collective-permute-start(bf16[256,512]{1,0:T(8,128)(2,1)S(1)} %slice.19), channel_id=1, source_target_pairs={{0,2},{1,3},{2,4},{3,5},{4,6},{5,7},{6,0},{7,1},{8,10},{9,11},{10,... | collective-permute-start | bytes 786440 | tf_op jit(solution)/shard_map/ppermute | solution.py:314
  98.1 17.2 %collective-permute-start.10 = (bf16[8,2,64,1024]{3,2,1,0:T(8,128)(2,1)}, bf16[8,2,64,1024]{3,2,1,0:T(8,128)(2,1)}, u32[]{:S(2)}, u32[]{:S(2)}) collective-permute-start(bf16[8,2,64,1024]{3,2,1,0:T(8,128)(2,1)} %all-to-all-done.1.refs_8_), channel_id=1, source_target_pairs={{0,8},{8,0},{16,24},{24,16},{32,40},{40,32},{48,56},{56,48},{64,72... | collective-permute-start | bytes 6291464 | tf_op jit(solution)/shard_map/ppermute | solution.py:398
  98.1 17.2 %collective-permute-start.11 = (bf16[8,1,64,1024]{3,2,1,0:T(8,128)(2,1)}, bf16[8,1,64,1024]{3,2,1,0:T(8,128)(2,1)}, u32[]{:S(2)}, u32[]{:S(2)}) collective-permute-start(bf16[8,1,64,1024]{3,2,1,0:T(8,128)(2,1)} %collective-permute-done.7.refs_9_), channel_id=1, source_target_pairs={{0,8},{8,0},{16,24},{24,16},{32,40},{40,32},{48,56},{56,48},{64,72... | collective-permute-start | bytes 3145736 | tf_op jit(solution)/shard_map/ppermute | solution.py:398
  98.6 16.7 %collective-permute-start.12 = (bf16[8,1,64,1024]{3,2,1,0:T(8,128)(2,1)}, bf16[8,1,64,1024]{3,2,1,0:T(8,128)(2,1)}, u32[]{:S(2)}, u32[]{:S(2)}) collective-permute-start(bf16[8,1,64,1024]{3,2,1,0:T(8,128)(2,1)} %collective-permute-done.8.refs_10_), channel_id=1, source_target_pairs={{0,8},{8,0},{16,24},{24,16},{32,40},{40,32},{48,56},{56,48},{64,72... | collective-permute-start | bytes 3145736 | tf_op jit(solution)/shard_map/ppermute | solution.py:398
  98.7 16.6 %collective-permute-start.9 = (bf16[512,512]{1,0:T(8,128)(2,1)S(1)}, bf16[512,512]{1,0:T(8,128)(2,1)}, u32[]{:S(2)}, u32[]{:S(2)}) collective-permute-start(bf16[512,512]{1,0:T(8,128)(2,1)S(1)} %pad_maximum_fusion.refs_6_), channel_id=1, source_target_pairs={{0,1},{1,0},{2,3},{3,2},{4,5},{5,4},{6,7},{7,6},{8,9},{9,8},{10,11... | collective-permute-start | bytes 1572872 | tf_op jit(solution)/shard_map/ppermute | solution.py:314
  102.5 34.2 %all-to-all-start.3 = ((bf16[128,32,128]{2,1,0:T(8,128)(2,1)}), bf16[128,32,128]{2,1,0:T(8,128)(2,1)}, u32[]{:S(2)}, u32[]{:S(2)}) async-start(bf16[128,32,128]{2,1,0:T(8,128)(2,1)} %look_up.3), calls=%async_computation.3 | async-start | bytes 2097152 | tf_op jit(solution)/shard_map/all_to_all | solution.py:443
  136.7 14.1 %copy-start.12 = (bf16[3584]{0:T(1024)(128)(2,1)S(1)}, bf16[3584]{0:T(1024)(128)(2,1)}, u32[]{:S(2)}) copy-start(bf16[3584]{0:T(1024)(128)(2,1)} %param.27) | copy-start | bytes 21508
  136.7 63.6 %all-to-all-start.2 = ((bf16[8,64,3584]{2,1,0:T(8,128)(2,1)}), bf16[8,64,3584]{2,1,0:T(8,128)(2,1)}, u32[]{:S(2)}, u32[]{:S(2)}) async-start(bf16[8,64,3584]{2,1,0:T(8,128)(2,1)} %bitcast.37), calls=%async_computation.2 | async-start | bytes 7340032 | tf_op jit(solution)/shard_map/all_to_all | solution.py:446
  154.6 45.7 %copy-start.1 = (f32[64,3584]{1,0:T(8,128)S(1)}, f32[64,3584]{1,0:T(8,128)}, u32[]{:S(2)}) copy-start(f32[64,3584]{1,0:T(8,128)} %place.1.emb_ref) | copy-start | bytes 2752516
  (7 other events, 14.8 us)

commit v4 on v3

--- a/solution.py
+++ b/solution.py
@@ -85,13 +85,13 @@
         ],
         out_specs=pl.BlockSpec((1, steps, SB, width), lambda i: (i, 0, 0, 0)),
         out_shape=jax.ShapeDtypeStruct((blocks, steps, SB, width), BF16),
-        compiler_params=pltpu.CompilerParams(vmem_limit_bytes=32 * MIB),
+        compiler_params=pltpu.CompilerParams(vmem_limit_bytes=58 * MIB),
         cost_estimate=pl.CostEstimate(flops=8 * 10**9, bytes_accessed=6 * MIB, transcendentals=0),
         name="attention",
     )(lengths, query, cache_keys, cache_values, new_keys, new_values)
 
 
-def look_kernel(shift_ref, id_ref, table_ref, *refs, group):
+def look_kernel(shift_ref, spot_ref, id_ref, table_ref, *refs, group):
     other_ref = refs[0] if len(refs) == 4 else None
     out_ref, turned, found = refs[-3:]
     feats, entries = table_ref.shape
@@ -134,11 +134,11 @@
     def look(i, _):
         def find(j, _):
             o = i * batch + j
-            base = o // (LANES // per) * (STEPS * LANES) + o % (LANES // per) * per
+            base = spot_ref[o // (LANES // per)] + o % (LANES // per) * per
             to = pl.multiple_of(j * rows, rows)
             for t in range(STEPS):
                 for s in range(per):
-                    at = id_ref[base + (t * LANES + s)]
+                    at = id_ref[base + ((group * STEPS + t) * LANES + s)]
                     found[pl.ds(to + (t * per + s), 1), :] = turned[pl.ds(at, 1), :]
             return 0
 
@@ -156,14 +156,14 @@
     lax.fori_loop(0, owners // batch, look, 0)
 
 
-def look_up(ids, table, shift, owners, group, *other):
+def look_up(ids, group, spots, table, shift, owners, *other):
     groups, _, streams = ids.shape
     rows = streams * STEPS // owners
     vmem = pl.BlockSpec(memory_space=pltpu.VMEM)
     smem = pl.BlockSpec(memory_space=pltpu.SMEM)
     return pl.pallas_call(
         functools.partial(look_kernel, group=group),
-        in_specs=[smem, smem, vmem] + [vmem] * len(other),
+        in_specs=[smem, smem, smem, vmem] + [vmem] * len(other),
         out_specs=vmem,
         out_shape=jax.ShapeDtypeStruct((groups * owners, rows // 2, LANES), BF16),
         scratch_shapes=[
@@ -175,65 +175,78 @@
             flops=0, bytes_accessed=(20 + table.shape[1] // 3000) * MIB, transcendentals=0
         ),
         name="look_up",
-    )(shift, ids.reshape(-1), table, *other)
-
-
-def project_kernel(order_ref, subs_ref, *refs, owners):
+    )(shift, spots, ids.reshape(-1), table, *other)
+
+
+def collect_rows_kernel(order_ref, *refs, owners):
     a_refs = refs[:owners]
-    *w_refs, res_ref, bridge_ref, hidden_ref, part_ref, a_all, w_all = refs[owners:]
+    res_ref, a_all, res_all, done, a_sem, res_sem = refs[owners:]
     depth = a_refs[0].shape[1]
-    cols = w_all.shape[2]
+    copies = []
+    for t in range(STEPS):
+        copies.append(pltpu.make_async_copy(res_ref.at[t], res_all.at[:, t], res_sem.at[t]))
     for k in range(owners):
         at = pl.multiple_of(order_ref[k] * depth, depth)
-        a_all[:, pl.ds(at, depth)] = a_refs[k][...]
-
-    def columns(n, _):
-        here = pl.ds(pl.multiple_of(n * cols, cols), cols)
-        sub = 0
-        for w_ref in w_refs:
-            for k in range(w_ref.shape[1]):
-                size = w_ref.shape[2]
-                at = pl.multiple_of(subs_ref[sub] * size, size)
-                w_all[:, pl.ds(at, size), :] = w_ref[:, k, :, here]
-                sub += 1
-        w = w_all[...].reshape(owners * depth, cols)
-        prod = jnp.dot(a_all[...], w, preferred_element_type=F32)
-        hidden_ref[:, here] = (res_ref[:, here].astype(F32) + prod).astype(BF16)
-        return 0
-
-    lax.fori_loop(0, hidden_ref.shape[1] // cols, columns, 0)
-    wide = 512
-
-    def bridge(n, _):
-        here = pl.ds(pl.multiple_of(n * wide, wide), wide)
-        part = jnp.dot(hidden_ref[...], bridge_ref[:, here], preferred_element_type=F32)
-        part_ref[:, here] = part.astype(BF16)
-        return 0
-
-    lax.fori_loop(0, part_ref.shape[1] // wide, bridge, 0)
-
-
-def project(attended, order, weights, subs, residual, bridge):
+        copies.append(pltpu.make_async_copy(a_refs[k], a_all.at[:, pl.ds(at, depth)], a_sem.at[k]))
+    for copy in copies:
+        copy.start()
+    for copy in copies:
+        copy.wait()
+    done[...] = jnp.zeros_like(done)
+
+
+def collect_rows(attended, order, residual):
     owners = len(attended)
     rows, depth = attended[0].shape
+    width = residual.shape[-1]
     vmem = pl.BlockSpec(memory_space=pltpu.VMEM)
-    smem = pl.BlockSpec(memory_space=pltpu.SMEM)
-    return pl.pallas_call(
-        functools.partial(project_kernel, owners=owners),
-        in_specs=[smem, smem] + [vmem] * (owners + len(weights) + 2),
-        out_specs=[vmem, vmem],
+    return pl.pallas_call(
+        functools.partial(collect_rows_kernel, owners=owners),
+        in_specs=[pl.BlockSpec(memory_space=pltpu.SMEM)]
+        + [pl.BlockSpec(memory_space=pl.ANY)] * (owners + 1),
+        out_specs=[vmem] * 3,
         out_shape=[
-            jax.ShapeDtypeStruct(residual.shape, BF16),
-            jax.ShapeDtypeStruct((rows, bridge.shape[1]), BF16),
+            jax.ShapeDtypeStruct((rows, owners * depth), BF16),
+            jax.ShapeDtypeStruct((owners, STEPS, rows // STEPS // owners, width), BF16),
+            jax.ShapeDtypeStruct((8, LANES), F32),
         ],
-        scratch_shapes=[
-            pltpu.VMEM((rows, owners * depth), BF16),
-            pltpu.VMEM((owners, depth, 256), BF16),
-        ],
-        compiler_params=pltpu.CompilerParams(vmem_limit_bytes=48 * MIB),
-        cost_estimate=pl.CostEstimate(flops=12 * 10**9, bytes_accessed=24 * MIB, transcendentals=0),
-        name="project",
-    )(order, subs, *attended, *weights, residual, bridge)
+        scratch_shapes=[pltpu.SemaphoreType.DMA((n,)) for n in (owners, STEPS)],
+        compiler_params=pltpu.CompilerParams(vmem_limit_bytes=12 * MIB),
+        cost_estimate=pl.CostEstimate(flops=0, bytes_accessed=8 * MIB, transcendentals=0),
+        name="collect_rows",
+    )(order, *attended, residual)
+
+
+def collect_weight_kernel(subs_ref, done_ref, *refs):
+    del done_ref
+    *w_refs, w_all, sems = refs
+    copies = []
+    for w_ref in w_refs:
+        for k in range(w_ref.shape[1]):
+            sub = len(copies)
+            copies.append(
+                pltpu.make_async_copy(w_ref.at[:, k], w_all.at[:, subs_ref[sub]], sems.at[sub])
+            )
+    for copy in copies:
+        copy.start()
+    for copy in copies:
+        copy.wait()
+
+
+def collect_weight(weights, subs, done):
+    owners, _, size, width = weights[0].shape
+    parts = subs.shape[0]
+    return pl.pallas_call(
+        collect_weight_kernel,
+        in_specs=[pl.BlockSpec(memory_space=pltpu.SMEM)]
+        + [pl.BlockSpec(memory_space=pl.ANY)] * (len(weights) + 1),
+        out_specs=pl.BlockSpec(memory_space=pltpu.VMEM),
+        out_shape=jax.ShapeDtypeStruct((owners, parts, size, width), BF16),
+        scratch_shapes=[pltpu.SemaphoreType.DMA((parts,))],
+        compiler_params=pltpu.CompilerParams(vmem_limit_bytes=12 * MIB),
+        cost_estimate=pl.CostEstimate(flops=0, bytes_accessed=10 * MIB, transcendentals=0),
+        name="collect_weight",
+    )(subs, done, *weights)
 
 
 def place_kernel(emb_ref, out_ref, *, feats):
@@ -303,11 +316,27 @@
     )(parts, emb, gain)
 
 
+def gather_ids(ids, share, later):
+    count = lax.axis_size("dp")
+    size = ids.size
+    get = lambda x, peer: lax.ppermute(x, "dp", [(peer(i), i) for i in range(count)])
+    turn = lambda by: lambda i: i // 8 * 8 + (i + 2 * by) % 8
+    across_y, share = lax.optimization_barrier((get(ids, lambda i: i ^ 8), share))
+    ids = jnp.stack([ids, across_y])
+    ids = jnp.concatenate([ids, get(ids, lambda i: i ^ 1)])
+    ids, later = lax.optimization_barrier((ids, later))
+    ids = jnp.concatenate([ids] + [get(ids, turn(by)) for by in (1, 2, 3)])
+    me = lax.axis_index("dp")
+    peer = jnp.arange(count, dtype=jnp.int32)
+    across = (peer // 2 - me // 2) % 4
+    other = (peer % 2 != me % 2) * 2 + (peer // 8 != me // 8)
+    return share, later, ids, ((across * 4 + other) * size).astype(jnp.int32)
+
+
 def tensor_pairs():
     size = lax.axis_size("tensor")
-    up = [(i, (i + 2) % size) for i in range(size)]
-    down = [(i, (i - 2) % size) for i in range(size)]
-    return up, down, [(i, i ^ 1) for i in range(size)]
+    along = lambda by: [(i, (i + 2 * by) % size) for i in range(size)]
+    return along(1), along(-1), along(2), [(i, i ^ 1) for i in range(size)]
 
 
 def send(x, pairs):
@@ -315,26 +344,22 @@
 
 
 def gather_first(own):
-    up, down, across = tensor_pairs()
-    return send(own, up), send(own, down), send(own, across)
-
-
-def gather_second(own, first):
-    up, down, _ = tensor_pairs()
-    from_up, from_down, beside = first
-    half = own.shape[0] // 2
-    far = jnp.concatenate([send(from_up[:half], up), send(from_down[half:], down)], axis=0)
-    return [own, beside, from_up, send(beside, up), from_down, send(beside, down), far]
-
-
-def gather_third(second):
+    return [send(own, pairs) for pairs in tensor_pairs()]
+
+
+def gather_second(first):
+    up, down, _, across = tensor_pairs()
+    _, _, far, beside = first
+    return [send(beside, up), send(beside, down), send(far, across)]
+
+
+def peers_order():
     size = lax.axis_size("tensor")
-    arrays = second + [send(second[-1], tensor_pairs()[2])]
     me = lax.axis_index("tensor")
     x, y = me // 2, me % 2
     spot = lambda k, other: (x + k) % (size // 2) * 2 + (y + other) % 2
-    order = [spot(k, other) for k in (0, 3, 1, 2) for other in (0, 1)]
-    return arrays, jnp.stack(order).astype(jnp.int32)
+    order = [(0, 0), (3, 0), (1, 0), (2, 0), (0, 1), (3, 1), (1, 1), (2, 1)]
+    return jnp.stack([spot(*o) for o in order]).astype(jnp.int32)
 
 
 def share_kernel(subs_ref, w_ref, out_ref, sems):
@@ -358,11 +383,11 @@
     owners = out_weight.shape[1] // width
     return pl.pallas_call(
         share_kernel,
-        in_specs=[pl.BlockSpec(memory_space=pltpu.SMEM), pl.BlockSpec(memory_space=pl.ANY)],
+        in_specs=[pl.BlockSpec(memory_space=pltpu.SMEM), pl.BlockSpec(memory_space=pltpu.HBM)],
         out_specs=pl.BlockSpec(memory_space=pltpu.VMEM),
         out_shape=jax.ShapeDtypeStruct((owners, subs.shape[0], size, width), BF16),
         scratch_shapes=[pltpu.SemaphoreType.DMA((owners, subs.shape[0]))],
-        compiler_params=pltpu.CompilerParams(vmem_limit_bytes=16 * MIB),
+        compiler_params=pltpu.CompilerParams(vmem_limit_bytes=58 * MIB),
         cost_estimate=pl.CostEstimate(flops=0, bytes_accessed=4 * MIB, transcendentals=0),
         name="share_rows",
     )(subs, out_weight)
@@ -376,7 +401,7 @@
     core, odd = me % 2, me // 2 % 2
     sub_a, sub_b = core * 4 + odd, core * 4 + 3 - odd
     pair = jnp.stack([sub_a, sub_b]).astype(jnp.int32)
-    share = lax.all_to_all(share_rows(out_weight, pair, size, width), "tensor", 0, 0, tiled=True)
+    share = share_rows(out_weight, pair, size, width)
 
     own = [sub_a, sub_b, core * 4 + 1 - odd, core * 4 + 2 + odd]
     return share, jnp.stack(own + [(k + 4) % 8 for k in own]).astype(jnp.int32)
@@ -422,27 +447,30 @@
     rows = steps * streams
     per = streams // tensor
 
-    share, subs = weight_first(out_weight, width)
-    ids = jnp.concatenate([tokens, frames], axis=0)
-    ids = lax.all_to_all(jnp.broadcast_to(ids[None], (dp,) + ids.shape), "dp", 0, 0, tiled=True)
     feats = text_table.shape[0]
     shift = (lax.axis_index("dp") * tensor + lax.axis_index("tensor")) * feats % LANES
     shift = shift[None].astype(jnp.int32)
+    share, subs = weight_first(out_weight, width)
+    ids = jnp.concatenate([tokens, frames], axis=0)
+    share, query, ids, spots = gather_ids(ids, share, query)
+    share = lax.all_to_all(share, "tensor", 0, 0, tiled=True)
 
     attended = attention(query, new_keys, new_values, cache_keys, cache_values, cache_lengths)
-    attended = attended.reshape(rows, depth)
+    attended, ids = lax.optimization_barrier((attended.reshape(rows, depth), ids))
     first = gather_first(attended)
-    codec = look_up(ids[:, steps:], codec_table, shift, tensor, 1)
-    first, codec, share = lax.optimization_barrier((first, codec, share))
-    second = gather_second(attended, first)
+    text = look_up(ids, 0, spots, text_table, shift, tensor)
+    first, text, share = lax.optimization_barrier((first, text, share))
     weights = weight_second(share)
-    emb = look_up(ids[:, :steps], text_table, shift, tensor, 0, codec)
-    second, weights, emb = lax.optimization_barrier((second, weights, emb))
-    attended, order = gather_third(second)
-    weights = weight_third(weights)
+    attended = [attended] + first + gather_second(first)
+    emb = look_up(ids, 1, spots, codec_table, shift, tensor, text)
+    residual = residual.reshape(steps, tensor, per, width)
+    attended, mine, done = collect_rows(attended, peers_order(), residual)
+    weights, done, emb = lax.optimization_barrier((weights, done, emb))
     emb = lax.all_to_all(emb, BOTH, 0, 0, tiled=True)
-    mine = residual.reshape(steps, tensor, per, width).transpose(1, 0, 2, 3).reshape(rows, width)
-    hidden, parts = project(attended, order, weights, subs, mine, bridge_weight)
+    weight = collect_weight(weight_third(weights), subs, done)
+    hidden = jnp.dot(attended, weight.reshape(tensor * depth, width), preferred_element_type=F32)
+    hidden = (mine.reshape(rows, width).astype(F32) + hidden).astype(BF16)
+    parts = jnp.dot(hidden, bridge_weight, preferred_element_type=F32).astype(BF16)
     parts = lax.all_to_all(parts.reshape(tensor, steps * per, talk), "tensor", 0, 0, tiled=True)
     talker = finish(parts, place(emb, talk), talk_gain.reshape(1, talk))
     hidden = hidden.reshape(tensor, steps, per, width).transpose(1, 0, 2, 3)

time: 205 us -> 187 us (0.912)
  matrix products: 0 us -> 9.98 us
  Pallas kernels: 68.4 us -> 59.9 us
  waiting for transfers between devices: 67.7 us -> 59.4 us
  starting transfers between devices: 50.3 us -> 43.5 us
  local copies, waits for them, and re-layouts: 15.5 us -> 11.4 us
    ppermute x8 -> x7, waiting for transfers between devices: 22.9 us -> 7.58 us  [send(): return lax.ppermute(x, 'tensor', pairs)]
    pallas_call x1 -> x2, Pallas kernels: 19.3 us -> 6.4 us  [the longest x1 3.61 us: collect_weight(): pl.pallas_call(collect_weight_kernel, in_specs=[pl.BlockSpec(memory_space...]
    dot_general x0 -> x2, matrix products: none -> 9.98 us  [the longest x1 5.44 us: local(): jnp.dot(hidden, bridge_weight, preferred_element_type=F32).astype(BF16)]
    all_to_all x1, starting transfers between devices: 14.1 us -> 4.49 us  [local(): lax.all_to_all(parts.reshape(tensor, steps * per, talk), 'tensor', 0, 0,...]
    ppermute x0 -> x5, starting transfers between devices: none -> 8.25 us  [gather_ids(): lax.ppermute(x, 'dp', [(peer(i), i) for i in range(count)])]
    all_to_all x2 -> x1, starting transfers between devices: 13.3 us -> 6.65 us  [local(): share = lax.all_to_all(share, 'tensor', 0, 0, tiled=True)]
    all_to_all x1, waiting for transfers between devices: 0.01 us -> 3.87 us  [local(): emb = lax.all_to_all(emb, BOTH, 0, 0, tiled=True)]
    reshape x1 -> x0, local copies, waits for them, and re-layouts: 2.3 us -> none  [local(): residual.reshape(steps, tensor, per, width).transpose(1, 0, 2, 3)]
  transfers between devices with their start and end apart: 17 -> 20, of which waited for: 7 -> 5; matrix products, arithmetic and copies ran while one was open for 2% -> 7% of each run, Pallas kernels for 32% -> 30%
where the time goes in v4:
time: 187 us; the launch traced here: 186 us
  Pallas kernels  59.9 us (32%)
  waiting for transfers between devices  59.4 us (32%)
  starting transfers between devices  43.5 us (23%)
  local copies, waits for them, and re-layouts  11.4 us (6%)
  matrix products  9.98 us (5%)
    all_to_all x1, waiting for transfers between devices, local(): lax.all_to_all(parts.reshape(tensor, steps * per, talk), 'tensor', 0, 0,...  46.7 us
    pallas_call x2, Pallas kernels, look_up(): pl.pallas_call(functools.partial(look_kernel, group=group), in_specs=[sme...  31.8 us
    ppermute x7, starting transfers between devices, send(): return lax.ppermute(x, 'tensor', pairs)  11 us
    pallas_call x1, Pallas kernels, attention(): pl.pallas_call(attention_kernel, grid=(blocks,), in_specs=[pl.BlockSpec((...  10.7 us
    all_to_all x1, starting transfers between devices, local(): emb = lax.all_to_all(emb, BOTH, 0, 0, tiled=True)  8.48 us
    ppermute x5, starting transfers between devices, gather_ids(): lax.ppermute(x, 'dp', [(peer(i), i) for i in range(count)])  8.25 us
    unnamed x24, local copies, waits for them, and re-layouts  7.83 us
    ppermute x7, waiting for transfers between devices, send(): return lax.ppermute(x, 'tensor', pairs)  7.58 us
  transfers between devices with their start and end apart: 20, of which 5 were waited for; matrix products, arithmetic and copies ran while one was open for 7% of the time, Pallas kernels for 30%

profile of v4, /device:TPU:0, one launch (start us, length us, event | category | flops | bytes accessed | tf_op | source)
XLA Modules:
  0.0 186.4 jit_solution(857463152823657848)
XLA Ops:
  1.3 1.7 collective-permute-start
  3.6 3.8 %share_rows.1 = bf16[8,2,64,1024]{3,2,1,0:T(8,128)(2,1)} custom-call(s32[2]{0:T(128)} %pad_add_fusion.4.subs_ref, bf16[512,8192]{1,0:T(8,128)(2,1)} %w_ref.1), custom_call_target="tpu_custom_call" | custom-call | bytes 4194304 | tf_op jit(solution)/shard_map/share_rows/pallas_call | solution.py:384
  7.4 6.6 %all-to-all-start = ((bf16[8,2,64,1024]{3,2,1,0:T(8,128)(2,1)}), bf16[8,2,64,1024]{3,2,1,0:T(8,128)(2,1)S(1)}, u32[]{:S(2)}, u32[]{:S(2)}) async-start(bf16[8,2,64,1024]{3,2,1,0:T(8,128)(2,1)} %share_rows.1), calls=%async_computation | async-start | bytes 4194304 | tf_op jit(solution)/shard_map/all_to_all | solution.py:456
  15.3 1.9 %collective-permute-start.4 = (s32[4,8,128]{2,1,0:T(8,128)S(1)}, s32[4,8,128]{2,1,0:T(8,128)S(1)}, u32[]{:S(2)}, u32[]{:S(2)}) collective-permute-start(s32[4,8,128]{2,1,0:T(8,128)S(1)} %pad_add_fusion.1), channel_id=1, source_target_pairs={{48,0},{56,8},{0,16},{8,24},{16,32},{24,40},{32,48},{40,56},{112,6... | collective-permute-start | bytes 49160 | tf_op jit(solution)/shard_map/ppermute | solution.py:322
  17.2 3.6 %collective-permute-start.3 = (s32[4,8,128]{2,1,0:T(8,128)S(1)}, s32[4,8,128]{2,1,0:T(8,128)S(1)}, u32[]{:S(2)}, u32[]{:S(2)}) collective-permute-start(s32[4,8,128]{2,1,0:T(8,128)S(1)} %pad_add_fusion.1), channel_id=1, source_target_pairs={{32,0},{40,8},{48,16},{56,24},{0,32},{8,40},{16,48},{24,56},{96,64... | collective-permute-start | bytes 49160 | tf_op jit(solution)/shard_map/ppermute | solution.py:322
  22.5 10.7 %attention.1 = bf16[8,4,16,512]{3,2,1,0:T(8,128)(2,1)} custom-call(s32[128,128]{1,0:T(8,128)} %broadcast_in_dim.4.len_ref, bf16[4,128,512]{2,1,0:T(8,128)(2,1)} %q_ref, bf16[128,64,128]{2,1,0:T(8,128)(2,1)} %ck_ref.1, bf16[128,64,128]{2,1,0:T(8,128)(2,1)} %cv_ref.1, bf16[4,128,128]{2,1,0:T(8,128)(2,1)} %nk_ref.1, bf16[4,128,128]{2,1,0:T(8,128)(2,1)} %nv_ref.1), custom_call_target="tpu_custom_call" | custom-call | flops 8000000000 | bytes 6291456 | tf_op jit(solution)/shard_map/attention/pallas_call | solution.py:75
  33.3 3.5 %collective-permute-start.8 = (bf16[512,512]{1,0:T(8,128)(2,1)}, bf16[512,512]{1,0:T(8,128)(2,1)}, u32[]{:S(2)}, u32[]{:S(2)}) collective-permute-start(bf16[512,512]{1,0:T(8,128)(2,1)} %bitcast.41), channel_id=1, source_target_pairs={{0,1},{1,0},{2,3},{3,2},{4,5},{5,4},{6,7},{7,6},{8,9},{9,8},{10,11... | collective-permute-start | bytes 1572872 | tf_op jit(solution)/shard_map/ppermute | solution.py:343
  36.8 3.0 %collective-permute-start.7 = (bf16[512,512]{1,0:T(8,128)(2,1)}, bf16[512,512]{1,0:T(8,128)(2,1)}, u32[]{:S(2)}, u32[]{:S(2)}) collective-permute-start(bf16[512,512]{1,0:T(8,128)(2,1)} %bitcast.42), channel_id=1, source_target_pairs={{0,4},{1,5},{2,6},{3,7},{4,0},{5,1},{6,2},{7,3},{8,12},{9,13},{10,... | collective-permute-start | bytes 1572872 | tf_op jit(solution)/shard_map/ppermute | solution.py:343
  41.8 17.8 %look_up.2.refs_0_ = bf16[128,32,128]{2,1,0:T(8,128)(2,1)S(1)} custom-call(s32[1]{0:T(128)} %bitcast.13.shift_ref, s32[16]{0:T(128)S(1)} %fusion.3.spot_ref, s32[16384]{0:T(1024)S(1)} %bitcast.39, bf16[28,76032]{1,0:T(8,128)(2,1)} %table_ref.2), custom_call_target="tpu_custom_call" | custom-call | bytes 47185920 | tf_op jit(solution)/shard_map/look_up/pallas_call | solution.py:164
  59.7 4.7 %collective-permute-done.6.refs_2_ = bf16[512,512]{1,0:T(8,128)(2,1)} collective-permute-done((bf16[512,512]{1,0:T(8,128)(2,1)}, bf16[512,512]{1,0:T(8,128)(2,1)}, u32[]{:S(2)}, u32[]{:S(2)}) %collective-permute-start.6) | collective-permute-done | bytes 524320 | tf_op jit(solution)/shard_map/ppermute | solution.py:343
  64.4 2.9 %collective-permute-done.5.refs_1_ = bf16[512,512]{1,0:T(8,128)(2,1)} collective-permute-done((bf16[512,512]{1,0:T(8,128)(2,1)}, bf16[512,512]{1,0:T(8,128)(2,1)}, u32[]{:S(2)}, u32[]{:S(2)}) %collective-permute-start.5) | collective-permute-done | bytes 524320 | tf_op jit(solution)/shard_map/ppermute | solution.py:343
  68.9 4.1 %collective-permute-start.13 = (bf16[8,1,64,1024]{3,2,1,0:T(8,128)(2,1)}, bf16[8,1,64,1024]{3,2,1,0:T(8,128)(2,1)}, u32[]{:S(2)}, u32[]{:S(2)}) collective-permute-start(bf16[8,1,64,1024]{3,2,1,0:T(8,128)(2,1)} %get-tuple-element.42), channel_id=1, source_target_pairs={{0,48},{8,56},{16,32},{24,40},{32,16},{40,24},{48,0},{56,8},{64,11... | collective-permute-start | bytes 3145736 | tf_op jit(solution)/shard_map/ppermute | solution.py:417
  76.6 13.9 %look_up.3 = bf16[128,32,128]{2,1,0:T(8,128)(2,1)} custom-call(s32[1]{0:T(128)} %bitcast.13.shift_ref, s32[16]{0:T(128)S(1)} %fusion.3.spot_ref, s32[16384]{0:T(1024)S(1)} %bitcast.40, bf16[28,8448]{1,0:T(8,128)(2,1)S(1)} %copy-done.2, bf16[128,32,128]{2,1,0:T(8,128)(2,1)S(1)} %look_up.2.refs_0_), custom_call_target="tpu_custom_call" | custom-call | bytes 23068672 | tf_op jit(solution)/shard_map/look_up/pallas_call | solution.py:164
  92.8 2.8 %collect_rows.1 = (bf16[512,4096]{1,0:T(8,128)(2,1)S(1)}, bf16[8,4,16,1024]{3,2,1,0:T(8,128)(2,1)S(1)}, f32[8,128]{1,0:T(8,128)S(1)}) custom-call(s32[8]{0:T(128)S(1)} %stack.76.order_ref, bf16[512,512]{1,0:T(8,128)(2,1)S(1)} %bitcast.45, bf16[512,512]{1,0:T(8,128)(2,1)} %collective-permute-done.5.refs_1_, bf16[512,512]{1,0:T(8,128)(2,1)} %collective-permute-done.6.refs_2_, ...), custom_call_target="tpu_custom_call" | custom-call | bytes 8388608 | tf_op jit(solution)/shard_map/collect_rows/pallas_call | solution.py:203
  95.6 2.0 %copy-done.4 = bf16[512,4096]{1,0:T(8,128)(2,1)} copy-done((bf16[512,4096]{1,0:T(8,128)(2,1)}, bf16[512,4096]{1,0:T(8,128)(2,1)S(1)}, u32[]{:S(2)}) %copy-start.4) | copy-done | bytes 4194328
  99.2 8.5 %all-to-all-start.2 = ((bf16[128,32,128]{2,1,0:T(8,128)(2,1)}), bf16[128,32,128]{2,1,0:T(8,128)(2,1)}, u32[]{:S(2)}, u32[]{:S(2)}) async-start(bf16[128,32,128]{2,1,0:T(8,128)(2,1)} %look_up.3), calls=%async_computation.2 | async-start | bytes 2097152 | tf_op jit(solution)/shard_map/all_to_all | solution.py:469
  107.8 3.6 %collect_weight.1 = bf16[8,8,64,1024]{3,2,1,0:T(8,128)(2,1)S(1)} custom-call(s32[8]{0:T(128)S(1)} %stack.89.subs_ref, f32[8,128]{1,0:T(8,128)S(1)} %get-tuple-element.37.done_ref, bf16[8,2,64,1024]{3,2,1,0:T(8,128)(2,1)S(1)} %all-to-all-done.refs_0_, bf16[8,1,64,1024]{3,2,1,0:T(8,128)(2,1)} %collective-permute-done.12.refs_1_, ...), custom_call_target="tpu_custom_call" | custom-call | bytes 10485760 | tf_op jit(solution)/shard_map/collect_weight/pallas_call | solution.py:239
  111.8 4.5 %fusion = bf16[512,1024]{1,0:T(8,128)(2,1)S(1)} fusion(bf16[8,4,16,1024]{3,2,1,0:T(8,128)(2,1)S(1)} %copy-done.7, bf16[512,4096]{1,0:T(8,128)(2,1)S(1)} %copy-done.5, bf16[4096,1024]{1,0:T(8,128)(2,1)S(1)} %bitcast.37), kind=kOutput, calls=%fused_computation.2 | convolution fusion | flops 4296540160 | bytes 14680064 | tf_op jit(solution)/shard_map/dot_general | solution.py:471
  116.4 5.4 %convolution_convert_fusion = bf16[512,3584]{1,0:T(8,128)(2,1)} fusion(bf16[512,1024]{1,0:T(8,128)(2,1)S(1)} %fusion, bf16[1024,3584]{1,0:T(8,128)(2,1)S(1)} %bitcast.53), kind=kOutput, calls=%fused_computation | convolution fusion | flops 3759931392 | bytes 12058624 | tf_op jit(solution)/shard_map/dot_general | solution.py:473
  121.8 3.9 %all-to-all-done.2.emb_ref = bf16[128,32,128]{2,1,0:T(8,128)(2,1)} async-done(((bf16[128,32,128]{2,1,0:T(8,128)(2,1)}), bf16[128,32,128]{2,1,0:T(8,128)(2,1)}, u32[]{:S(2)}, u32[]{:S(2)}) %all-to-all-start.2) | async-done | bytes 1048608 | tf_op jit(solution)/shard_map/all_to_all | solution.py:469
  125.7 4.5 %all-to-all-start.1 = ((bf16[8,64,3584]{2,1,0:T(8,128)(2,1)}), bf16[8,64,3584]{2,1,0:T(8,128)(2,1)}, u32[]{:S(2)}, u32[]{:S(2)}) async-start(bf16[8,64,3584]{2,1,0:T(8,128)(2,1)} %bitcast.46), calls=%async_computation.1 | async-start | bytes 7340032 | tf_op jit(solution)/shard_map/all_to_all | solution.py:474
  130.2 3.8 %place.1.emb_ref = f32[64,3584]{1,0:T(8,128)} custom-call(bf16[128,32,128]{2,1,0:T(8,128)(2,1)} %all-to-all-done.2.emb_ref), custom_call_target="tpu_custom_call" | custom-call | bytes 8388608 | tf_op jit(solution)/shard_map/place/pallas_call | solution.py:274
  135.0 46.7 %all-to-all-done.1.part_ref = bf16[8,64,3584]{2,1,0:T(8,128)(2,1)} async-done(((bf16[8,64,3584]{2,1,0:T(8,128)(2,1)}), bf16[8,64,3584]{2,1,0:T(8,128)(2,1)}, u32[]{:S(2)}, u32[]{:S(2)}) %all-to-all-start.1) | async-done | bytes 3670048 | tf_op jit(solution)/shard_map/all_to_all | solution.py:474
  182.9 3.5 %finish.1 = bf16[64,3584]{1,0:T(8,128)(2,1)} custom-call(bf16[8,64,3584]{2,1,0:T(8,128)(2,1)} %all-to-all-done.1.part_ref, f32[64,3584]{1,0:T(8,128)S(1)} %copy-done, bf16[1,3584]{1,0:T(2,128)(2,1)S(1)} %reshape.43.gain_ref), custom_call_target="tpu_custom_call" | custom-call | bytes 8388608 | tf_op jit(solution)/shard_map/finish/pallas_call | solution.py:307
  (63 shorter events, 18.1 us)
Async XLA Ops:
  1.3 6.0 %collective-permute-start = (s32[8,128]{1,0:T(8,128)S(1)}, s32[8,128]{1,0:T(8,128)S(1)}, u32[]{:S(2)}, u32[]{:S(2)}) collective-permute-start(s32[8,128]{1,0:T(8,128)S(1)} %get-tuple-element.45), channel_id=1, source_target_pairs={{64,0},{72,8},{80,16},{88,24},{96,32},{104,40},{112,48},{120,56},{... | collective-permute-start | bytes 12296 | tf_op jit(solution)/shard_map/ppermute | solution.py:322
  7.4 14.4 %copy-start.9 = (s32[128]{0:T(128)S(1)}, s32[128]{0:T(128)}, u32[]{:S(2)}) copy-start(s32[128]{0:T(128)} %param.19) | copy-start | bytes 1540
  7.4 59.9 %all-to-all-start = ((bf16[8,2,64,1024]{3,2,1,0:T(8,128)(2,1)}), bf16[8,2,64,1024]{3,2,1,0:T(8,128)(2,1)S(1)}, u32[]{:S(2)}, u32[]{:S(2)}) async-start(bf16[8,2,64,1024]{3,2,1,0:T(8,128)(2,1)} %share_rows.1), calls=%async_computation | async-start | bytes 4194304 | tf_op jit(solution)/shard_map/all_to_all | solution.py:456
  14.0 1.3 collective-permute-start.1
  15.3 18.0 %collective-permute-start.4 = (s32[4,8,128]{2,1,0:T(8,128)S(1)}, s32[4,8,128]{2,1,0:T(8,128)S(1)}, u32[]{:S(2)}, u32[]{:S(2)}) collective-permute-start(s32[4,8,128]{2,1,0:T(8,128)S(1)} %pad_add_fusion.1), channel_id=1, source_target_pairs={{48,0},{56,8},{0,16},{8,24},{16,32},{24,40},{32,48},{40,56},{112,6... | collective-permute-start | bytes 49160 | tf_op jit(solution)/shard_map/ppermute | solution.py:322
  17.2 16.1 %collective-permute-start.3 = (s32[4,8,128]{2,1,0:T(8,128)S(1)}, s32[4,8,128]{2,1,0:T(8,128)S(1)}, u32[]{:S(2)}, u32[]{:S(2)}) collective-permute-start(s32[4,8,128]{2,1,0:T(8,128)S(1)} %pad_add_fusion.1), channel_id=1, source_target_pairs={{32,0},{40,8},{48,16},{56,24},{0,32},{8,40},{16,48},{24,56},{96,64... | collective-permute-start | bytes 49160 | tf_op jit(solution)/shard_map/ppermute | solution.py:322
  20.8 12.5 %collective-permute-start.2 = (s32[4,8,128]{2,1,0:T(8,128)S(1)}, s32[4,8,128]{2,1,0:T(8,128)S(1)}, u32[]{:S(2)}, u32[]{:S(2)}) collective-permute-start(s32[4,8,128]{2,1,0:T(8,128)S(1)} %pad_add_fusion.1), channel_id=1, source_target_pairs={{16,0},{24,8},{32,16},{40,24},{48,32},{56,40},{0,48},{8,56},{80,64... | collective-permute-start | bytes 49160 | tf_op jit(solution)/shard_map/ppermute | solution.py:322
  33.3 26.4 %collective-permute-start.8 = (bf16[512,512]{1,0:T(8,128)(2,1)}, bf16[512,512]{1,0:T(8,128)(2,1)}, u32[]{:S(2)}, u32[]{:S(2)}) collective-permute-start(bf16[512,512]{1,0:T(8,128)(2,1)} %bitcast.41), channel_id=1, source_target_pairs={{0,1},{1,0},{2,3},{3,2},{4,5},{5,4},{6,7},{7,6},{8,9},{9,8},{10,11... | collective-permute-start | bytes 1572872 | tf_op jit(solution)/shard_map/ppermute | solution.py:343
  36.8 22.8 %collective-permute-start.7 = (bf16[512,512]{1,0:T(8,128)(2,1)}, bf16[512,512]{1,0:T(8,128)(2,1)}, u32[]{:S(2)}, u32[]{:S(2)}) collective-permute-start(bf16[512,512]{1,0:T(8,128)(2,1)} %bitcast.42), channel_id=1, source_target_pairs={{0,4},{1,5},{2,6},{3,7},{4,0},{5,1},{6,2},{7,3},{8,12},{9,13},{10,... | collective-permute-start | bytes 1572872 | tf_op jit(solution)/shard_map/ppermute | solution.py:343
  39.8 24.6 %collective-permute-start.6 = (bf16[512,512]{1,0:T(8,128)(2,1)}, bf16[512,512]{1,0:T(8,128)(2,1)}, u32[]{:S(2)}, u32[]{:S(2)}) collective-permute-start(bf16[512,512]{1,0:T(8,128)(2,1)} %bitcast.43), channel_id=1, source_target_pairs={{0,6},{1,7},{2,0},{3,1},{4,2},{5,3},{6,4},{7,5},{8,14},{9,15},{10,... | collective-permute-start | bytes 1572872 | tf_op jit(solution)/shard_map/ppermute | solution.py:343
  41.0 26.3 %collective-permute-start.5 = (bf16[512,512]{1,0:T(8,128)(2,1)}, bf16[512,512]{1,0:T(8,128)(2,1)}, u32[]{:S(2)}, u32[]{:S(2)}) collective-permute-start(bf16[512,512]{1,0:T(8,128)(2,1)} %bitcast.44), channel_id=1, source_target_pairs={{0,2},{1,3},{2,4},{3,5},{4,6},{5,7},{6,0},{7,1},{8,10},{9,11},{10,... | collective-permute-start | bytes 1572872 | tf_op jit(solution)/shard_map/ppermute | solution.py:343
  68.9 29.7 %collective-permute-start.13 = (bf16[8,1,64,1024]{3,2,1,0:T(8,128)(2,1)}, bf16[8,1,64,1024]{3,2,1,0:T(8,128)(2,1)}, u32[]{:S(2)}, u32[]{:S(2)}) collective-permute-start(bf16[8,1,64,1024]{3,2,1,0:T(8,128)(2,1)} %get-tuple-element.42), channel_id=1, source_target_pairs={{0,48},{8,56},{16,32},{24,40},{32,16},{40,24},{48,0},{56,8},{64,11... | collective-permute-start | bytes 3145736 | tf_op jit(solution)/shard_map/ppermute | solution.py:417
  72.9 25.6 %collective-permute-start.12 = (bf16[8,1,64,1024]{3,2,1,0:T(8,128)(2,1)}, bf16[8,1,64,1024]{3,2,1,0:T(8,128)(2,1)}, u32[]{:S(2)}, u32[]{:S(2)}) collective-permute-start(bf16[8,1,64,1024]{3,2,1,0:T(8,128)(2,1)} %get-tuple-element.43), channel_id=1, source_target_pairs={{0,16},{8,24},{16,0},{24,8},{32,48},{40,56},{48,32},{56,40},{64,80... | collective-permute-start | bytes 3145736 | tf_op jit(solution)/shard_map/ppermute | solution.py:416
  72.9 17.6 %collective-permute-start.11 = (bf16[512,512]{1,0:T(8,128)(2,1)}, bf16[512,512]{1,0:T(8,128)(2,1)}, u32[]{:S(2)}, u32[]{:S(2)}) collective-permute-start(bf16[512,512]{1,0:T(8,128)(2,1)} %collective-permute-done.7.refs_3_), channel_id=1, source_target_pairs={{0,1},{1,0},{2,3},{3,2},{4,5},{5,4},{6,7},{7,6},{8,9},{9,8},{10,11... | collective-permute-start | bytes 1572872 | tf_op jit(solution)/shard_map/ppermute | solution.py:343
  73.4 17.1 %collective-permute-start.10 = (bf16[512,512]{1,0:T(8,128)(2,1)}, bf16[512,512]{1,0:T(8,128)(2,1)}, u32[]{:S(2)}, u32[]{:S(2)}) collective-permute-start(bf16[512,512]{1,0:T(8,128)(2,1)} %collective-permute-done.8.refs_4_), channel_id=1, source_target_pairs={{0,6},{1,7},{2,0},{3,1},{4,2},{5,3},{6,4},{7,5},{8,14},{9,15},{10,... | collective-permute-start | bytes 1572872 | tf_op jit(solution)/shard_map/ppermute | solution.py:343
  74.8 15.7 %collective-permute-start.9 = (bf16[512,512]{1,0:T(8,128)(2,1)}, bf16[512,512]{1,0:T(8,128)(2,1)}, u32[]{:S(2)}, u32[]{:S(2)}) collective-permute-start(bf16[512,512]{1,0:T(8,128)(2,1)} %collective-permute-done.8.refs_4_), channel_id=1, source_target_pairs={{0,2},{1,3},{2,4},{3,5},{4,6},{5,7},{6,0},{7,1},{8,10},{9,11},{10,... | collective-permute-start | bytes 1572872 | tf_op jit(solution)/shard_map/ppermute | solution.py:343
  98.5 9.2 %collective-permute-start.14 = (bf16[8,2,64,1024]{3,2,1,0:T(8,128)(2,1)S(1)}, bf16[8,2,64,1024]{3,2,1,0:T(8,128)(2,1)}, u32[]{:S(2)}, u32[]{:S(2)}) collective-permute-start(bf16[8,2,64,1024]{3,2,1,0:T(8,128)(2,1)S(1)} %all-to-all-done.refs_0_), channel_id=1, source_target_pairs={{0,8},{8,0},{16,24},{24,16},{32,40},{40,32},{48,56},{56,48},{64,72... | collective-permute-start | bytes 6291464 | tf_op jit(solution)/shard_map/ppermute | solution.py:423
  98.6 9.2 %collective-permute-start.15 = (bf16[8,1,64,1024]{3,2,1,0:T(8,128)(2,1)}, bf16[8,1,64,1024]{3,2,1,0:T(8,128)(2,1)S(1)}, u32[]{:S(2)}, u32[]{:S(2)}) collective-permute-start(bf16[8,1,64,1024]{3,2,1,0:T(8,128)(2,1)} %collective-permute-done.12.refs_1_), channel_id=1, source_target_pairs={{0,8},{8,0},{16,24},{24,16},{32,40},{40,32},{48,56},{56,48},{64,72... | collective-permute-start | bytes 3145736 | tf_op jit(solution)/shard_map/ppermute | solution.py:423
  99.1 8.7 %collective-permute-start.16 = (bf16[8,1,64,1024]{3,2,1,0:T(8,128)(2,1)}, bf16[8,1,64,1024]{3,2,1,0:T(8,128)(2,1)}, u32[]{:S(2)}, u32[]{:S(2)}) collective-permute-start(bf16[8,1,64,1024]{3,2,1,0:T(8,128)(2,1)} %collective-permute-done.13.refs_2_), channel_id=1, source_target_pairs={{0,8},{8,0},{16,24},{24,16},{32,40},{40,32},{48,56},{56,48},{64,72... | collective-permute-start | bytes 3145736 | tf_op jit(solution)/shard_map/ppermute | solution.py:423
  99.2 26.4 %all-to-all-start.2 = ((bf16[128,32,128]{2,1,0:T(8,128)(2,1)}), bf16[128,32,128]{2,1,0:T(8,128)(2,1)}, u32[]{:S(2)}, u32[]{:S(2)}) async-start(bf16[128,32,128]{2,1,0:T(8,128)(2,1)} %look_up.3), calls=%async_computation.2 | async-start | bytes 2097152 | tf_op jit(solution)/shard_map/all_to_all | solution.py:469
  107.8 8.6 %slice-start = ((s8[7340032]{0:T(1024)(128)(4,1)}), s8[4194304]{0:T(1024)(128)(4,1)S(1)}, s32[]{:S(2)}) async-start(s8[7340032]{0:T(1024)(128)(4,1)} %bitcast.52), calls=%async_computation.3 | async-start | bytes 8388608
  111.8 4.6 %slice-start.1 = ((s8[7340032]{0:T(1024)(128)(4,1)}), s8[3145728]{0:T(1024)(128)(4,1)S(1)}, s32[]{:S(2)}) async-start(s8[7340032]{0:T(1024)(128)(4,1)} %bitcast.52), calls=%async_computation.4 | async-start | bytes 6291456
  121.8 8.4 %copy-start.8 = (bf16[3584]{0:T(1024)(128)(2,1)S(1)}, bf16[3584]{0:T(1024)(128)(2,1)}, u32[]{:S(2)}) copy-start(bf16[3584]{0:T(1024)(128)(2,1)} %param.27) | copy-start | bytes 21508
  125.7 56.1 %all-to-all-start.1 = ((bf16[8,64,3584]{2,1,0:T(8,128)(2,1)}), bf16[8,64,3584]{2,1,0:T(8,128)(2,1)}, u32[]{:S(2)}, u32[]{:S(2)}) async-start(bf16[8,64,3584]{2,1,0:T(8,128)(2,1)} %bitcast.46), calls=%async_computation.1 | async-start | bytes 7340032 | tf_op jit(solution)/shard_map/all_to_all | solution.py:474
  (8 other events, 15.3 us)

commit v5 on v4

--- a/solution.py
+++ b/solution.py
@@ -14,6 +14,7 @@
 GROUP = QH // KVH
 STEPS = 4
 SB = 16
+BLOCKS = 2
 LANES = 128
 FPAD = 32
 PACK = LANES // FPAD
@@ -28,62 +29,69 @@
 
 
 def attention_kernel(len_ref, q_ref, ck_ref, cv_ref, nk_ref, nv_ref, out_ref):
-    rows = STEPS * GROUP * SB
+    some = SB // 2
+    rows = STEPS * GROUP * some
     scale = 1.0 / HD**0.5
-    queries = jnp.concatenate(
-        [q_ref[t, :, h * HD : (h + 1) * HD] for t in range(STEPS) for h in range(GROUP)], axis=0
-    )
-    cached_k = ck_ref[...].reshape(SB * CAP, HD)
-    cached_v = cv_ref[...].reshape(SB * CAP, HD)
-    fresh_k = nk_ref[...].reshape(STEPS * SB, HD)
-    fresh_v = nv_ref[...].reshape(STEPS * SB, HD)
     contract = (((1,), (1,)), ((), ()))
-    score_c = lax.dot_general(queries, cached_k, contract, preferred_element_type=F32) * scale
-    score_n = lax.dot_general(queries, fresh_k, contract, preferred_element_type=F32) * scale
-    own = iota((rows, 1), 0) % SB
+    query = [
+        q_ref[t, :, h * HD : (h + 1) * HD].astype(F32) for t in range(STEPS) for h in range(GROUP)
+    ]
+    fresh = [[ref[t].astype(F32) for t in range(STEPS)] for ref in (nk_ref, nv_ref)]
+    own = iota((rows, 1), 0) % some
     start = own * CAP
-    stop = start + jnp.concatenate([len_ref[:, :1]] * (STEPS * GROUP), axis=0)
-    spot = iota((rows, SB * CAP), 1)
-    score_c = jnp.where((spot >= start) & (spot < stop), score_c, -1e30)
-    row, col = iota((rows, STEPS * SB), 0), iota((rows, STEPS * SB), 1)
-    seen = (row % SB == col % SB) & (col // SB <= row // (GROUP * SB))
-    score_n = jnp.where(seen, score_n, -1e30)
-    top = jnp.maximum(
-        jnp.max(score_c, axis=-1, keepdims=True), jnp.max(score_n, axis=-1, keepdims=True)
-    )
-    exp_c = jnp.exp(score_c - top)
-    exp_n = jnp.exp(score_n - top)
-    total = jnp.sum(exp_c, axis=-1, keepdims=True) + jnp.sum(exp_n, axis=-1, keepdims=True)
-    inverse = 1.0 / total
-    weight_c = (exp_c * inverse).astype(BF16)
-    weight_n = (exp_n * inverse).astype(BF16)
-    attended = jnp.dot(weight_c, cached_v, preferred_element_type=F32)
-    attended = attended + jnp.dot(weight_n, fresh_v, preferred_element_type=F32)
-    attended = attended.astype(BF16)
+    spot = iota((rows, some * CAP), 1)
+    row, col = iota((rows, STEPS * some), 0), iota((rows, STEPS * some), 1)
+    seen = (row % some == col % some) & (col // some <= row // (GROUP * some))
+    results = []
+    for part in range(2 * BLOCKS):
+        here = slice(part * some, (part + 1) * some)
+        queries = jnp.concatenate([q[here] for q in query], axis=0).astype(BF16)
+        cached_k = ck_ref[here].reshape(some * CAP, HD)
+        cached_v = cv_ref[here].reshape(some * CAP, HD)
+        fresh_k, fresh_v = [jnp.concatenate([x[here] for x in f], axis=0).astype(BF16) for f in fresh]
+        score_c = lax.dot_general(queries, cached_k, contract, preferred_element_type=F32) * scale
+        score_n = lax.dot_general(queries, fresh_k, contract, preferred_element_type=F32) * scale
+        stop = start + jnp.concatenate([len_ref[here, :1]] * (STEPS * GROUP), axis=0)
+        score_c = jnp.where((spot >= start) & (spot < stop), score_c, -1e30)
+        score_n = jnp.where(seen, score_n, -1e30)
+        top = jnp.maximum(
+            jnp.max(score_c, axis=-1, keepdims=True), jnp.max(score_n, axis=-1, keepdims=True)
+        )
+        exp_c = jnp.exp(score_c - top)
+        exp_n = jnp.exp(score_n - top)
+        total = jnp.sum(exp_c, axis=-1, keepdims=True) + jnp.sum(exp_n, axis=-1, keepdims=True)
+        inverse = 1.0 / total
+        weight_c = (exp_c * inverse).astype(BF16)
+        weight_n = (exp_n * inverse).astype(BF16)
+        attended = jnp.dot(weight_c, cached_v, preferred_element_type=F32)
+        results.append(attended + jnp.dot(weight_n, fresh_v, preferred_element_type=F32))
     for t in range(STEPS):
         for h in range(GROUP):
-            at = (t * GROUP + h) * SB
-            out_ref[0, t, :, h * HD : (h + 1) * HD] = attended[at : at + SB]
+            at = (t * GROUP + h) * some
+            for b in range(BLOCKS):
+                both = [r[at : at + some] for r in results[2 * b : 2 * b + 2]]
+                both = jnp.concatenate(both, axis=0).astype(BF16)
+                out_ref[b, t, :, h * HD : (h + 1) * HD] = both
 
 
 def attention(query, new_keys, new_values, cache_keys, cache_values, cache_lengths):
     steps, streams, width = query.shape
     blocks = streams // SB
     lengths = jnp.broadcast_to(cache_lengths[:, None], (streams, LANES))
-    fresh = pl.BlockSpec((steps, SB, HD), lambda i: (0, i, 0))
-    cached = pl.BlockSpec((SB, CAP, HD), lambda i: (i, 0, 0))
+    fresh = pl.BlockSpec((steps, BLOCKS * SB, HD), lambda i: (0, i, 0))
+    cached = pl.BlockSpec((BLOCKS * SB, CAP, HD), lambda i: (i, 0, 0))
     return pl.pallas_call(
         attention_kernel,
-        grid=(blocks,),
+        grid=(blocks // BLOCKS,),
         in_specs=[
-            pl.BlockSpec((SB, LANES), lambda i: (i, 0)),
-            pl.BlockSpec((steps, SB, width), lambda i: (0, i, 0)),
+            pl.BlockSpec((BLOCKS * SB, LANES), lambda i: (i, 0)),
+            pl.BlockSpec((steps, BLOCKS * SB, width), lambda i: (0, i, 0)),
             cached,
             cached,
             fresh,
             fresh,
         ],
-        out_specs=pl.BlockSpec((1, steps, SB, width), lambda i: (i, 0, 0, 0)),
+        out_specs=pl.BlockSpec((BLOCKS, steps, SB, width), lambda i: (i, 0, 0, 0)),
         out_shape=jax.ShapeDtypeStruct((blocks, steps, SB, width), BF16),
         compiler_params=pltpu.CompilerParams(vmem_limit_bytes=58 * MIB),
         cost_estimate=pl.CostEstimate(flops=8 * 10**9, bytes_accessed=6 * MIB, transcendentals=0),
@@ -168,7 +176,7 @@
         out_shape=jax.ShapeDtypeStruct((groups * owners, rows // 2, LANES), BF16),
         scratch_shapes=[
             pltpu.VMEM((table.shape[1], LANES), F32),
-            pltpu.VMEM((8 * rows, LANES), F32),
+            pltpu.VMEM((32 * rows, LANES), F32),
         ],
         compiler_params=pltpu.CompilerParams(vmem_limit_bytes=(table.shape[1] // 2048 + 14) * MIB),
         cost_estimate=pl.CostEstimate(
@@ -178,16 +186,22 @@
     )(shift, spots, ids.reshape(-1), table, *other)
 
 
-def collect_rows_kernel(order_ref, *refs, owners):
+def collect_rows_kernel(order_ref, spot_ref, *refs, owners):
     a_refs = refs[:owners]
     res_ref, a_all, res_all, done, a_sem, res_sem = refs[owners:]
-    depth = a_refs[0].shape[1]
+    rows, depth = a_refs[0].shape
+    size = rows // owners
     copies = []
-    for t in range(STEPS):
-        copies.append(pltpu.make_async_copy(res_ref.at[t], res_all.at[:, t], res_sem.at[t]))
-    for k in range(owners):
-        at = pl.multiple_of(order_ref[k] * depth, depth)
-        copies.append(pltpu.make_async_copy(a_refs[k], a_all.at[:, pl.ds(at, depth)], a_sem.at[k]))
+    for b in range(owners):
+        to = pl.ds(pl.multiple_of(spot_ref[b] * size, size), size)
+        for k in range(owners):
+            at = pl.multiple_of(order_ref[k] * depth, depth)
+            source = a_refs[k].at[b * size : (b + 1) * size]
+            target = a_all.at[to, pl.ds(at, depth)]
+            copies.append(pltpu.make_async_copy(source, target, a_sem.at[b, k]))
+        for t in range(STEPS):
+            target = res_all.at[spot_ref[b], t]
+            copies.append(pltpu.make_async_copy(res_ref.at[t, b], target, res_sem.at[b, t]))
     for copy in copies:
         copy.start()
     for copy in copies:
@@ -195,26 +209,54 @@
     done[...] = jnp.zeros_like(done)
 
 
-def collect_rows(attended, order, residual):
+def collect_rows(attended, order, spots, residual):
     owners = len(attended)
     rows, depth = attended[0].shape
     width = residual.shape[-1]
     vmem = pl.BlockSpec(memory_space=pltpu.VMEM)
+    smem = pl.BlockSpec(memory_space=pltpu.SMEM)
     return pl.pallas_call(
         functools.partial(collect_rows_kernel, owners=owners),
-        in_specs=[pl.BlockSpec(memory_space=pltpu.SMEM)]
-        + [pl.BlockSpec(memory_space=pl.ANY)] * (owners + 1),
+        in_specs=[smem, smem] + [pl.BlockSpec(memory_space=pl.ANY)] * (owners + 1),
         out_specs=[vmem] * 3,
         out_shape=[
             jax.ShapeDtypeStruct((rows, owners * depth), BF16),
             jax.ShapeDtypeStruct((owners, STEPS, rows // STEPS // owners, width), BF16),
             jax.ShapeDtypeStruct((8, LANES), F32),
         ],
-        scratch_shapes=[pltpu.SemaphoreType.DMA((n,)) for n in (owners, STEPS)],
+        scratch_shapes=[pltpu.SemaphoreType.DMA((owners, n)) for n in (owners, STEPS)],
         compiler_params=pltpu.CompilerParams(vmem_limit_bytes=12 * MIB),
         cost_estimate=pl.CostEstimate(flops=0, bytes_accessed=8 * MIB, transcendentals=0),
         name="collect_rows",
-    )(order, *attended, residual)
+    )(order, spots, *attended, residual)
+
+
+def restore_kernel(spot_ref, x_ref, out_ref, sems):
+    steps, owners = out_ref.shape[:2]
+    copies = [
+        pltpu.make_async_copy(x_ref.at[spot_ref[b], t], out_ref.at[t, b], sems.at[b, t])
+        for b in range(owners)
+        for t in range(steps)
+    ]
+    for copy in copies:
+        copy.start()
+    for copy in copies:
+        copy.wait()
+
+
+def restore(x, spots):
+    owners, steps, per, width = x.shape
+    anywhere = pl.BlockSpec(memory_space=pl.ANY)
+    return pl.pallas_call(
+        restore_kernel,
+        in_specs=[pl.BlockSpec(memory_space=pltpu.SMEM), anywhere],
+        out_specs=anywhere,
+        out_shape=jax.ShapeDtypeStruct((steps, owners, per, width), x.dtype),
+        scratch_shapes=[pltpu.SemaphoreType.DMA((owners, steps))],
+        compiler_params=pltpu.CompilerParams(vmem_limit_bytes=12 * MIB),
+        cost_estimate=pl.CostEstimate(flops=0, bytes_accessed=2 * MIB, transcendentals=0),
+        name="restore",
+    )(spots, x)
 
 
 def collect_weight_kernel(subs_ref, done_ref, *refs):
@@ -277,20 +319,23 @@
         in_specs=[pl.BlockSpec((holders // blocks, half, LANES), lambda i: (i, 0, 0))],
         out_specs=pl.BlockSpec((2 * half, talk // blocks), lambda i: (0, i)),
         out_shape=jax.ShapeDtypeStruct((2 * half, talk), F32),
+        compiler_params=pltpu.CompilerParams(vmem_limit_bytes=8 * MIB),
         cost_estimate=pl.CostEstimate(flops=0, bytes_accessed=8 * MIB, transcendentals=0),
         name="place",
     )(emb)
 
 
-def finish_kernel(part_ref, emb_ref, gain_ref, out_ref, mixed):
-    sources, rows, talk = part_ref.shape
+def finish_kernel(*refs):
+    *part_refs, emb_ref, gain_ref, out_ref, mixed = refs
+    rows, talk = out_ref.shape
+    halves = [part_refs[: len(part_refs) // 2], part_refs[len(part_refs) // 2 :]]
     square = jnp.zeros((rows, LANES), F32)
     for c in range(talk // LANES):
         cols = slice(c * LANES, (c + 1) * LANES)
-        total = part_ref[0, :, cols].astype(F32)
-        for s in range(1, sources):
-            total = total + part_ref[s, :, cols].astype(F32)
-        total = total + emb_ref[:, cols]
+        half, at = divmod(c * LANES, talk // 2)
+        total = emb_ref[:, cols]
+        for ref in halves[half]:
+            total = total + ref[:rows, at : at + LANES].astype(F32)
         mixed[:, cols] = total
         square = square + total * total
     mean = jnp.sum(square, axis=-1, keepdims=True) * (1.0 / talk)
@@ -302,18 +347,43 @@
 
 
 def finish(parts, emb, gain):
-    _, rows, talk = parts.shape
+    rows, talk = emb.shape
     vmem = pl.BlockSpec(memory_space=pltpu.VMEM)
     return pl.pallas_call(
         finish_kernel,
-        in_specs=[vmem, vmem, vmem],
+        in_specs=[vmem] * (len(parts) + 2),
         out_specs=vmem,
         out_shape=jax.ShapeDtypeStruct((rows, talk), BF16),
         scratch_shapes=[pltpu.VMEM((rows, talk), F32)],
-        compiler_params=pltpu.CompilerParams(vmem_limit_bytes=32 * MIB),
+        compiler_params=pltpu.CompilerParams(vmem_limit_bytes=8 * MIB),
         cost_estimate=pl.CostEstimate(flops=0, bytes_accessed=8 * MIB, transcendentals=0),
         name="finish",
-    )(parts, emb, gain)
+    )(*parts, emb, gain)
+
+
+def bridge_parts(hidden, bridge_weight):
+    up, down, _, across = tensor_pairs()
+    talk = bridge_weight.shape[1]
+    rows = hidden.shape[0] // 4
+    own = rows // 2
+
+    def product(block, half):
+        weight = bridge_weight[:, half * (talk // 2) : (half + 1) * (talk // 2)]
+        block = hidden[block * rows : (block + 1) * rows]
+        return jnp.dot(block, weight, preferred_element_type=F32)
+
+    by_up = send(product(2, 0).astype(BF16), up)
+    by_down = send(product(2, 1).astype(BF16), down)
+    from_down = [send(product(3, 0).astype(BF16), down)]
+    from_up = [None, send(product(1, 1).astype(BF16), up)]
+    from_up[0] = send((product(1, 0) + by_up.astype(F32)).astype(BF16), up)
+    from_down.append(send((product(3, 1) + by_down.astype(F32)).astype(BF16), down))
+    parts = []
+    for half in range(2):
+        mine = product(0, half)
+        other = mine[own:] + from_up[half][own:].astype(F32) + from_down[half][own:].astype(F32)
+        parts += [mine, from_up[half], from_down[half], send(other.astype(BF16), across)]
+    return parts
 
 
 def gather_ids(ids, share, later):
@@ -359,7 +429,9 @@
     x, y = me // 2, me % 2
     spot = lambda k, other: (x + k) % (size // 2) * 2 + (y + other) % 2
     order = [(0, 0), (3, 0), (1, 0), (2, 0), (0, 1), (3, 1), (1, 1), (2, 1)]
-    return jnp.stack([spot(*o) for o in order]).astype(jnp.int32)
+    order = jnp.stack([spot(*o) for o in order]).astype(jnp.int32)
+    peer = jnp.arange(size, dtype=jnp.int32)
+    return order, (peer // 2 - x) % (size // 2) * 2 + (peer % 2 != y)
 
 
 def share_kernel(subs_ref, w_ref, out_ref, sems):
@@ -464,16 +536,16 @@
     attended = [attended] + first + gather_second(first)
     emb = look_up(ids, 1, spots, codec_table, shift, tensor, text)
     residual = residual.reshape(steps, tensor, per, width)
-    attended, mine, done = collect_rows(attended, peers_order(), residual)
+    order, owner_spots = peers_order()
+    attended, mine, done = collect_rows(attended, order, owner_spots, residual)
     weights, done, emb = lax.optimization_barrier((weights, done, emb))
     emb = lax.all_to_all(emb, BOTH, 0, 0, tiled=True)
     weight = collect_weight(weight_third(weights), subs, done)
     hidden = jnp.dot(attended, weight.reshape(tensor * depth, width), preferred_element_type=F32)
     hidden = (mine.reshape(rows, width).astype(F32) + hidden).astype(BF16)
-    parts = jnp.dot(hidden, bridge_weight, preferred_element_type=F32).astype(BF16)
-    parts = lax.all_to_all(parts.reshape(tensor, steps * per, talk), "tensor", 0, 0, tiled=True)
+    parts = bridge_parts(hidden, bridge_weight)
     talker = finish(parts, place(emb, talk), talk_gain.reshape(1, talk))
-    hidden = hidden.reshape(tensor, steps, per, width).transpose(1, 0, 2, 3)
+    hidden = restore(hidden.reshape(tensor, steps, per, width), owner_spots)
     return hidden.reshape(steps, streams, width), talker.reshape(steps, per, talk)
 
 

time: 187 us -> 165 us (0.88)
  waiting for transfers between devices: 59.4 us -> 32.7 us
  starting transfers between devices: 43.5 us -> 53.3 us
  Pallas kernels: 59.9 us -> 53.9 us
    all_to_all x1 -> x0, waiting for transfers between devices: 46.7 us -> none  [local(): lax.all_to_all(parts.reshape(tensor, steps * per, talk), 'tensor', 0, 0,...]
    ppermute x7 -> x15, waiting for transfers between devices: 7.58 us -> 31.6 us  [send(): return lax.ppermute(x, 'tensor', pairs)]
    ppermute x7 -> x15, starting transfers between devices: 11 us -> 25.4 us  [send(): return lax.ppermute(x, 'tensor', pairs)]
    all_to_all x1 -> x0, starting transfers between devices: 4.49 us -> none  [local(): lax.all_to_all(parts.reshape(tensor, steps * per, talk), 'tensor', 0, 0,...]
    all_to_all x1, waiting for transfers between devices: 3.87 us -> 0.01 us  [local(): emb = lax.all_to_all(emb, BOTH, 0, 0, tiled=True)]
    pallas_call x1, Pallas kernels: 3.78 us -> 0.9 us  [place(): pl.pallas_call(functools.partial(place_kernel, feats=talk // holders), gr...]
    pallas_call x2, Pallas kernels: 31.8 us -> 28.9 us  [look_up(): pl.pallas_call(functools.partial(look_kernel, group=group), in_specs=[sme...]
    pallas_call x2 -> x3, Pallas kernels: 14.2 us -> 12.2 us  [the longest x1 9.29 us: attention(): pl.pallas_call(attention_kernel, grid=(blocks // BLOCKS,), in_specs=[pl.B...]
  transfers between devices with their start and end apart: 20 -> 27, of which waited for: 5 -> 10; matrix products, arithmetic and copies ran while one was open for 7% -> 8% of each run, Pallas kernels for 30% -> 32%
where the time goes in v5:
time: 165 us; the launch traced here: 164 us
  Pallas kernels  53.9 us (33%)
  starting transfers between devices  53.3 us (32%)
  waiting for transfers between devices  32.7 us (20%)
  local copies, waits for them, and re-layouts  10.4 us (6%)
  matrix products  9.82 us (6%)
  other arithmetic  3.07 us (2%)
    ppermute x15, waiting for transfers between devices, send(): return lax.ppermute(x, 'tensor', pairs)  31.6 us
    pallas_call x2, Pallas kernels, look_up(): pl.pallas_call(functools.partial(look_kernel, group=group), in_specs=[sme...  28.9 us
    ppermute x15, starting transfers between devices, send(): return lax.ppermute(x, 'tensor', pairs)  25.4 us
    pallas_call x1, Pallas kernels, attention(): pl.pallas_call(attention_kernel, grid=(blocks // BLOCKS,), in_specs=[pl.B...  9.29 us
    all_to_all x1, starting transfers between devices, local(): emb = lax.all_to_all(emb, BOTH, 0, 0, tiled=True)  8.39 us
    ppermute x5, starting transfers between devices, gather_ids(): lax.ppermute(x, 'dp', [(peer(i), i) for i in range(count)])  8.25 us
    unnamed x42, local copies, waits for them, and re-layouts  7.91 us
    all_to_all x1, starting transfers between devices, local(): share = lax.all_to_all(share, 'tensor', 0, 0, tiled=True)  6.65 us
  transfers between devices with their start and end apart: 27, of which 10 were waited for; matrix products, arithmetic and copies ran while one was open for 8% of the time, Pallas kernels for 32%

profile of v5, /device:TPU:0, one launch (start us, length us, event | category | flops | bytes accessed | tf_op | source)
XLA Modules:
  0.0 164.3 jit_solution(17489544605458549713)
XLA Ops:
  3.6 3.8 %share_rows.1 = bf16[8,2,64,1024]{3,2,1,0:T(8,128)(2,1)} custom-call(s32[2]{0:T(128)} %pad_add_fusion.4.subs_ref, bf16[512,8192]{1,0:T(8,128)(2,1)} %w_ref.1), custom_call_target="tpu_custom_call" | custom-call | bytes 4194304 | tf_op jit(solution)/shard_map/share_rows/pallas_call | solution.py:456
  7.4 6.6 %all-to-all-start = ((bf16[8,2,64,1024]{3,2,1,0:T(8,128)(2,1)}), bf16[8,2,64,1024]{3,2,1,0:T(8,128)(2,1)S(1)}, u32[]{:S(2)}, u32[]{:S(2)}) async-start(bf16[8,2,64,1024]{3,2,1,0:T(8,128)(2,1)} %share_rows.1), calls=%async_computation | async-start | bytes 4194304 | tf_op jit(solution)/shard_map/all_to_all | solution.py:528
  17.2 3.6 %collective-permute-start.3 = (s32[4,8,128]{2,1,0:T(8,128)S(1)}, s32[4,8,128]{2,1,0:T(8,128)S(1)}, u32[]{:S(2)}, u32[]{:S(2)}) collective-permute-start(s32[4,8,128]{2,1,0:T(8,128)S(1)} %pad_add_fusion.1), channel_id=1, source_target_pairs={{32,0},{40,8},{48,16},{56,24},{0,32},{8,40},{16,48},{24,56},{96,64... | collective-permute-start | bytes 49160 | tf_op jit(solution)/shard_map/ppermute | solution.py:392
  22.5 9.3 %attention.1 = bf16[8,4,16,512]{3,2,1,0:T(8,128)(2,1)} custom-call(s32[128,128]{1,0:T(8,128)} %broadcast_in_dim.4.len_ref, bf16[4,128,512]{2,1,0:T(8,128)(2,1)} %q_ref, bf16[128,64,128]{2,1,0:T(8,128)(2,1)} %ck_ref.1, bf16[128,64,128]{2,1,0:T(8,128)(2,1)} %cv_ref.1, bf16[4,128,128]{2,1,0:T(8,128)(2,1)} %nk_ref.1, bf16[4,128,128]{2,1,0:T(8,128)(2,1)} %nv_ref.1), custom_call_target="tpu_custom_call" | custom-call | flops 8000000000 | bytes 6291456 | tf_op jit(solution)/shard_map/attention/pallas_call | solution.py:83
  31.8 3.5 %collective-permute-start.8 = (bf16[512,512]{1,0:T(8,128)(2,1)}, bf16[512,512]{1,0:T(8,128)(2,1)}, u32[]{:S(2)}, u32[]{:S(2)}) collective-permute-start(bf16[512,512]{1,0:T(8,128)(2,1)} %bitcast.37), channel_id=1, source_target_pairs={{0,1},{1,0},{2,3},{3,2},{4,5},{5,4},{6,7},{7,6},{8,9},{9,8},{10,11... | collective-permute-start | bytes 1572872 | tf_op jit(solution)/shard_map/ppermute | solution.py:413
  35.3 3.0 %collective-permute-start.7 = (bf16[512,512]{1,0:T(8,128)(2,1)}, bf16[512,512]{1,0:T(8,128)(2,1)}, u32[]{:S(2)}, u32[]{:S(2)}) collective-permute-start(bf16[512,512]{1,0:T(8,128)(2,1)} %bitcast.38), channel_id=1, source_target_pairs={{0,4},{1,5},{2,6},{3,7},{4,0},{5,1},{6,2},{7,3},{8,12},{9,13},{10,... | collective-permute-start | bytes 1572872 | tf_op jit(solution)/shard_map/ppermute | solution.py:413
  40.4 16.4 %look_up.2.refs_0_ = bf16[128,32,128]{2,1,0:T(8,128)(2,1)S(1)} custom-call(s32[1]{0:T(128)} %bitcast.13.shift_ref, s32[16]{0:T(128)S(1)} %fusion.36.spot_ref, s32[16384]{0:T(1024)S(1)} %bitcast.35, bf16[28,76032]{1,0:T(8,128)(2,1)} %table_ref.2), custom_call_target="tpu_custom_call" | custom-call | bytes 47185920 | tf_op jit(solution)/shard_map/look_up/pallas_call | solution.py:172
  57.4 7.0 %collective-permute-done.6.refs_2_ = bf16[512,512]{1,0:T(8,128)(2,1)} collective-permute-done((bf16[512,512]{1,0:T(8,128)(2,1)}, bf16[512,512]{1,0:T(8,128)(2,1)}, u32[]{:S(2)}, u32[]{:S(2)}) %collective-permute-start.6) | collective-permute-done | bytes 524320 | tf_op jit(solution)/shard_map/ppermute | solution.py:413
  64.4 2.9 %collective-permute-done.5.refs_1_ = bf16[512,512]{1,0:T(8,128)(2,1)} collective-permute-done((bf16[512,512]{1,0:T(8,128)(2,1)}, bf16[512,512]{1,0:T(8,128)(2,1)}, u32[]{:S(2)}, u32[]{:S(2)}) %collective-permute-start.5) | collective-permute-done | bytes 524320 | tf_op jit(solution)/shard_map/ppermute | solution.py:413
  68.8 4.1 %collective-permute-start.13 = (bf16[8,1,64,1024]{3,2,1,0:T(8,128)(2,1)}, bf16[8,1,64,1024]{3,2,1,0:T(8,128)(2,1)}, u32[]{:S(2)}, u32[]{:S(2)}) collective-permute-start(bf16[8,1,64,1024]{3,2,1,0:T(8,128)(2,1)} %get-tuple-element.42), channel_id=1, source_target_pairs={{0,48},{8,56},{16,32},{24,40},{32,16},{40,24},{48,0},{56,8},{64,11... | collective-permute-start | bytes 3145736 | tf_op jit(solution)/shard_map/ppermute | solution.py:489
  76.1 12.5 %look_up.3 = bf16[128,32,128]{2,1,0:T(8,128)(2,1)} custom-call(s32[1]{0:T(128)} %bitcast.13.shift_ref, s32[16]{0:T(128)S(1)} %fusion.36.spot_ref, s32[16384]{0:T(1024)S(1)} %bitcast.36, bf16[28,8448]{1,0:T(8,128)(2,1)S(1)} %copy-done.11, bf16[128,32,128]{2,1,0:T(8,128)(2,1)S(1)} %look_up.2.refs_0_), custom_call_target="tpu_custom_call" | custom-call | bytes 23068672 | tf_op jit(solution)/shard_map/look_up/pallas_call | solution.py:172
  90.8 4.2 %collect_rows.1 = (bf16[512,4096]{1,0:T(8,128)(2,1)S(1)}, bf16[8,4,16,1024]{3,2,1,0:T(8,128)(2,1)S(1)}, f32[8,128]{1,0:T(8,128)S(1)}) custom-call(s32[8]{0:T(128)S(1)} %stack.76.order_ref, s32[8]{0:T(128)S(1)} %fusion.33.spot_ref, bf16[512,512]{1,0:T(8,128)(2,1)S(1)} %bitcast.41, bf16[512,512]{1,0:T(8,128)(2,1)} %collective-permute-done.5.refs_1_, ...), custom_call_target="tpu_custom_call" | custom-call | bytes 8388608 | tf_op jit(solution)/shard_map/collect_rows/pallas_call | solution.py:218
  95.1 2.0 %copy-done.13 = bf16[512,4096]{1,0:T(8,128)(2,1)} copy-done((bf16[512,4096]{1,0:T(8,128)(2,1)}, bf16[512,4096]{1,0:T(8,128)(2,1)S(1)}, u32[]{:S(2)}) %copy-start.13) | copy-done | bytes 4194328
  98.7 8.4 %all-to-all-start.1 = ((bf16[128,32,128]{2,1,0:T(8,128)(2,1)}), bf16[128,32,128]{2,1,0:T(8,128)(2,1)S(1)}, u32[]{:S(2)}, u32[]{:S(2)}) async-start(bf16[128,32,128]{2,1,0:T(8,128)(2,1)} %look_up.3), calls=%async_computation.1 | async-start | bytes 2097152 | tf_op jit(solution)/shard_map/all_to_all | solution.py:542
  107.2 3.9 %collect_weight.1 = bf16[8,8,64,1024]{3,2,1,0:T(8,128)(2,1)S(1)} custom-call(s32[8]{0:T(128)S(1)} %stack.89.subs_ref, f32[8,128]{1,0:T(8,128)S(1)} %get-tuple-element.37.done_ref, bf16[8,2,64,1024]{3,2,1,0:T(8,128)(2,1)S(1)} %all-to-all-done.refs_0_, bf16[8,1,64,1024]{3,2,1,0:T(8,128)(2,1)} %collective-permute-done.12.refs_1_, ...), custom_call_target="tpu_custom_call" | custom-call | bytes 10485760 | tf_op jit(solution)/shard_map/collect_weight/pallas_call | solution.py:281
  111.5 4.5 %fusion.12 = bf16[512,1024]{1,0:T(8,128)(2,1)S(1)} fusion(bf16[8,4,16,1024]{3,2,1,0:T(8,128)(2,1)S(1)} %copy-done.16, bf16[512,4096]{1,0:T(8,128)(2,1)S(1)} %copy-done.14, bf16[4096,1024]{1,0:T(8,128)(2,1)S(1)} %bitcast.32), kind=kOutput, calls=%fused_computation.17 | convolution fusion | flops 4296540160 | bytes 14680064 | tf_op jit(solution)/shard_map/dot_general | solution.py:544
  118.1 2.1 %collective-permute-start.22 = (bf16[128,1792]{1,0:T(8,128)(2,1)S(1)}, bf16[128,1792]{1,0:T(8,128)(2,1)S(1)}, u32[]{:S(2)}, u32[]{:S(2)}) collective-permute-start(bf16[128,1792]{1,0:T(8,128)(2,1)S(1)} %convolution_convert_fusion), channel_id=1, source_target_pairs={{0,6},{1,7},{2,0},{3,1},{4,2},{5,3},{6,4},{7,5},{8,14},{9,15},{10,... | collective-permute-start | bytes 1376264 | tf_op jit(solution)/shard_map/ppermute | solution.py:413
  122.3 7.9 %collective-permute-done.22 = bf16[128,1792]{1,0:T(8,128)(2,1)S(1)} collective-permute-done((bf16[128,1792]{1,0:T(8,128)(2,1)S(1)}, bf16[128,1792]{1,0:T(8,128)(2,1)S(1)}, u32[]{:S(2)}, u32[]{:S(2)}) %collective-permute-start.22) | collective-permute-done | bytes 458784 | tf_op jit(solution)/shard_map/ppermute | solution.py:413
  130.9 3.8 %collective-permute-start.23 = (bf16[128,1792]{1,0:T(8,128)(2,1)S(1)}, bf16[128,1792]{1,0:T(8,128)(2,1)S(1)}, u32[]{:S(2)}, u32[]{:S(2)}) collective-permute-start(bf16[128,1792]{1,0:T(8,128)(2,1)S(1)} %add_convert_fusion), channel_id=1, source_target_pairs={{0,6},{1,7},{2,0},{3,1},{4,2},{5,3},{6,4},{7,5},{8,14},{9,15},{10,... | collective-permute-start | bytes 1376264 | tf_op jit(solution)/shard_map/ppermute | solution.py:413
  136.2 2.0 %collective-permute-start.18 = (bf16[128,1792]{1,0:T(8,128)(2,1)S(1)}, bf16[128,1792]{1,0:T(8,128)(2,1)S(1)}, u32[]{:S(2)}, u32[]{:S(2)}) collective-permute-start(bf16[128,1792]{1,0:T(8,128)(2,1)S(1)} %add_convert_fusion.1), channel_id=1, source_target_pairs={{0,2},{1,3},{2,4},{3,5},{4,6},{5,7},{6,0},{7,1},{8,10},{9,11},{10,... | collective-permute-start | bytes 1376264 | tf_op jit(solution)/shard_map/ppermute | solution.py:413
  138.2 7.1 %collective-permute-done.21.refs_5_ = bf16[128,1792]{1,0:T(8,128)(2,1)S(1)} collective-permute-done((bf16[128,1792]{1,0:T(8,128)(2,1)S(1)}, bf16[128,1792]{1,0:T(8,128)(2,1)S(1)}, u32[]{:S(2)}, u32[]{:S(2)}) %collective-permute-start.21) | collective-permute-done | bytes 458784 | tf_op jit(solution)/shard_map/ppermute | solution.py:413
  146.5 3.0 %collective-permute-start.24 = (bf16[64,1792]{1,0:T(8,128)(2,1)}, bf16[64,1792]{1,0:T(8,128)(2,1)S(1)}, u32[]{:S(2)}, u32[]{:S(2)}) collective-permute-start(bf16[64,1792]{1,0:T(8,128)(2,1)} %fusion.14), channel_id=1, source_target_pairs={{0,1},{1,0},{2,3},{3,2},{4,5},{5,4},{6,7},{7,6},{8,9},{9,8},{10,11... | collective-permute-start | bytes 688136 | tf_op jit(solution)/shard_map/ppermute | solution.py:413
  149.5 4.2 %collective-permute-done.19.refs_2_ = bf16[128,1792]{1,0:T(8,128)(2,1)S(1)} collective-permute-done((bf16[128,1792]{1,0:T(8,128)(2,1)S(1)}, bf16[128,1792]{1,0:T(8,128)(2,1)S(1)}, u32[]{:S(2)}, u32[]{:S(2)}) %collective-permute-start.19) | collective-permute-done | bytes 458784 | tf_op jit(solution)/shard_map/ppermute | solution.py:413
  154.9 3.0 %collective-permute-start.20 = (bf16[64,1792]{1,0:T(8,128)(2,1)}, bf16[64,1792]{1,0:T(8,128)(2,1)S(1)}, u32[]{:S(2)}, u32[]{:S(2)}) collective-permute-start(bf16[64,1792]{1,0:T(8,128)(2,1)} %fusion.16), channel_id=1, source_target_pairs={{0,1},{1,0},{2,3},{3,2},{4,5},{5,4},{6,7},{7,6},{8,9},{9,8},{10,11... | collective-permute-start | bytes 688136 | tf_op jit(solution)/shard_map/ppermute | solution.py:413
  (105 shorter events, 34.5 us)
Async XLA Ops:
  7.4 59.9 %all-to-all-start = ((bf16[8,2,64,1024]{3,2,1,0:T(8,128)(2,1)}), bf16[8,2,64,1024]{3,2,1,0:T(8,128)(2,1)S(1)}, u32[]{:S(2)}, u32[]{:S(2)}) async-start(bf16[8,2,64,1024]{3,2,1,0:T(8,128)(2,1)} %share_rows.1), calls=%async_computation | async-start | bytes 4194304 | tf_op jit(solution)/shard_map/all_to_all | solution.py:528
  15.3 16.5 %collective-permute-start.4 = (s32[4,8,128]{2,1,0:T(8,128)S(1)}, s32[4,8,128]{2,1,0:T(8,128)S(1)}, u32[]{:S(2)}, u32[]{:S(2)}) collective-permute-start(s32[4,8,128]{2,1,0:T(8,128)S(1)} %pad_add_fusion.1), channel_id=1, source_target_pairs={{48,0},{56,8},{0,16},{8,24},{16,32},{24,40},{32,48},{40,56},{112,6... | collective-permute-start | bytes 49160 | tf_op jit(solution)/shard_map/ppermute | solution.py:392
  17.2 14.6 %collective-permute-start.3 = (s32[4,8,128]{2,1,0:T(8,128)S(1)}, s32[4,8,128]{2,1,0:T(8,128)S(1)}, u32[]{:S(2)}, u32[]{:S(2)}) collective-permute-start(s32[4,8,128]{2,1,0:T(8,128)S(1)} %pad_add_fusion.1), channel_id=1, source_target_pairs={{32,0},{40,8},{48,16},{56,24},{0,32},{8,40},{16,48},{24,56},{96,64... | collective-permute-start | bytes 49160 | tf_op jit(solution)/shard_map/ppermute | solution.py:392
  20.8 11.0 %collective-permute-start.2 = (s32[4,8,128]{2,1,0:T(8,128)S(1)}, s32[4,8,128]{2,1,0:T(8,128)S(1)}, u32[]{:S(2)}, u32[]{:S(2)}) collective-permute-start(s32[4,8,128]{2,1,0:T(8,128)S(1)} %pad_add_fusion.1), channel_id=1, source_target_pairs={{16,0},{24,8},{32,16},{40,24},{48,32},{56,40},{0,48},{8,56},{80,64... | collective-permute-start | bytes 49160 | tf_op jit(solution)/shard_map/ppermute | solution.py:392
  31.8 24.9 %collective-permute-start.8 = (bf16[512,512]{1,0:T(8,128)(2,1)}, bf16[512,512]{1,0:T(8,128)(2,1)}, u32[]{:S(2)}, u32[]{:S(2)}) collective-permute-start(bf16[512,512]{1,0:T(8,128)(2,1)} %bitcast.37), channel_id=1, source_target_pairs={{0,1},{1,0},{2,3},{3,2},{4,5},{5,4},{6,7},{7,6},{8,9},{9,8},{10,11... | collective-permute-start | bytes 1572872 | tf_op jit(solution)/shard_map/ppermute | solution.py:413
  35.3 22.0 %collective-permute-start.7 = (bf16[512,512]{1,0:T(8,128)(2,1)}, bf16[512,512]{1,0:T(8,128)(2,1)}, u32[]{:S(2)}, u32[]{:S(2)}) collective-permute-start(bf16[512,512]{1,0:T(8,128)(2,1)} %bitcast.38), channel_id=1, source_target_pairs={{0,4},{1,5},{2,6},{3,7},{4,0},{5,1},{6,2},{7,3},{8,12},{9,13},{10,... | collective-permute-start | bytes 1572872 | tf_op jit(solution)/shard_map/ppermute | solution.py:413
  38.3 26.0 %collective-permute-start.6 = (bf16[512,512]{1,0:T(8,128)(2,1)}, bf16[512,512]{1,0:T(8,128)(2,1)}, u32[]{:S(2)}, u32[]{:S(2)}) collective-permute-start(bf16[512,512]{1,0:T(8,128)(2,1)} %bitcast.39), channel_id=1, source_target_pairs={{0,6},{1,7},{2,0},{3,1},{4,2},{5,3},{6,4},{7,5},{8,14},{9,15},{10,... | collective-permute-start | bytes 1572872 | tf_op jit(solution)/shard_map/ppermute | solution.py:413
  39.5 27.7 %collective-permute-start.5 = (bf16[512,512]{1,0:T(8,128)(2,1)}, bf16[512,512]{1,0:T(8,128)(2,1)}, u32[]{:S(2)}, u32[]{:S(2)}) collective-permute-start(bf16[512,512]{1,0:T(8,128)(2,1)} %bitcast.40), channel_id=1, source_target_pairs={{0,2},{1,3},{2,4},{3,5},{4,6},{5,7},{6,0},{7,1},{8,10},{9,11},{10,... | collective-permute-start | bytes 1572872 | tf_op jit(solution)/shard_map/ppermute | solution.py:413
  68.8 29.2 %collective-permute-start.13 = (bf16[8,1,64,1024]{3,2,1,0:T(8,128)(2,1)}, bf16[8,1,64,1024]{3,2,1,0:T(8,128)(2,1)}, u32[]{:S(2)}, u32[]{:S(2)}) collective-permute-start(bf16[8,1,64,1024]{3,2,1,0:T(8,128)(2,1)} %get-tuple-element.42), channel_id=1, source_target_pairs={{0,48},{8,56},{16,32},{24,40},{32,16},{40,24},{48,0},{56,8},{64,11... | collective-permute-start | bytes 3145736 | tf_op jit(solution)/shard_map/ppermute | solution.py:489
  72.9 25.1 %collective-permute-start.12 = (bf16[8,1,64,1024]{3,2,1,0:T(8,128)(2,1)}, bf16[8,1,64,1024]{3,2,1,0:T(8,128)(2,1)}, u32[]{:S(2)}, u32[]{:S(2)}) collective-permute-start(bf16[8,1,64,1024]{3,2,1,0:T(8,128)(2,1)} %get-tuple-element.43), channel_id=1, source_target_pairs={{0,16},{8,24},{16,0},{24,8},{32,48},{40,56},{48,32},{56,40},{64,80... | collective-permute-start | bytes 3145736 | tf_op jit(solution)/shard_map/ppermute | solution.py:488
  72.9 15.7 %collective-permute-start.11 = (bf16[512,512]{1,0:T(8,128)(2,1)}, bf16[512,512]{1,0:T(8,128)(2,1)}, u32[]{:S(2)}, u32[]{:S(2)}) collective-permute-start(bf16[512,512]{1,0:T(8,128)(2,1)} %collective-permute-done.7.refs_3_), channel_id=1, source_target_pairs={{0,1},{1,0},{2,3},{3,2},{4,5},{5,4},{6,7},{7,6},{8,9},{9,8},{10,11... | collective-permute-start | bytes 1572872 | tf_op jit(solution)/shard_map/ppermute | solution.py:413
  72.9 15.7 %collective-permute-start.10 = (bf16[512,512]{1,0:T(8,128)(2,1)}, bf16[512,512]{1,0:T(8,128)(2,1)}, u32[]{:S(2)}, u32[]{:S(2)}) collective-permute-start(bf16[512,512]{1,0:T(8,128)(2,1)} %collective-permute-done.8.refs_4_), channel_id=1, source_target_pairs={{0,6},{1,7},{2,0},{3,1},{4,2},{5,3},{6,4},{7,5},{8,14},{9,15},{10,... | collective-permute-start | bytes 1572872 | tf_op jit(solution)/shard_map/ppermute | solution.py:413
  74.7 13.8 %collective-permute-start.9 = (bf16[512,512]{1,0:T(8,128)(2,1)}, bf16[512,512]{1,0:T(8,128)(2,1)}, u32[]{:S(2)}, u32[]{:S(2)}) collective-permute-start(bf16[512,512]{1,0:T(8,128)(2,1)} %collective-permute-done.8.refs_4_), channel_id=1, source_target_pairs={{0,2},{1,3},{2,4},{3,5},{4,6},{5,7},{6,0},{7,1},{8,10},{9,11},{10,... | collective-permute-start | bytes 1572872 | tf_op jit(solution)/shard_map/ppermute | solution.py:413
  98.0 9.1 %collective-permute-start.14 = (bf16[8,2,64,1024]{3,2,1,0:T(8,128)(2,1)S(1)}, bf16[8,2,64,1024]{3,2,1,0:T(8,128)(2,1)}, u32[]{:S(2)}, u32[]{:S(2)}) collective-permute-start(bf16[8,2,64,1024]{3,2,1,0:T(8,128)(2,1)S(1)} %all-to-all-done.refs_0_), channel_id=1, source_target_pairs={{0,8},{8,0},{16,24},{24,16},{32,40},{40,32},{48,56},{56,48},{64,72... | collective-permute-start | bytes 6291464 | tf_op jit(solution)/shard_map/ppermute | solution.py:495
  98.0 9.1 %collective-permute-start.15 = (bf16[8,1,64,1024]{3,2,1,0:T(8,128)(2,1)}, bf16[8,1,64,1024]{3,2,1,0:T(8,128)(2,1)}, u32[]{:S(2)}, u32[]{:S(2)}) collective-permute-start(bf16[8,1,64,1024]{3,2,1,0:T(8,128)(2,1)} %collective-permute-done.12.refs_1_), channel_id=1, source_target_pairs={{0,8},{8,0},{16,24},{24,16},{32,40},{40,32},{48,56},{56,48},{64,72... | collective-permute-start | bytes 3145736 | tf_op jit(solution)/shard_map/ppermute | solution.py:495
  98.6 8.6 %collective-permute-start.16 = (bf16[8,1,64,1024]{3,2,1,0:T(8,128)(2,1)}, bf16[8,1,64,1024]{3,2,1,0:T(8,128)(2,1)}, u32[]{:S(2)}, u32[]{:S(2)}) collective-permute-start(bf16[8,1,64,1024]{3,2,1,0:T(8,128)(2,1)} %collective-permute-done.13.refs_2_), channel_id=1, source_target_pairs={{0,8},{8,0},{16,24},{24,16},{32,40},{40,32},{48,56},{56,48},{64,72... | collective-permute-start | bytes 3145736 | tf_op jit(solution)/shard_map/ppermute | solution.py:495
  98.7 59.2 %all-to-all-start.1 = ((bf16[128,32,128]{2,1,0:T(8,128)(2,1)}), bf16[128,32,128]{2,1,0:T(8,128)(2,1)S(1)}, u32[]{:S(2)}, u32[]{:S(2)}) async-start(bf16[128,32,128]{2,1,0:T(8,128)(2,1)} %look_up.3), calls=%async_computation.1 | async-start | bytes 2097152 | tf_op jit(solution)/shard_map/all_to_all | solution.py:542
  118.1 12.2 %collective-permute-start.22 = (bf16[128,1792]{1,0:T(8,128)(2,1)S(1)}, bf16[128,1792]{1,0:T(8,128)(2,1)S(1)}, u32[]{:S(2)}, u32[]{:S(2)}) collective-permute-start(bf16[128,1792]{1,0:T(8,128)(2,1)S(1)} %convolution_convert_fusion), channel_id=1, source_target_pairs={{0,6},{1,7},{2,0},{3,1},{4,2},{5,3},{6,4},{7,5},{8,14},{9,15},{10,... | collective-permute-start | bytes 1376264 | tf_op jit(solution)/shard_map/ppermute | solution.py:413
  120.8 14.7 %collective-permute-start.17 = (bf16[128,1792]{1,0:T(8,128)(2,1)S(1)}, bf16[128,1792]{1,0:T(8,128)(2,1)S(1)}, u32[]{:S(2)}, u32[]{:S(2)}) collective-permute-start(bf16[128,1792]{1,0:T(8,128)(2,1)S(1)} %convolution_convert_fusion.3), channel_id=1, source_target_pairs={{0,2},{1,3},{2,4},{3,5},{4,6},{5,7},{6,0},{7,1},{8,10},{9,11},{10,... | collective-permute-start | bytes 1376264 | tf_op jit(solution)/shard_map/ppermute | solution.py:413
  120.9 24.4 %collective-permute-start.21 = (bf16[128,1792]{1,0:T(8,128)(2,1)S(1)}, bf16[128,1792]{1,0:T(8,128)(2,1)S(1)}, u32[]{:S(2)}, u32[]{:S(2)}) collective-permute-start(bf16[128,1792]{1,0:T(8,128)(2,1)S(1)} %convolution_convert_fusion.1), channel_id=1, source_target_pairs={{0,2},{1,3},{2,4},{3,5},{4,6},{5,7},{6,0},{7,1},{8,10},{9,11},{10,... | collective-permute-start | bytes 1376264 | tf_op jit(solution)/shard_map/ppermute | solution.py:413
  130.9 14.7 %collective-permute-start.23 = (bf16[128,1792]{1,0:T(8,128)(2,1)S(1)}, bf16[128,1792]{1,0:T(8,128)(2,1)S(1)}, u32[]{:S(2)}, u32[]{:S(2)}) collective-permute-start(bf16[128,1792]{1,0:T(8,128)(2,1)S(1)} %add_convert_fusion), channel_id=1, source_target_pairs={{0,6},{1,7},{2,0},{3,1},{4,2},{5,3},{6,4},{7,5},{8,14},{9,15},{10,... | collective-permute-start | bytes 1376264 | tf_op jit(solution)/shard_map/ppermute | solution.py:413
  135.3 18.4 %collective-permute-start.19 = (bf16[128,1792]{1,0:T(8,128)(2,1)S(1)}, bf16[128,1792]{1,0:T(8,128)(2,1)S(1)}, u32[]{:S(2)}, u32[]{:S(2)}) collective-permute-start(bf16[128,1792]{1,0:T(8,128)(2,1)S(1)} %convolution_convert_fusion.2), channel_id=1, source_target_pairs={{0,6},{1,7},{2,0},{3,1},{4,2},{5,3},{6,4},{7,5},{8,14},{9,15},{10,... | collective-permute-start | bytes 1376264 | tf_op jit(solution)/shard_map/ppermute | solution.py:413
  136.2 17.9 %collective-permute-start.18 = (bf16[128,1792]{1,0:T(8,128)(2,1)S(1)}, bf16[128,1792]{1,0:T(8,128)(2,1)S(1)}, u32[]{:S(2)}, u32[]{:S(2)}) collective-permute-start(bf16[128,1792]{1,0:T(8,128)(2,1)S(1)} %add_convert_fusion.1), channel_id=1, source_target_pairs={{0,2},{1,3},{2,4},{3,5},{4,6},{5,7},{6,0},{7,1},{8,10},{9,11},{10,... | collective-permute-start | bytes 1376264 | tf_op jit(solution)/shard_map/ppermute | solution.py:413
  146.5 15.3 %collective-permute-start.24 = (bf16[64,1792]{1,0:T(8,128)(2,1)}, bf16[64,1792]{1,0:T(8,128)(2,1)S(1)}, u32[]{:S(2)}, u32[]{:S(2)}) collective-permute-start(bf16[64,1792]{1,0:T(8,128)(2,1)} %fusion.14), channel_id=1, source_target_pairs={{0,1},{1,0},{2,3},{3,2},{4,5},{5,4},{6,7},{7,6},{8,9},{9,8},{10,11... | collective-permute-start | bytes 688136 | tf_op jit(solution)/shard_map/ppermute | solution.py:413
  (24 other events, 154.7 us)

commit v6 on v5

--- a/solution.py
+++ b/solution.py
@@ -18,6 +18,7 @@
 LANES = 128
 FPAD = 32
 PACK = LANES // FPAD
+UNITS = 8
 BF16 = jnp.bfloat16
 F32 = jnp.float32
 BOTH = ("dp", "tensor")
@@ -123,14 +124,14 @@
             turned[pl.ds(at, LANES), :] = jnp.where(slot == k, packed, 0.0)
 
     def turn_units(i, _):
-        for u in range(4):
-            turn((i * 4 + u) * PACK, PACK)
+        for u in range(UNITS):
+            turn((i * UNITS + u) * PACK, PACK)
         return 0
 
     blocks = entries // LANES
-    loops = blocks // (4 * PACK)
+    loops = blocks // (UNITS * PACK)
     lax.fori_loop(0, loops, turn_units, 0)
-    for first in range(loops * 4 * PACK, blocks, PACK):
+    for first in range(loops * UNITS * PACK, blocks, PACK):
         turn(first, min(PACK, blocks - first))
 
     place = (iota((LANES, LANES), 1) - shift_ref[0]) & (LANES - 1)
@@ -150,7 +151,7 @@
                     found[pl.ds(to + (t * per + s), 1), :] = turned[pl.ds(at, 1), :]
             return 0
 
-        lax.fori_loop(0, batch, find, 0)
+        lax.fori_loop(0, batch, find, 0, unroll=4)
         moved = jnp.dot(found[...].astype(BF16), move, preferred_element_type=F32)
         for j in range(batch):
             a = moved[j * rows : j * rows + rows // 2]
@@ -180,7 +181,7 @@
         ],
         compiler_params=pltpu.CompilerParams(vmem_limit_bytes=(table.shape[1] // 2048 + 14) * MIB),
         cost_estimate=pl.CostEstimate(
-            flops=0, bytes_accessed=(20 + table.shape[1] // 3000) * MIB, transcendentals=0
+            flops=0, bytes_accessed=table.shape[1] // 1000 * MIB, transcendentals=0
         ),
         name="look_up",
     )(shift, spots, ids.reshape(-1), table, *other)
@@ -225,7 +226,7 @@
             jax.ShapeDtypeStruct((8, LANES), F32),
         ],
         scratch_shapes=[pltpu.SemaphoreType.DMA((owners, n)) for n in (owners, STEPS)],
-        compiler_params=pltpu.CompilerParams(vmem_limit_bytes=12 * MIB),
+        compiler_params=pltpu.CompilerParams(vmem_limit_bytes=58 * MIB),
         cost_estimate=pl.CostEstimate(flops=0, bytes_accessed=8 * MIB, transcendentals=0),
         name="collect_rows",
     )(order, spots, *attended, residual)
@@ -531,14 +532,15 @@
     attended, ids = lax.optimization_barrier((attended.reshape(rows, depth), ids))
     first = gather_first(attended)
     text = look_up(ids, 0, spots, text_table, shift, tensor)
-    first, text, share = lax.optimization_barrier((first, text, share))
+    text, share = lax.optimization_barrier((text, share))
     weights = weight_second(share)
+    emb = look_up(ids, 1, spots, codec_table, shift, tensor, text)
+    first, emb = lax.optimization_barrier((first, emb))
     attended = [attended] + first + gather_second(first)
-    emb = look_up(ids, 1, spots, codec_table, shift, tensor, text)
     residual = residual.reshape(steps, tensor, per, width)
     order, owner_spots = peers_order()
     attended, mine, done = collect_rows(attended, order, owner_spots, residual)
-    weights, done, emb = lax.optimization_barrier((weights, done, emb))
+    weights, done = lax.optimization_barrier((weights, done))
     emb = lax.all_to_all(emb, BOTH, 0, 0, tiled=True)
     weight = collect_weight(weight_third(weights), subs, done)
     hidden = jnp.dot(attended, weight.reshape(tensor * depth, width), preferred_element_type=F32)

time: 165 us -> 159 us (0.964)
  local copies, waits for them, and re-layouts: 10.4 us -> 5.47 us
    unnamed x42, local copies, waits for them, and re-layouts: 7.91 us -> 2.44 us
    ppermute x1, starting transfers between devices: 4.08 us -> 0.01 us  [weight_second(): beside_b = lax.ppermute(share[:, 1:], 'dp', pairs_b)]
    pallas_call x2, Pallas kernels: 28.9 us -> 26.1 us  [look_up(): pl.pallas_call(functools.partial(look_kernel, group=group), in_specs=[sme...]
    pallas_call x1, Pallas kernels: 4.22 us -> 6.38 us  [collect_rows(): pl.pallas_call(functools.partial(collect_rows_kernel, owners=owners), in_...]
    ppermute x15, starting transfers between devices: 25.4 us -> 27.4 us  [send(): return lax.ppermute(x, 'tensor', pairs)]
  transfers between devices with their start and end apart: 27 -> 27, of which waited for: 10 -> 9; matrix products, arithmetic and copies ran while one was open for 8% -> 10% of each run, Pallas kernels for 32% -> 33%
where the time goes in v6:
time: 159 us; the launch traced here: 158 us
  Pallas kernels  53.3 us (34%)
  starting transfers between devices  52.3 us (33%)
  waiting for transfers between devices  32.8 us (21%)
  matrix products  9.81 us (6%)
  local copies, waits for them, and re-layouts  5.47 us (3%)
  other arithmetic  3.65 us (2%)
    ppermute x15, waiting for transfers between devices, send(): return lax.ppermute(x, 'tensor', pairs)  31.6 us
    ppermute x15, starting transfers between devices, send(): return lax.ppermute(x, 'tensor', pairs)  27.4 us
    pallas_call x2, Pallas kernels, look_up(): pl.pallas_call(functools.partial(look_kernel, group=group), in_specs=[sme...  26.1 us
    pallas_call x1, Pallas kernels, attention(): pl.pallas_call(attention_kernel, grid=(blocks // BLOCKS,), in_specs=[pl.B...  9.29 us
    all_to_all x1, starting transfers between devices, local(): emb = lax.all_to_all(emb, BOTH, 0, 0, tiled=True)  8.36 us
    ppermute x5, starting transfers between devices, gather_ids(): lax.ppermute(x, 'dp', [(peer(i), i) for i in range(count)])  8.25 us
    all_to_all x1, starting transfers between devices, local(): share = lax.all_to_all(share, 'tensor', 0, 0, tiled=True)  6.65 us
    pallas_call x1, Pallas kernels, collect_rows(): pl.pallas_call(functools.partial(collect_rows_kernel, owners=owners), in_...  6.38 us
  transfers between devices with their start and end apart: 27, of which 9 were waited for; matrix products, arithmetic and copies ran while one was open for 10% of the time, Pallas kernels for 33%

profile of v6, /device:TPU:0, one launch (start us, length us, event | category | flops | bytes accessed | tf_op | source)
XLA Modules:
  0.0 158.4 jit_solution(3191741282122061652)
XLA Ops:
  3.6 3.8 %share_rows.1 = bf16[8,2,64,1024]{3,2,1,0:T(8,128)(2,1)} custom-call(s32[2]{0:T(128)} %pad_add_fusion.4.subs_ref, bf16[512,8192]{1,0:T(8,128)(2,1)} %w_ref.1), custom_call_target="tpu_custom_call" | custom-call | bytes 4194304 | tf_op jit(solution)/shard_map/share_rows/pallas_call | solution.py:457
  7.4 6.6 %all-to-all-start = ((bf16[8,2,64,1024]{3,2,1,0:T(8,128)(2,1)}), bf16[8,2,64,1024]{3,2,1,0:T(8,128)(2,1)S(1)}, u32[]{:S(2)}, u32[]{:S(2)}) async-start(bf16[8,2,64,1024]{3,2,1,0:T(8,128)(2,1)} %share_rows.1), calls=%async_computation | async-start | bytes 4194304 | tf_op jit(solution)/shard_map/all_to_all | solution.py:529
  15.3 1.9 %collective-permute-start.4 = (s32[4,8,128]{2,1,0:T(8,128)S(1)}, s32[4,8,128]{2,1,0:T(8,128)S(1)}, u32[]{:S(2)}, u32[]{:S(2)}) collective-permute-start(s32[4,8,128]{2,1,0:T(8,128)S(1)} %pad_add_fusion.1), channel_id=1, source_target_pairs={{48,0},{56,8},{0,16},{8,24},{16,32},{24,40},{32,48},{40,56},{112,6... | collective-permute-start | bytes 49160 | tf_op jit(solution)/shard_map/ppermute | solution.py:393
  17.2 3.6 %collective-permute-start.3 = (s32[4,8,128]{2,1,0:T(8,128)S(1)}, s32[4,8,128]{2,1,0:T(8,128)S(1)}, u32[]{:S(2)}, u32[]{:S(2)}) collective-permute-start(s32[4,8,128]{2,1,0:T(8,128)S(1)} %pad_add_fusion.1), channel_id=1, source_target_pairs={{32,0},{40,8},{48,16},{56,24},{0,32},{8,40},{16,48},{24,56},{96,64... | collective-permute-start | bytes 49160 | tf_op jit(solution)/shard_map/ppermute | solution.py:393
  22.5 9.3 %attention.1 = bf16[8,4,16,512]{3,2,1,0:T(8,128)(2,1)} custom-call(s32[128,128]{1,0:T(8,128)} %broadcast_in_dim.4.len_ref, bf16[4,128,512]{2,1,0:T(8,128)(2,1)} %q_ref, bf16[128,64,128]{2,1,0:T(8,128)(2,1)} %ck_ref.1, bf16[128,64,128]{2,1,0:T(8,128)(2,1)} %cv_ref.1, bf16[4,128,128]{2,1,0:T(8,128)(2,1)} %nk_ref.1, bf16[4,128,128]{2,1,0:T(8,128)(2,1)} %nv_ref.1), custom_call_target="tpu_custom_call" | custom-call | flops 8000000000 | bytes 6291456 | tf_op jit(solution)/shard_map/attention/pallas_call | solution.py:84
  31.8 3.5 %collective-permute-start.8 = (bf16[512,512]{1,0:T(8,128)(2,1)}, bf16[512,512]{1,0:T(8,128)(2,1)}, u32[]{:S(2)}, u32[]{:S(2)}) collective-permute-start(bf16[512,512]{1,0:T(8,128)(2,1)} %bitcast.38), channel_id=1, source_target_pairs={{0,1},{1,0},{2,3},{3,2},{4,5},{5,4},{6,7},{7,6},{8,9},{9,8},{10,11... | collective-permute-start | bytes 1572872 | tf_op jit(solution)/shard_map/ppermute | solution.py:414
  35.4 3.0 %collective-permute-start.7 = (bf16[512,512]{1,0:T(8,128)(2,1)}, bf16[512,512]{1,0:T(8,128)(2,1)}, u32[]{:S(2)}, u32[]{:S(2)}) collective-permute-start(bf16[512,512]{1,0:T(8,128)(2,1)} %bitcast.39), channel_id=1, source_target_pairs={{0,4},{1,5},{2,6},{3,7},{4,0},{5,1},{6,2},{7,3},{8,12},{9,13},{10,... | collective-permute-start | bytes 1572872 | tf_op jit(solution)/shard_map/ppermute | solution.py:414
  40.4 14.5 %look_up.2.refs_0_ = bf16[128,32,128]{2,1,0:T(8,128)(2,1)S(1)} custom-call(s32[1]{0:T(128)} %bitcast.13.shift_ref, s32[16]{0:T(128)S(1)} %fusion.36.spot_ref, s32[16384]{0:T(1024)S(1)} %bitcast.34, bf16[28,76032]{1,0:T(8,128)(2,1)} %table_ref.2), custom_call_target="tpu_custom_call" | custom-call | bytes 79691776 | tf_op jit(solution)/shard_map/look_up/pallas_call | solution.py:173
  57.6 11.6 %look_up.3 = bf16[128,32,128]{2,1,0:T(8,128)(2,1)} custom-call(s32[1]{0:T(128)} %bitcast.13.shift_ref, s32[16]{0:T(128)S(1)} %fusion.36.spot_ref, s32[16384]{0:T(1024)S(1)} %bitcast.35, bf16[28,8448]{1,0:T(8,128)(2,1)S(1)} %copy-done.10, bf16[128,32,128]{2,1,0:T(8,128)(2,1)S(1)} %look_up.2.refs_0_), custom_call_target="tpu_custom_call" | custom-call | bytes 8388608 | tf_op jit(solution)/shard_map/look_up/pallas_call | solution.py:173
  69.9 2.4 %collective-permute-start.10 = (bf16[512,512]{1,0:T(8,128)(2,1)}, bf16[512,512]{1,0:T(8,128)(2,1)S(1)}, u32[]{:S(2)}, u32[]{:S(2)}) collective-permute-start(bf16[512,512]{1,0:T(8,128)(2,1)} %collective-permute-done.8.refs_4_), channel_id=1, source_target_pairs={{0,6},{1,7},{2,0},{3,1},{4,2},{5,3},{6,4},{7,5},{8,14},{9,15},{10,... | collective-permute-start | bytes 1572872 | tf_op jit(solution)/shard_map/ppermute | solution.py:414
  74.4 8.4 %collective-permute-done.11.refs_7_ = bf16[512,512]{1,0:T(8,128)(2,1)S(1)} collective-permute-done((bf16[512,512]{1,0:T(8,128)(2,1)}, bf16[512,512]{1,0:T(8,128)(2,1)S(1)}, u32[]{:S(2)}, u32[]{:S(2)}) %collective-permute-start.11) | collective-permute-done | bytes 524320 | tf_op jit(solution)/shard_map/ppermute | solution.py:414
  82.8 2.2 %collective-permute-done.9.refs_5_ = bf16[512,512]{1,0:T(8,128)(2,1)} collective-permute-done((bf16[512,512]{1,0:T(8,128)(2,1)}, bf16[512,512]{1,0:T(8,128)(2,1)}, u32[]{:S(2)}, u32[]{:S(2)}) %collective-permute-start.9) | collective-permute-done | bytes 524320 | tf_op jit(solution)/shard_map/ppermute | solution.py:414
  85.0 6.4 %collect_rows.1 = (bf16[512,4096]{1,0:T(8,128)(2,1)}, bf16[8,4,16,1024]{3,2,1,0:T(8,128)(2,1)}, f32[8,128]{1,0:T(8,128)}) custom-call(s32[8]{0:T(128)} %stack.76.order_ref, s32[8]{0:T(128)} %fusion.33.spot_ref, bf16[512,512]{1,0:T(8,128)(2,1)} %bitcast.42, bf16[512,512]{1,0:T(8,128)(2,1)} %collective-permute-done.5.refs_1_, ...), custom_call_target="tpu_custom_call" | custom-call | bytes 8388608 | tf_op jit(solution)/shard_map/collect_rows/pallas_call | solution.py:219
  92.2 8.4 %all-to-all-start.1 = ((bf16[128,32,128]{2,1,0:T(8,128)(2,1)}), bf16[128,32,128]{2,1,0:T(8,128)(2,1)S(1)}, u32[]{:S(2)}, u32[]{:S(2)}) async-start(bf16[128,32,128]{2,1,0:T(8,128)(2,1)} %look_up.3), calls=%async_computation.1 | async-start | bytes 2097152 | tf_op jit(solution)/shard_map/all_to_all | solution.py:544
  101.2 3.9 %collect_weight.1 = bf16[8,8,64,1024]{3,2,1,0:T(8,128)(2,1)S(1)} custom-call(s32[8]{0:T(128)S(1)} %stack.89.subs_ref, f32[8,128]{1,0:T(8,128)S(1)} %copy-done.11, bf16[8,2,64,1024]{3,2,1,0:T(8,128)(2,1)S(1)} %all-to-all-done.refs_0_, bf16[8,1,64,1024]{3,2,1,0:T(8,128)(2,1)} %collective-permute-done.12.refs_1_, ...), custom_call_target="tpu_custom_call" | custom-call | bytes 10485760 | tf_op jit(solution)/shard_map/collect_weight/pallas_call | solution.py:282
  105.6 4.5 %fusion.12 = bf16[512,1024]{1,0:T(8,128)(2,1)S(1)} fusion(bf16[8,4,16,1024]{3,2,1,0:T(8,128)(2,1)S(1)} %copy-done.18, bf16[512,4096]{1,0:T(8,128)(2,1)S(1)} %copy-done.17, bf16[4096,1024]{1,0:T(8,128)(2,1)S(1)} %bitcast.32), kind=kOutput, calls=%fused_computation.17 | convolution fusion | flops 4296540160 | bytes 14680064 | tf_op jit(solution)/shard_map/dot_general | solution.py:546
  112.2 2.1 %collective-permute-start.22 = (bf16[128,1792]{1,0:T(8,128)(2,1)S(1)}, bf16[128,1792]{1,0:T(8,128)(2,1)S(1)}, u32[]{:S(2)}, u32[]{:S(2)}) collective-permute-start(bf16[128,1792]{1,0:T(8,128)(2,1)S(1)} %convolution_convert_fusion), channel_id=1, source_target_pairs={{0,6},{1,7},{2,0},{3,1},{4,2},{5,3},{6,4},{7,5},{8,14},{9,15},{10,... | collective-permute-start | bytes 1376264 | tf_op jit(solution)/shard_map/ppermute | solution.py:414
  116.5 7.9 %collective-permute-done.22 = bf16[128,1792]{1,0:T(8,128)(2,1)S(1)} collective-permute-done((bf16[128,1792]{1,0:T(8,128)(2,1)S(1)}, bf16[128,1792]{1,0:T(8,128)(2,1)S(1)}, u32[]{:S(2)}, u32[]{:S(2)}) %collective-permute-start.22) | collective-permute-done | bytes 458784 | tf_op jit(solution)/shard_map/ppermute | solution.py:414
  125.0 3.8 %collective-permute-start.23 = (bf16[128,1792]{1,0:T(8,128)(2,1)S(1)}, bf16[128,1792]{1,0:T(8,128)(2,1)S(1)}, u32[]{:S(2)}, u32[]{:S(2)}) collective-permute-start(bf16[128,1792]{1,0:T(8,128)(2,1)S(1)} %add_convert_fusion), channel_id=1, source_target_pairs={{0,6},{1,7},{2,0},{3,1},{4,2},{5,3},{6,4},{7,5},{8,14},{9,15},{10,... | collective-permute-start | bytes 1376264 | tf_op jit(solution)/shard_map/ppermute | solution.py:414
  130.3 2.0 %collective-permute-start.18 = (bf16[128,1792]{1,0:T(8,128)(2,1)S(1)}, bf16[128,1792]{1,0:T(8,128)(2,1)S(1)}, u32[]{:S(2)}, u32[]{:S(2)}) collective-permute-start(bf16[128,1792]{1,0:T(8,128)(2,1)S(1)} %add_convert_fusion.1), channel_id=1, source_target_pairs={{0,2},{1,3},{2,4},{3,5},{4,6},{5,7},{6,0},{7,1},{8,10},{9,11},{10,... | collective-permute-start | bytes 1376264 | tf_op jit(solution)/shard_map/ppermute | solution.py:414
  132.3 7.1 %collective-permute-done.21.refs_5_ = bf16[128,1792]{1,0:T(8,128)(2,1)S(1)} collective-permute-done((bf16[128,1792]{1,0:T(8,128)(2,1)S(1)}, bf16[128,1792]{1,0:T(8,128)(2,1)S(1)}, u32[]{:S(2)}, u32[]{:S(2)}) %collective-permute-start.21) | collective-permute-done | bytes 458784 | tf_op jit(solution)/shard_map/ppermute | solution.py:414
  140.7 3.0 %collective-permute-start.24 = (bf16[64,1792]{1,0:T(8,128)(2,1)}, bf16[64,1792]{1,0:T(8,128)(2,1)S(1)}, u32[]{:S(2)}, u32[]{:S(2)}) collective-permute-start(bf16[64,1792]{1,0:T(8,128)(2,1)} %fusion.14), channel_id=1, source_target_pairs={{0,1},{1,0},{2,3},{3,2},{4,5},{5,4},{6,7},{7,6},{8,9},{9,8},{10,11... | collective-permute-start | bytes 688136 | tf_op jit(solution)/shard_map/ppermute | solution.py:414
  143.7 4.2 %collective-permute-done.19.refs_2_ = bf16[128,1792]{1,0:T(8,128)(2,1)S(1)} collective-permute-done((bf16[128,1792]{1,0:T(8,128)(2,1)S(1)}, bf16[128,1792]{1,0:T(8,128)(2,1)S(1)}, u32[]{:S(2)}, u32[]{:S(2)}) %collective-permute-start.19) | collective-permute-done | bytes 458784 | tf_op jit(solution)/shard_map/ppermute | solution.py:414
  149.0 3.0 %collective-permute-start.20 = (bf16[64,1792]{1,0:T(8,128)(2,1)}, bf16[64,1792]{1,0:T(8,128)(2,1)S(1)}, u32[]{:S(2)}, u32[]{:S(2)}) collective-permute-start(bf16[64,1792]{1,0:T(8,128)(2,1)} %fusion.16), channel_id=1, source_target_pairs={{0,1},{1,0},{2,3},{3,2},{4,5},{5,4},{6,7},{7,6},{8,9},{9,8},{10,11... | collective-permute-start | bytes 688136 | tf_op jit(solution)/shard_map/ppermute | solution.py:414
  (105 shorter events, 30.2 us)
Async XLA Ops:
  7.4 47.6 %all-to-all-start = ((bf16[8,2,64,1024]{3,2,1,0:T(8,128)(2,1)}), bf16[8,2,64,1024]{3,2,1,0:T(8,128)(2,1)S(1)}, u32[]{:S(2)}, u32[]{:S(2)}) async-start(bf16[8,2,64,1024]{3,2,1,0:T(8,128)(2,1)} %share_rows.1), calls=%async_computation | async-start | bytes 4194304 | tf_op jit(solution)/shard_map/all_to_all | solution.py:529
  15.3 16.5 %collective-permute-start.4 = (s32[4,8,128]{2,1,0:T(8,128)S(1)}, s32[4,8,128]{2,1,0:T(8,128)S(1)}, u32[]{:S(2)}, u32[]{:S(2)}) collective-permute-start(s32[4,8,128]{2,1,0:T(8,128)S(1)} %pad_add_fusion.1), channel_id=1, source_target_pairs={{48,0},{56,8},{0,16},{8,24},{16,32},{24,40},{32,48},{40,56},{112,6... | collective-permute-start | bytes 49160 | tf_op jit(solution)/shard_map/ppermute | solution.py:393
  17.2 14.6 %collective-permute-start.3 = (s32[4,8,128]{2,1,0:T(8,128)S(1)}, s32[4,8,128]{2,1,0:T(8,128)S(1)}, u32[]{:S(2)}, u32[]{:S(2)}) collective-permute-start(s32[4,8,128]{2,1,0:T(8,128)S(1)} %pad_add_fusion.1), channel_id=1, source_target_pairs={{32,0},{40,8},{48,16},{56,24},{0,32},{8,40},{16,48},{24,56},{96,64... | collective-permute-start | bytes 49160 | tf_op jit(solution)/shard_map/ppermute | solution.py:393
  20.8 11.0 %collective-permute-start.2 = (s32[4,8,128]{2,1,0:T(8,128)S(1)}, s32[4,8,128]{2,1,0:T(8,128)S(1)}, u32[]{:S(2)}, u32[]{:S(2)}) collective-permute-start(s32[4,8,128]{2,1,0:T(8,128)S(1)} %pad_add_fusion.1), channel_id=1, source_target_pairs={{16,0},{24,8},{32,16},{40,24},{48,32},{56,40},{0,48},{8,56},{80,64... | collective-permute-start | bytes 49160 | tf_op jit(solution)/shard_map/ppermute | solution.py:393
  31.8 24.8 %collective-permute-start.8 = (bf16[512,512]{1,0:T(8,128)(2,1)}, bf16[512,512]{1,0:T(8,128)(2,1)}, u32[]{:S(2)}, u32[]{:S(2)}) collective-permute-start(bf16[512,512]{1,0:T(8,128)(2,1)} %bitcast.38), channel_id=1, source_target_pairs={{0,1},{1,0},{2,3},{3,2},{4,5},{5,4},{6,7},{7,6},{8,9},{9,8},{10,11... | collective-permute-start | bytes 1572872 | tf_op jit(solution)/shard_map/ppermute | solution.py:414
  35.4 33.9 %collective-permute-start.7 = (bf16[512,512]{1,0:T(8,128)(2,1)}, bf16[512,512]{1,0:T(8,128)(2,1)}, u32[]{:S(2)}, u32[]{:S(2)}) collective-permute-start(bf16[512,512]{1,0:T(8,128)(2,1)} %bitcast.39), channel_id=1, source_target_pairs={{0,4},{1,5},{2,6},{3,7},{4,0},{5,1},{6,2},{7,3},{8,12},{9,13},{10,... | collective-permute-start | bytes 1572872 | tf_op jit(solution)/shard_map/ppermute | solution.py:414
  38.4 30.8 %collective-permute-start.6 = (bf16[512,512]{1,0:T(8,128)(2,1)}, bf16[512,512]{1,0:T(8,128)(2,1)}, u32[]{:S(2)}, u32[]{:S(2)}) collective-permute-start(bf16[512,512]{1,0:T(8,128)(2,1)} %bitcast.40), channel_id=1, source_target_pairs={{0,6},{1,7},{2,0},{3,1},{4,2},{5,3},{6,4},{7,5},{8,14},{9,15},{10,... | collective-permute-start | bytes 1572872 | tf_op jit(solution)/shard_map/ppermute | solution.py:414
  39.6 29.7 %collective-permute-start.5 = (bf16[512,512]{1,0:T(8,128)(2,1)}, bf16[512,512]{1,0:T(8,128)(2,1)}, u32[]{:S(2)}, u32[]{:S(2)}) collective-permute-start(bf16[512,512]{1,0:T(8,128)(2,1)} %bitcast.41), channel_id=1, source_target_pairs={{0,2},{1,3},{2,4},{3,5},{4,6},{5,7},{6,0},{7,1},{8,10},{9,11},{10,... | collective-permute-start | bytes 1572872 | tf_op jit(solution)/shard_map/ppermute | solution.py:414
  56.6 34.8 %collective-permute-start.13 = (bf16[8,1,64,1024]{3,2,1,0:T(8,128)(2,1)}, bf16[8,1,64,1024]{3,2,1,0:T(8,128)(2,1)}, u32[]{:S(2)}, u32[]{:S(2)}) collective-permute-start(bf16[8,1,64,1024]{3,2,1,0:T(8,128)(2,1)} %get-tuple-element.42), channel_id=1, source_target_pairs={{0,48},{8,56},{16,32},{24,40},{32,16},{40,24},{48,0},{56,8},{64,11... | collective-permute-start | bytes 3145736 | tf_op jit(solution)/shard_map/ppermute | solution.py:490
  56.6 34.8 %collective-permute-start.12 = (bf16[8,1,64,1024]{3,2,1,0:T(8,128)(2,1)}, bf16[8,1,64,1024]{3,2,1,0:T(8,128)(2,1)}, u32[]{:S(2)}, u32[]{:S(2)}) collective-permute-start(bf16[8,1,64,1024]{3,2,1,0:T(8,128)(2,1)} %get-tuple-element.43), channel_id=1, source_target_pairs={{0,16},{8,24},{16,0},{24,8},{32,48},{40,56},{48,32},{56,40},{64,80... | collective-permute-start | bytes 3145736 | tf_op jit(solution)/shard_map/ppermute | solution.py:489
  69.2 13.6 %collective-permute-start.11 = (bf16[512,512]{1,0:T(8,128)(2,1)}, bf16[512,512]{1,0:T(8,128)(2,1)S(1)}, u32[]{:S(2)}, u32[]{:S(2)}) collective-permute-start(bf16[512,512]{1,0:T(8,128)(2,1)} %collective-permute-done.7.refs_3_), channel_id=1, source_target_pairs={{0,1},{1,0},{2,3},{3,2},{4,5},{5,4},{6,7},{7,6},{8,9},{9,8},{10,11... | collective-permute-start | bytes 1572872 | tf_op jit(solution)/shard_map/ppermute | solution.py:414
  69.9 12.9 %collective-permute-start.10 = (bf16[512,512]{1,0:T(8,128)(2,1)}, bf16[512,512]{1,0:T(8,128)(2,1)S(1)}, u32[]{:S(2)}, u32[]{:S(2)}) collective-permute-start(bf16[512,512]{1,0:T(8,128)(2,1)} %collective-permute-done.8.refs_4_), channel_id=1, source_target_pairs={{0,6},{1,7},{2,0},{3,1},{4,2},{5,3},{6,4},{7,5},{8,14},{9,15},{10,... | collective-permute-start | bytes 1572872 | tf_op jit(solution)/shard_map/ppermute | solution.py:414
  72.3 12.7 %collective-permute-start.9 = (bf16[512,512]{1,0:T(8,128)(2,1)}, bf16[512,512]{1,0:T(8,128)(2,1)}, u32[]{:S(2)}, u32[]{:S(2)}) collective-permute-start(bf16[512,512]{1,0:T(8,128)(2,1)} %collective-permute-done.8.refs_4_), channel_id=1, source_target_pairs={{0,2},{1,3},{2,4},{3,5},{4,6},{5,7},{6,0},{7,1},{8,10},{9,11},{10,... | collective-permute-start | bytes 1572872 | tf_op jit(solution)/shard_map/ppermute | solution.py:414
  91.4 9.2 %collective-permute-start.14 = (bf16[8,2,64,1024]{3,2,1,0:T(8,128)(2,1)S(1)}, bf16[8,2,64,1024]{3,2,1,0:T(8,128)(2,1)}, u32[]{:S(2)}, u32[]{:S(2)}) collective-permute-start(bf16[8,2,64,1024]{3,2,1,0:T(8,128)(2,1)S(1)} %all-to-all-done.refs_0_), channel_id=1, source_target_pairs={{0,8},{8,0},{16,24},{24,16},{32,40},{40,32},{48,56},{56,48},{64,72... | collective-permute-start | bytes 6291464 | tf_op jit(solution)/shard_map/ppermute | solution.py:496
  91.5 9.0 %collective-permute-start.15 = (bf16[8,1,64,1024]{3,2,1,0:T(8,128)(2,1)}, bf16[8,1,64,1024]{3,2,1,0:T(8,128)(2,1)}, u32[]{:S(2)}, u32[]{:S(2)}) collective-permute-start(bf16[8,1,64,1024]{3,2,1,0:T(8,128)(2,1)} %collective-permute-done.12.refs_1_), channel_id=1, source_target_pairs={{0,8},{8,0},{16,24},{24,16},{32,40},{40,32},{48,56},{56,48},{64,72... | collective-permute-start | bytes 3145736 | tf_op jit(solution)/shard_map/ppermute | solution.py:496
  92.0 8.6 %collective-permute-start.16 = (bf16[8,1,64,1024]{3,2,1,0:T(8,128)(2,1)}, bf16[8,1,64,1024]{3,2,1,0:T(8,128)(2,1)}, u32[]{:S(2)}, u32[]{:S(2)}) collective-permute-start(bf16[8,1,64,1024]{3,2,1,0:T(8,128)(2,1)} %collective-permute-done.13.refs_2_), channel_id=1, source_target_pairs={{0,8},{8,0},{16,24},{24,16},{32,40},{40,32},{48,56},{56,48},{64,72... | collective-permute-start | bytes 3145736 | tf_op jit(solution)/shard_map/ppermute | solution.py:496
  92.2 59.9 %all-to-all-start.1 = ((bf16[128,32,128]{2,1,0:T(8,128)(2,1)}), bf16[128,32,128]{2,1,0:T(8,128)(2,1)S(1)}, u32[]{:S(2)}, u32[]{:S(2)}) async-start(bf16[128,32,128]{2,1,0:T(8,128)(2,1)} %look_up.3), calls=%async_computation.1 | async-start | bytes 2097152 | tf_op jit(solution)/shard_map/all_to_all | solution.py:544
  112.2 12.2 %collective-permute-start.22 = (bf16[128,1792]{1,0:T(8,128)(2,1)S(1)}, bf16[128,1792]{1,0:T(8,128)(2,1)S(1)}, u32[]{:S(2)}, u32[]{:S(2)}) collective-permute-start(bf16[128,1792]{1,0:T(8,128)(2,1)S(1)} %convolution_convert_fusion), channel_id=1, source_target_pairs={{0,6},{1,7},{2,0},{3,1},{4,2},{5,3},{6,4},{7,5},{8,14},{9,15},{10,... | collective-permute-start | bytes 1376264 | tf_op jit(solution)/shard_map/ppermute | solution.py:414
  114.9 14.7 %collective-permute-start.17 = (bf16[128,1792]{1,0:T(8,128)(2,1)S(1)}, bf16[128,1792]{1,0:T(8,128)(2,1)S(1)}, u32[]{:S(2)}, u32[]{:S(2)}) collective-permute-start(bf16[128,1792]{1,0:T(8,128)(2,1)S(1)} %convolution_convert_fusion.3), channel_id=1, source_target_pairs={{0,2},{1,3},{2,4},{3,5},{4,6},{5,7},{6,0},{7,1},{8,10},{9,11},{10,... | collective-permute-start | bytes 1376264 | tf_op jit(solution)/shard_map/ppermute | solution.py:414
  115.0 24.4 %collective-permute-start.21 = (bf16[128,1792]{1,0:T(8,128)(2,1)S(1)}, bf16[128,1792]{1,0:T(8,128)(2,1)S(1)}, u32[]{:S(2)}, u32[]{:S(2)}) collective-permute-start(bf16[128,1792]{1,0:T(8,128)(2,1)S(1)} %convolution_convert_fusion.1), channel_id=1, source_target_pairs={{0,2},{1,3},{2,4},{3,5},{4,6},{5,7},{6,0},{7,1},{8,10},{9,11},{10,... | collective-permute-start | bytes 1376264 | tf_op jit(solution)/shard_map/ppermute | solution.py:414
  125.0 14.7 %collective-permute-start.23 = (bf16[128,1792]{1,0:T(8,128)(2,1)S(1)}, bf16[128,1792]{1,0:T(8,128)(2,1)S(1)}, u32[]{:S(2)}, u32[]{:S(2)}) collective-permute-start(bf16[128,1792]{1,0:T(8,128)(2,1)S(1)} %add_convert_fusion), channel_id=1, source_target_pairs={{0,6},{1,7},{2,0},{3,1},{4,2},{5,3},{6,4},{7,5},{8,14},{9,15},{10,... | collective-permute-start | bytes 1376264 | tf_op jit(solution)/shard_map/ppermute | solution.py:414
  129.5 18.4 %collective-permute-start.19 = (bf16[128,1792]{1,0:T(8,128)(2,1)S(1)}, bf16[128,1792]{1,0:T(8,128)(2,1)S(1)}, u32[]{:S(2)}, u32[]{:S(2)}) collective-permute-start(bf16[128,1792]{1,0:T(8,128)(2,1)S(1)} %convolution_convert_fusion.2), channel_id=1, source_target_pairs={{0,6},{1,7},{2,0},{3,1},{4,2},{5,3},{6,4},{7,5},{8,14},{9,15},{10,... | collective-permute-start | bytes 1376264 | tf_op jit(solution)/shard_map/ppermute | solution.py:414
  130.3 17.9 %collective-permute-start.18 = (bf16[128,1792]{1,0:T(8,128)(2,1)S(1)}, bf16[128,1792]{1,0:T(8,128)(2,1)S(1)}, u32[]{:S(2)}, u32[]{:S(2)}) collective-permute-start(bf16[128,1792]{1,0:T(8,128)(2,1)S(1)} %add_convert_fusion.1), channel_id=1, source_target_pairs={{0,2},{1,3},{2,4},{3,5},{4,6},{5,7},{6,0},{7,1},{8,10},{9,11},{10,... | collective-permute-start | bytes 1376264 | tf_op jit(solution)/shard_map/ppermute | solution.py:414
  140.7 15.4 %collective-permute-start.24 = (bf16[64,1792]{1,0:T(8,128)(2,1)}, bf16[64,1792]{1,0:T(8,128)(2,1)S(1)}, u32[]{:S(2)}, u32[]{:S(2)}) collective-permute-start(bf16[64,1792]{1,0:T(8,128)(2,1)} %fusion.14), channel_id=1, source_target_pairs={{0,1},{1,0},{2,3},{3,2},{4,5},{5,4},{6,7},{7,6},{8,9},{9,8},{10,11... | collective-permute-start | bytes 688136 | tf_op jit(solution)/shard_map/ppermute | solution.py:414
  (24 other events, 179.7 us)

commit v7 on v6

--- a/solution.py
+++ b/solution.py
@@ -100,27 +100,26 @@
     )(lengths, query, cache_keys, cache_values, new_keys, new_values)
 
 
-def look_kernel(shift_ref, spot_ref, id_ref, table_ref, *refs, group):
+def look_kernel(shift_ref, spot_ref, id_ref, table_ref, *refs, group, first, count):
     other_ref = refs[0] if len(refs) == 4 else None
     out_ref, turned, found = refs[-3:]
     feats, entries = table_ref.shape
-    owners = out_ref.shape[0]
     rows = 2 * out_ref.shape[1]
     per = rows // STEPS
     batch = found.shape[0] // rows
     pad = jnp.zeros((FPAD - feats, LANES), BF16)
     slot = iota((LANES, LANES), 1) // FPAD
 
-    def turn(first, count):
+    def turn(begin, amount):
         parts = []
-        for k in range(count):
-            at = pl.multiple_of((first + k) * LANES, LANES)
+        for k in range(amount):
+            at = pl.multiple_of((begin + k) * LANES, LANES)
             parts += [table_ref[:, pl.ds(at, LANES)], pad]
-        if count < PACK:
-            parts.append(jnp.zeros(((PACK - count) * FPAD, LANES), BF16))
+        if amount < PACK:
+            parts.append(jnp.zeros(((PACK - amount) * FPAD, LANES), BF16))
         packed = jnp.concatenate(parts, axis=0).T.astype(F32)
-        for k in range(count):
-            at = pl.multiple_of((first + k) * LANES, LANES)
+        for k in range(amount):
+            at = pl.multiple_of((begin + k) * LANES, LANES)
             turned[pl.ds(at, LANES), :] = jnp.where(slot == k, packed, 0.0)
 
     def turn_units(i, _):
@@ -131,8 +130,8 @@
     blocks = entries // LANES
     loops = blocks // (UNITS * PACK)
     lax.fori_loop(0, loops, turn_units, 0)
-    for first in range(loops * UNITS * PACK, blocks, PACK):
-        turn(first, min(PACK, blocks - first))
+    for begin in range(loops * UNITS * PACK, blocks, PACK):
+        turn(begin, min(PACK, blocks - begin))
 
     place = (iota((LANES, LANES), 1) - shift_ref[0]) & (LANES - 1)
     row = iota((LANES, LANES), 0)
@@ -142,7 +141,7 @@
 
     def look(i, _):
         def find(j, _):
-            o = i * batch + j
+            o = first + i * batch + j
             base = spot_ref[o // (LANES // per)] + o % (LANES // per) * per
             to = pl.multiple_of(j * rows, rows)
             for t in range(STEPS):
@@ -157,21 +156,25 @@
             a = moved[j * rows : j * rows + rows // 2]
             b = moved[j * rows + rows // 2 : (j + 1) * rows]
             both = jnp.where(place < 2 * FPAD, a, b)
+            o = first + i * batch + j
             if other_ref is not None:
-                both = both + other_ref[i * batch + j].astype(F32)
-            out_ref[i * batch + j] = both.astype(BF16)
+                both = both + other_ref[o].astype(F32)
+            out_ref[o] = both.astype(BF16)
         return 0
 
-    lax.fori_loop(0, owners // batch, look, 0)
-
-
-def look_up(ids, group, spots, table, shift, owners, *other):
+    lax.fori_loop(0, count // batch, look, 0)
+    for start, stop in ((0, first), (first + count, out_ref.shape[0])):
+        if start < stop:
+            out_ref[start:stop] = other_ref[start:stop]
+
+
+def look_up(ids, group, spots, table, shift, owners, first, count, *other):
     groups, _, streams = ids.shape
     rows = streams * STEPS // owners
     vmem = pl.BlockSpec(memory_space=pltpu.VMEM)
     smem = pl.BlockSpec(memory_space=pltpu.SMEM)
     return pl.pallas_call(
-        functools.partial(look_kernel, group=group),
+        functools.partial(look_kernel, group=group, first=first, count=count),
         in_specs=[smem, smem, smem, vmem] + [vmem] * len(other),
         out_specs=vmem,
         out_shape=jax.ShapeDtypeStruct((groups * owners, rows // 2, LANES), BF16),
@@ -531,16 +534,18 @@
     attended = attention(query, new_keys, new_values, cache_keys, cache_values, cache_lengths)
     attended, ids = lax.optimization_barrier((attended.reshape(rows, depth), ids))
     first = gather_first(attended)
-    text = look_up(ids, 0, spots, text_table, shift, tensor)
+    text = look_up(ids, 0, spots, text_table, shift, tensor, 0, dp * tensor)
     text, share = lax.optimization_barrier((text, share))
     weights = weight_second(share)
-    emb = look_up(ids, 1, spots, codec_table, shift, tensor, text)
+    half = dp * tensor // 2
+    emb = look_up(ids, 1, spots, codec_table, shift, tensor, 0, half, text)
     first, emb = lax.optimization_barrier((first, emb))
     attended = [attended] + first + gather_second(first)
+    emb = look_up(ids, 1, spots, codec_table, shift, tensor, half, half, emb)
     residual = residual.reshape(steps, tensor, per, width)
     order, owner_spots = peers_order()
     attended, mine, done = collect_rows(attended, order, owner_spots, residual)
-    weights, done = lax.optimization_barrier((weights, done))
+    weights, done, emb = lax.optimization_barrier((weights, done, emb))
     emb = lax.all_to_all(emb, BOTH, 0, 0, tiled=True)
     weight = collect_weight(weight_third(weights), subs, done)
     hidden = jnp.dot(attended, weight.reshape(tensor * depth, width), preferred_element_type=F32)

time: 159 us -> 158 us (level)
  waiting for transfers between devices: 32.8 us -> 26.7 us
  local copies, waits for them, and re-layouts: 5.47 us -> 9.33 us
  Pallas kernels: 53.3 us -> 55.4 us
    ppermute x15, waiting for transfers between devices: 31.6 us -> 25.5 us  [send(): return lax.ppermute(x, 'tensor', pairs)]
    unnamed x42 -> x46, local copies, waits for them, and re-layouts: 2.44 us -> 6.29 us
    pallas_call x2 -> x3, Pallas kernels: 26.1 us -> 28.3 us  [look_up(): pl.pallas_call(functools.partial(look_kernel, group=group, first=first, c...]
  transfers between devices with their start and end apart: 27 -> 27, of which waited for: 9 -> 10; matrix products, arithmetic and copies ran while one was open for 10% -> 10% of each run, Pallas kernels for 33% -> 35%
where the time goes in v7:
time: 158 us; the launch traced here: 157 us
  Pallas kernels  55.4 us (35%)
  starting transfers between devices  51.1 us (32%)
  waiting for transfers between devices  26.7 us (17%)
  matrix products  9.81 us (6%)
  local copies, waits for them, and re-layouts  9.33 us (6%)
  other arithmetic  3.55 us (2%)
    pallas_call x3, Pallas kernels, look_up(): pl.pallas_call(functools.partial(look_kernel, group=group, first=first, c...  28.3 us
    ppermute x15, starting transfers between devices, send(): return lax.ppermute(x, 'tensor', pairs)  26.8 us
    ppermute x15, waiting for transfers between devices, send(): return lax.ppermute(x, 'tensor', pairs)  25.5 us
    pallas_call x1, Pallas kernels, attention(): pl.pallas_call(attention_kernel, grid=(blocks // BLOCKS,), in_specs=[pl.B...  9.3 us
    ppermute x5, starting transfers between devices, gather_ids(): lax.ppermute(x, 'dp', [(peer(i), i) for i in range(count)])  8.25 us
    all_to_all x1, starting transfers between devices, local(): emb = lax.all_to_all(emb, BOTH, 0, 0, tiled=True)  7.69 us
    all_to_all x1, starting transfers between devices, local(): share = lax.all_to_all(share, 'tensor', 0, 0, tiled=True)  6.65 us
    pallas_call x1, Pallas kernels, collect_rows(): pl.pallas_call(functools.partial(collect_rows_kernel, owners=owners), in_...  6.37 us
  transfers between devices with their start and end apart: 27, of which 10 were waited for; matrix products, arithmetic and copies ran while one was open for 10% of the time, Pallas kernels for 35%

profile of v7, /device:TPU:0, one launch (start us, length us, event | category | flops | bytes accessed | tf_op | source)
XLA Modules:
  0.0 156.9 jit_solution(6186774882256932581)
XLA Ops:
  3.6 3.8 %share_rows.1 = bf16[8,2,64,1024]{3,2,1,0:T(8,128)(2,1)} custom-call(s32[2]{0:T(128)} %pad_add_fusion.4.subs_ref, bf16[512,8192]{1,0:T(8,128)(2,1)} %w_ref.1), custom_call_target="tpu_custom_call" | custom-call | bytes 4194304 | tf_op jit(solution)/shard_map/share_rows/pallas_call | solution.py:460
  7.4 6.6 %all-to-all-start = ((bf16[8,2,64,1024]{3,2,1,0:T(8,128)(2,1)}), bf16[8,2,64,1024]{3,2,1,0:T(8,128)(2,1)S(1)}, u32[]{:S(2)}, u32[]{:S(2)}) async-start(bf16[8,2,64,1024]{3,2,1,0:T(8,128)(2,1)} %share_rows.1), calls=%async_computation | async-start | bytes 4194304 | tf_op jit(solution)/shard_map/all_to_all | solution.py:532
  15.3 1.9 %collective-permute-start.4 = (s32[4,8,128]{2,1,0:T(8,128)S(1)}, s32[4,8,128]{2,1,0:T(8,128)S(1)}, u32[]{:S(2)}, u32[]{:S(2)}) collective-permute-start(s32[4,8,128]{2,1,0:T(8,128)S(1)} %pad_add_fusion.1), channel_id=1, source_target_pairs={{48,0},{56,8},{0,16},{8,24},{16,32},{24,40},{32,48},{40,56},{112,6... | collective-permute-start | bytes 49160 | tf_op jit(solution)/shard_map/ppermute | solution.py:396
  17.2 3.6 %collective-permute-start.3 = (s32[4,8,128]{2,1,0:T(8,128)S(1)}, s32[4,8,128]{2,1,0:T(8,128)S(1)}, u32[]{:S(2)}, u32[]{:S(2)}) collective-permute-start(s32[4,8,128]{2,1,0:T(8,128)S(1)} %pad_add_fusion.1), channel_id=1, source_target_pairs={{32,0},{40,8},{48,16},{56,24},{0,32},{8,40},{16,48},{24,56},{96,64... | collective-permute-start | bytes 49160 | tf_op jit(solution)/shard_map/ppermute | solution.py:396
  22.5 9.3 %attention.1 = bf16[8,4,16,512]{3,2,1,0:T(8,128)(2,1)} custom-call(s32[128,128]{1,0:T(8,128)} %broadcast_in_dim.4.len_ref, bf16[4,128,512]{2,1,0:T(8,128)(2,1)} %q_ref, bf16[128,64,128]{2,1,0:T(8,128)(2,1)} %ck_ref.1, bf16[128,64,128]{2,1,0:T(8,128)(2,1)} %cv_ref.1, bf16[4,128,128]{2,1,0:T(8,128)(2,1)} %nk_ref.1, bf16[4,128,128]{2,1,0:T(8,128)(2,1)} %nv_ref.1), custom_call_target="tpu_custom_call" | custom-call | flops 8000000000 | bytes 6291456 | tf_op jit(solution)/shard_map/attention/pallas_call | solution.py:84
  31.8 3.5 %collective-permute-start.8 = (bf16[512,512]{1,0:T(8,128)(2,1)}, bf16[512,512]{1,0:T(8,128)(2,1)S(1)}, u32[]{:S(2)}, u32[]{:S(2)}) collective-permute-start(bf16[512,512]{1,0:T(8,128)(2,1)} %bitcast.39), channel_id=1, source_target_pairs={{0,1},{1,0},{2,3},{3,2},{4,5},{5,4},{6,7},{7,6},{8,9},{9,8},{10,11... | collective-permute-start | bytes 1572872 | tf_op jit(solution)/shard_map/ppermute | solution.py:417
  35.4 3.0 %collective-permute-start.7 = (bf16[512,512]{1,0:T(8,128)(2,1)}, bf16[512,512]{1,0:T(8,128)(2,1)}, u32[]{:S(2)}, u32[]{:S(2)}) collective-permute-start(bf16[512,512]{1,0:T(8,128)(2,1)} %bitcast.40), channel_id=1, source_target_pairs={{0,4},{1,5},{2,6},{3,7},{4,0},{5,1},{6,2},{7,3},{8,12},{9,13},{10,... | collective-permute-start | bytes 1572872 | tf_op jit(solution)/shard_map/ppermute | solution.py:417
  40.4 14.5 %look_up.3.refs_0_ = bf16[128,32,128]{2,1,0:T(8,128)(2,1)S(1)} custom-call(s32[1]{0:T(128)} %bitcast.13.shift_ref, s32[16]{0:T(128)S(1)} %fusion.36.spot_ref, s32[16384]{0:T(1024)S(1)} %bitcast.33, bf16[28,76032]{1,0:T(8,128)(2,1)} %table_ref.3), custom_call_target="tpu_custom_call" | custom-call | bytes 79691776 | tf_op jit(solution)/shard_map/look_up/pallas_call | solution.py:176
  60.5 6.4 %look_up.4.refs_0_ = bf16[128,32,128]{2,1,0:T(8,128)(2,1)S(1)} custom-call(s32[1]{0:T(128)} %bitcast.13.shift_ref, s32[16]{0:T(128)S(1)} %fusion.36.spot_ref, s32[16384]{0:T(1024)S(1)} %bitcast.34, bf16[28,8448]{1,0:T(8,128)(2,1)S(1)} %copy-done.2, bf16[128,32,128]{2,1,0:T(8,128)(2,1)S(1)} %copy-done.1), custom_call_target="tpu_custom_call" | custom-call | bytes 8388608 | tf_op jit(solution)/shard_map/look_up/pallas_call | solution.py:176
  72.8 7.3 %look_up.5 = bf16[128,32,128]{2,1,0:T(8,128)(2,1)} custom-call(s32[1]{0:T(128)} %bitcast.13.shift_ref, s32[16]{0:T(128)S(1)} %fusion.36.spot_ref, s32[16384]{0:T(1024)S(1)} %bitcast.35, bf16[28,8448]{1,0:T(8,128)(2,1)S(1)} %copy-done.3, bf16[128,32,128]{2,1,0:T(8,128)(2,1)S(1)} %look_up.4.refs_0_), custom_call_target="tpu_custom_call" | custom-call | bytes 8388608 | tf_op jit(solution)/shard_map/look_up/pallas_call | solution.py:176
  80.1 2.8 %collective-permute-done.11.refs_7_ = bf16[512,512]{1,0:T(8,128)(2,1)} collective-permute-done((bf16[512,512]{1,0:T(8,128)(2,1)}, bf16[512,512]{1,0:T(8,128)(2,1)}, u32[]{:S(2)}, u32[]{:S(2)}) %collective-permute-start.11) | collective-permute-done | bytes 524320 | tf_op jit(solution)/shard_map/ppermute | solution.py:417
  84.2 6.4 %collect_rows.1 = (bf16[512,4096]{1,0:T(8,128)(2,1)}, bf16[8,4,16,1024]{3,2,1,0:T(8,128)(2,1)}, f32[8,128]{1,0:T(8,128)}) custom-call(s32[8]{0:T(128)} %stack.76.order_ref, s32[8]{0:T(128)} %fusion.33.spot_ref, bf16[512,512]{1,0:T(8,128)(2,1)} %bitcast.43, bf16[512,512]{1,0:T(8,128)(2,1)} %collective-permute-done.5.refs_1_, ...), custom_call_target="tpu_custom_call" | custom-call | bytes 8388608 | tf_op jit(solution)/shard_map/collect_rows/pallas_call | solution.py:222
  91.3 7.7 %all-to-all-start.1 = ((bf16[128,32,128]{2,1,0:T(8,128)(2,1)}), bf16[128,32,128]{2,1,0:T(8,128)(2,1)S(1)}, u32[]{:S(2)}, u32[]{:S(2)}) async-start(bf16[128,32,128]{2,1,0:T(8,128)(2,1)} %look_up.5), calls=%async_computation.1 | async-start | bytes 2097152 | tf_op jit(solution)/shard_map/all_to_all | solution.py:549
  99.7 3.9 %collect_weight.1 = bf16[8,8,64,1024]{3,2,1,0:T(8,128)(2,1)S(1)} custom-call(s32[8]{0:T(128)S(1)} %stack.89.subs_ref, f32[8,128]{1,0:T(8,128)S(1)} %copy-done.14, bf16[8,2,64,1024]{3,2,1,0:T(8,128)(2,1)S(1)} %all-to-all-done.refs_0_, bf16[8,1,64,1024]{3,2,1,0:T(8,128)(2,1)} %collective-permute-done.12.refs_1_, ...), custom_call_target="tpu_custom_call" | custom-call | bytes 10485760 | tf_op jit(solution)/shard_map/collect_weight/pallas_call | solution.py:285
  104.1 4.5 %fusion.12 = bf16[512,1024]{1,0:T(8,128)(2,1)S(1)} fusion(bf16[8,4,16,1024]{3,2,1,0:T(8,128)(2,1)S(1)} %copy-done.20, bf16[512,4096]{1,0:T(8,128)(2,1)S(1)} %copy-done.19, bf16[4096,1024]{1,0:T(8,128)(2,1)S(1)} %bitcast.32), kind=kOutput, calls=%fused_computation.17 | convolution fusion | flops 4296540160 | bytes 14680064 | tf_op jit(solution)/shard_map/dot_general | solution.py:551
  110.7 2.1 %collective-permute-start.22 = (bf16[128,1792]{1,0:T(8,128)(2,1)S(1)}, bf16[128,1792]{1,0:T(8,128)(2,1)S(1)}, u32[]{:S(2)}, u32[]{:S(2)}) collective-permute-start(bf16[128,1792]{1,0:T(8,128)(2,1)S(1)} %convolution_convert_fusion), channel_id=1, source_target_pairs={{0,6},{1,7},{2,0},{3,1},{4,2},{5,3},{6,4},{7,5},{8,14},{9,15},{10,... | collective-permute-start | bytes 1376264 | tf_op jit(solution)/shard_map/ppermute | solution.py:417
  115.0 7.9 %collective-permute-done.22 = bf16[128,1792]{1,0:T(8,128)(2,1)S(1)} collective-permute-done((bf16[128,1792]{1,0:T(8,128)(2,1)S(1)}, bf16[128,1792]{1,0:T(8,128)(2,1)S(1)}, u32[]{:S(2)}, u32[]{:S(2)}) %collective-permute-start.22) | collective-permute-done | bytes 458784 | tf_op jit(solution)/shard_map/ppermute | solution.py:417
  123.5 3.8 %collective-permute-start.23 = (bf16[128,1792]{1,0:T(8,128)(2,1)S(1)}, bf16[128,1792]{1,0:T(8,128)(2,1)S(1)}, u32[]{:S(2)}, u32[]{:S(2)}) collective-permute-start(bf16[128,1792]{1,0:T(8,128)(2,1)S(1)} %add_convert_fusion), channel_id=1, source_target_pairs={{0,6},{1,7},{2,0},{3,1},{4,2},{5,3},{6,4},{7,5},{8,14},{9,15},{10,... | collective-permute-start | bytes 1376264 | tf_op jit(solution)/shard_map/ppermute | solution.py:417
  128.8 2.0 %collective-permute-start.18 = (bf16[128,1792]{1,0:T(8,128)(2,1)S(1)}, bf16[128,1792]{1,0:T(8,128)(2,1)S(1)}, u32[]{:S(2)}, u32[]{:S(2)}) collective-permute-start(bf16[128,1792]{1,0:T(8,128)(2,1)S(1)} %add_convert_fusion.1), channel_id=1, source_target_pairs={{0,2},{1,3},{2,4},{3,5},{4,6},{5,7},{6,0},{7,1},{8,10},{9,11},{10,... | collective-permute-start | bytes 1376264 | tf_op jit(solution)/shard_map/ppermute | solution.py:417
  130.8 7.1 %collective-permute-done.21.refs_5_ = bf16[128,1792]{1,0:T(8,128)(2,1)S(1)} collective-permute-done((bf16[128,1792]{1,0:T(8,128)(2,1)S(1)}, bf16[128,1792]{1,0:T(8,128)(2,1)S(1)}, u32[]{:S(2)}, u32[]{:S(2)}) %collective-permute-start.21) | collective-permute-done | bytes 458784 | tf_op jit(solution)/shard_map/ppermute | solution.py:417
  139.1 3.0 %collective-permute-start.24 = (bf16[64,1792]{1,0:T(8,128)(2,1)}, bf16[64,1792]{1,0:T(8,128)(2,1)S(1)}, u32[]{:S(2)}, u32[]{:S(2)}) collective-permute-start(bf16[64,1792]{1,0:T(8,128)(2,1)} %fusion.14), channel_id=1, source_target_pairs={{0,1},{1,0},{2,3},{3,2},{4,5},{5,4},{6,7},{7,6},{8,9},{9,8},{10,11... | collective-permute-start | bytes 688136 | tf_op jit(solution)/shard_map/ppermute | solution.py:417
  142.1 4.2 %collective-permute-done.19.refs_2_ = bf16[128,1792]{1,0:T(8,128)(2,1)S(1)} collective-permute-done((bf16[128,1792]{1,0:T(8,128)(2,1)S(1)}, bf16[128,1792]{1,0:T(8,128)(2,1)S(1)}, u32[]{:S(2)}, u32[]{:S(2)}) %collective-permute-start.19) | collective-permute-done | bytes 458784 | tf_op jit(solution)/shard_map/ppermute | solution.py:417
  147.5 3.0 %collective-permute-start.20 = (bf16[64,1792]{1,0:T(8,128)(2,1)}, bf16[64,1792]{1,0:T(8,128)(2,1)S(1)}, u32[]{:S(2)}, u32[]{:S(2)}) collective-permute-start(bf16[64,1792]{1,0:T(8,128)(2,1)} %fusion.16), channel_id=1, source_target_pairs={{0,1},{1,0},{2,3},{3,2},{4,5},{5,4},{6,7},{7,6},{8,9},{9,8},{10,11... | collective-permute-start | bytes 688136 | tf_op jit(solution)/shard_map/ppermute | solution.py:417
  152.7 1.8 %restore.1 = bf16[4,8,16,1024]{3,2,1,0:T(8,128)(2,1)} custom-call(s32[8]{0:T(128)S(1)} %copy-done.15, bf16[8,4,16,1024]{3,2,1,0:T(8,128)(2,1)S(1)} %bitcast.36), custom_call_target="tpu_custom_call" | custom-call | bytes 2097152 | tf_op jit(solution)/shard_map/restore/pallas_call | solution.py:254
  (110 shorter events, 35.6 us)
Async XLA Ops:
  7.4 48.6 %all-to-all-start = ((bf16[8,2,64,1024]{3,2,1,0:T(8,128)(2,1)}), bf16[8,2,64,1024]{3,2,1,0:T(8,128)(2,1)S(1)}, u32[]{:S(2)}, u32[]{:S(2)}) async-start(bf16[8,2,64,1024]{3,2,1,0:T(8,128)(2,1)} %share_rows.1), calls=%async_computation | async-start | bytes 4194304 | tf_op jit(solution)/shard_map/all_to_all | solution.py:532
  15.3 16.5 %collective-permute-start.4 = (s32[4,8,128]{2,1,0:T(8,128)S(1)}, s32[4,8,128]{2,1,0:T(8,128)S(1)}, u32[]{:S(2)}, u32[]{:S(2)}) collective-permute-start(s32[4,8,128]{2,1,0:T(8,128)S(1)} %pad_add_fusion.1), channel_id=1, source_target_pairs={{48,0},{56,8},{0,16},{8,24},{16,32},{24,40},{32,48},{40,56},{112,6... | collective-permute-start | bytes 49160 | tf_op jit(solution)/shard_map/ppermute | solution.py:396
  17.2 14.6 %collective-permute-start.3 = (s32[4,8,128]{2,1,0:T(8,128)S(1)}, s32[4,8,128]{2,1,0:T(8,128)S(1)}, u32[]{:S(2)}, u32[]{:S(2)}) collective-permute-start(s32[4,8,128]{2,1,0:T(8,128)S(1)} %pad_add_fusion.1), channel_id=1, source_target_pairs={{32,0},{40,8},{48,16},{56,24},{0,32},{8,40},{16,48},{24,56},{96,64... | collective-permute-start | bytes 49160 | tf_op jit(solution)/shard_map/ppermute | solution.py:396
  20.8 11.0 %collective-permute-start.2 = (s32[4,8,128]{2,1,0:T(8,128)S(1)}, s32[4,8,128]{2,1,0:T(8,128)S(1)}, u32[]{:S(2)}, u32[]{:S(2)}) collective-permute-start(s32[4,8,128]{2,1,0:T(8,128)S(1)} %pad_add_fusion.1), channel_id=1, source_target_pairs={{16,0},{24,8},{32,16},{40,24},{48,32},{56,40},{0,48},{8,56},{80,64... | collective-permute-start | bytes 49160 | tf_op jit(solution)/shard_map/ppermute | solution.py:396
  31.8 25.7 %collective-permute-start.8 = (bf16[512,512]{1,0:T(8,128)(2,1)}, bf16[512,512]{1,0:T(8,128)(2,1)S(1)}, u32[]{:S(2)}, u32[]{:S(2)}) collective-permute-start(bf16[512,512]{1,0:T(8,128)(2,1)} %bitcast.39), channel_id=1, source_target_pairs={{0,1},{1,0},{2,3},{3,2},{4,5},{5,4},{6,7},{7,6},{8,9},{9,8},{10,11... | collective-permute-start | bytes 1572872 | tf_op jit(solution)/shard_map/ppermute | solution.py:417
  35.4 31.5 %collective-permute-start.7 = (bf16[512,512]{1,0:T(8,128)(2,1)}, bf16[512,512]{1,0:T(8,128)(2,1)}, u32[]{:S(2)}, u32[]{:S(2)}) collective-permute-start(bf16[512,512]{1,0:T(8,128)(2,1)} %bitcast.40), channel_id=1, source_target_pairs={{0,4},{1,5},{2,6},{3,7},{4,0},{5,1},{6,2},{7,3},{8,12},{9,13},{10,... | collective-permute-start | bytes 1572872 | tf_op jit(solution)/shard_map/ppermute | solution.py:417
  38.4 28.4 %collective-permute-start.6 = (bf16[512,512]{1,0:T(8,128)(2,1)}, bf16[512,512]{1,0:T(8,128)(2,1)}, u32[]{:S(2)}, u32[]{:S(2)}) collective-permute-start(bf16[512,512]{1,0:T(8,128)(2,1)} %bitcast.41), channel_id=1, source_target_pairs={{0,6},{1,7},{2,0},{3,1},{4,2},{5,3},{6,4},{7,5},{8,14},{9,15},{10,... | collective-permute-start | bytes 1572872 | tf_op jit(solution)/shard_map/ppermute | solution.py:417
  39.6 27.6 %collective-permute-start.5 = (bf16[512,512]{1,0:T(8,128)(2,1)}, bf16[512,512]{1,0:T(8,128)(2,1)}, u32[]{:S(2)}, u32[]{:S(2)}) collective-permute-start(bf16[512,512]{1,0:T(8,128)(2,1)} %bitcast.42), channel_id=1, source_target_pairs={{0,2},{1,3},{2,4},{3,5},{4,6},{5,7},{6,0},{7,1},{8,10},{9,11},{10,... | collective-permute-start | bytes 1572872 | tf_op jit(solution)/shard_map/ppermute | solution.py:417
  57.6 33.0 %collective-permute-start.13 = (bf16[8,1,64,1024]{3,2,1,0:T(8,128)(2,1)}, bf16[8,1,64,1024]{3,2,1,0:T(8,128)(2,1)}, u32[]{:S(2)}, u32[]{:S(2)}) collective-permute-start(bf16[8,1,64,1024]{3,2,1,0:T(8,128)(2,1)} %get-tuple-element.44), channel_id=1, source_target_pairs={{0,48},{8,56},{16,32},{24,40},{32,16},{40,24},{48,0},{56,8},{64,11... | collective-permute-start | bytes 3145736 | tf_op jit(solution)/shard_map/ppermute | solution.py:493
  58.4 32.2 %collective-permute-start.12 = (bf16[8,1,64,1024]{3,2,1,0:T(8,128)(2,1)}, bf16[8,1,64,1024]{3,2,1,0:T(8,128)(2,1)}, u32[]{:S(2)}, u32[]{:S(2)}) collective-permute-start(bf16[8,1,64,1024]{3,2,1,0:T(8,128)(2,1)} %get-tuple-element.45), channel_id=1, source_target_pairs={{0,16},{8,24},{16,0},{24,8},{32,48},{40,56},{48,32},{56,40},{64,80... | collective-permute-start | bytes 3145736 | tf_op jit(solution)/shard_map/ppermute | solution.py:492
  67.2 15.7 %collective-permute-start.11 = (bf16[512,512]{1,0:T(8,128)(2,1)}, bf16[512,512]{1,0:T(8,128)(2,1)}, u32[]{:S(2)}, u32[]{:S(2)}) collective-permute-start(bf16[512,512]{1,0:T(8,128)(2,1)} %collective-permute-done.7.refs_3_), channel_id=1, source_target_pairs={{0,1},{1,0},{2,3},{3,2},{4,5},{5,4},{6,7},{7,6},{8,9},{9,8},{10,11... | collective-permute-start | bytes 1572872 | tf_op jit(solution)/shard_map/ppermute | solution.py:417
  68.5 14.4 %collective-permute-start.10 = (bf16[512,512]{1,0:T(8,128)(2,1)}, bf16[512,512]{1,0:T(8,128)(2,1)}, u32[]{:S(2)}, u32[]{:S(2)}) collective-permute-start(bf16[512,512]{1,0:T(8,128)(2,1)} %copy-done.16), channel_id=1, source_target_pairs={{0,6},{1,7},{2,0},{3,1},{4,2},{5,3},{6,4},{7,5},{8,14},{9,15},{10,... | collective-permute-start | bytes 1572872 | tf_op jit(solution)/shard_map/ppermute | solution.py:417
  69.9 14.3 %collective-permute-start.9 = (bf16[512,512]{1,0:T(8,128)(2,1)}, bf16[512,512]{1,0:T(8,128)(2,1)}, u32[]{:S(2)}, u32[]{:S(2)}) collective-permute-start(bf16[512,512]{1,0:T(8,128)(2,1)} %copy-done.16), channel_id=1, source_target_pairs={{0,2},{1,3},{2,4},{3,5},{4,6},{5,7},{6,0},{7,1},{8,10},{9,11},{10,... | collective-permute-start | bytes 1572872 | tf_op jit(solution)/shard_map/ppermute | solution.py:417
  90.6 8.5 %collective-permute-start.14 = (bf16[8,2,64,1024]{3,2,1,0:T(8,128)(2,1)S(1)}, bf16[8,2,64,1024]{3,2,1,0:T(8,128)(2,1)}, u32[]{:S(2)}, u32[]{:S(2)}) collective-permute-start(bf16[8,2,64,1024]{3,2,1,0:T(8,128)(2,1)S(1)} %all-to-all-done.refs_0_), channel_id=1, source_target_pairs={{0,8},{8,0},{16,24},{24,16},{32,40},{40,32},{48,56},{56,48},{64,72... | collective-permute-start | bytes 6291464 | tf_op jit(solution)/shard_map/ppermute | solution.py:499
  90.6 8.4 %collective-permute-start.15 = (bf16[8,1,64,1024]{3,2,1,0:T(8,128)(2,1)}, bf16[8,1,64,1024]{3,2,1,0:T(8,128)(2,1)}, u32[]{:S(2)}, u32[]{:S(2)}) collective-permute-start(bf16[8,1,64,1024]{3,2,1,0:T(8,128)(2,1)} %collective-permute-done.12.refs_1_), channel_id=1, source_target_pairs={{0,8},{8,0},{16,24},{24,16},{32,40},{40,32},{48,56},{56,48},{64,72... | collective-permute-start | bytes 3145736 | tf_op jit(solution)/shard_map/ppermute | solution.py:499
  91.3 59.2 %all-to-all-start.1 = ((bf16[128,32,128]{2,1,0:T(8,128)(2,1)}), bf16[128,32,128]{2,1,0:T(8,128)(2,1)S(1)}, u32[]{:S(2)}, u32[]{:S(2)}) async-start(bf16[128,32,128]{2,1,0:T(8,128)(2,1)} %look_up.5), calls=%async_computation.1 | async-start | bytes 2097152 | tf_op jit(solution)/shard_map/all_to_all | solution.py:549
  110.7 12.2 %collective-permute-start.22 = (bf16[128,1792]{1,0:T(8,128)(2,1)S(1)}, bf16[128,1792]{1,0:T(8,128)(2,1)S(1)}, u32[]{:S(2)}, u32[]{:S(2)}) collective-permute-start(bf16[128,1792]{1,0:T(8,128)(2,1)S(1)} %convolution_convert_fusion), channel_id=1, source_target_pairs={{0,6},{1,7},{2,0},{3,1},{4,2},{5,3},{6,4},{7,5},{8,14},{9,15},{10,... | collective-permute-start | bytes 1376264 | tf_op jit(solution)/shard_map/ppermute | solution.py:417
  113.4 14.7 %collective-permute-start.17 = (bf16[128,1792]{1,0:T(8,128)(2,1)S(1)}, bf16[128,1792]{1,0:T(8,128)(2,1)S(1)}, u32[]{:S(2)}, u32[]{:S(2)}) collective-permute-start(bf16[128,1792]{1,0:T(8,128)(2,1)S(1)} %convolution_convert_fusion.3), channel_id=1, source_target_pairs={{0,2},{1,3},{2,4},{3,5},{4,6},{5,7},{6,0},{7,1},{8,10},{9,11},{10,... | collective-permute-start | bytes 1376264 | tf_op jit(solution)/shard_map/ppermute | solution.py:417
  113.5 24.4 %collective-permute-start.21 = (bf16[128,1792]{1,0:T(8,128)(2,1)S(1)}, bf16[128,1792]{1,0:T(8,128)(2,1)S(1)}, u32[]{:S(2)}, u32[]{:S(2)}) collective-permute-start(bf16[128,1792]{1,0:T(8,128)(2,1)S(1)} %convolution_convert_fusion.1), channel_id=1, source_target_pairs={{0,2},{1,3},{2,4},{3,5},{4,6},{5,7},{6,0},{7,1},{8,10},{9,11},{10,... | collective-permute-start | bytes 1376264 | tf_op jit(solution)/shard_map/ppermute | solution.py:417
  123.5 14.7 %collective-permute-start.23 = (bf16[128,1792]{1,0:T(8,128)(2,1)S(1)}, bf16[128,1792]{1,0:T(8,128)(2,1)S(1)}, u32[]{:S(2)}, u32[]{:S(2)}) collective-permute-start(bf16[128,1792]{1,0:T(8,128)(2,1)S(1)} %add_convert_fusion), channel_id=1, source_target_pairs={{0,6},{1,7},{2,0},{3,1},{4,2},{5,3},{6,4},{7,5},{8,14},{9,15},{10,... | collective-permute-start | bytes 1376264 | tf_op jit(solution)/shard_map/ppermute | solution.py:417
  128.0 18.4 %collective-permute-start.19 = (bf16[128,1792]{1,0:T(8,128)(2,1)S(1)}, bf16[128,1792]{1,0:T(8,128)(2,1)S(1)}, u32[]{:S(2)}, u32[]{:S(2)}) collective-permute-start(bf16[128,1792]{1,0:T(8,128)(2,1)S(1)} %convolution_convert_fusion.2), channel_id=1, source_target_pairs={{0,6},{1,7},{2,0},{3,1},{4,2},{5,3},{6,4},{7,5},{8,14},{9,15},{10,... | collective-permute-start | bytes 1376264 | tf_op jit(solution)/shard_map/ppermute | solution.py:417
  128.8 17.9 %collective-permute-start.18 = (bf16[128,1792]{1,0:T(8,128)(2,1)S(1)}, bf16[128,1792]{1,0:T(8,128)(2,1)S(1)}, u32[]{:S(2)}, u32[]{:S(2)}) collective-permute-start(bf16[128,1792]{1,0:T(8,128)(2,1)S(1)} %add_convert_fusion.1), channel_id=1, source_target_pairs={{0,2},{1,3},{2,4},{3,5},{4,6},{5,7},{6,0},{7,1},{8,10},{9,11},{10,... | collective-permute-start | bytes 1376264 | tf_op jit(solution)/shard_map/ppermute | solution.py:417
  139.1 15.4 %collective-permute-start.24 = (bf16[64,1792]{1,0:T(8,128)(2,1)}, bf16[64,1792]{1,0:T(8,128)(2,1)S(1)}, u32[]{:S(2)}, u32[]{:S(2)}) collective-permute-start(bf16[64,1792]{1,0:T(8,128)(2,1)} %fusion.14), channel_id=1, source_target_pairs={{0,1},{1,0},{2,3},{3,2},{4,5},{5,4},{6,7},{7,6},{8,9},{9,8},{10,11... | collective-permute-start | bytes 688136 | tf_op jit(solution)/shard_map/ppermute | solution.py:417
  147.5 8.2 %collective-permute-start.20 = (bf16[64,1792]{1,0:T(8,128)(2,1)}, bf16[64,1792]{1,0:T(8,128)(2,1)S(1)}, u32[]{:S(2)}, u32[]{:S(2)}) collective-permute-start(bf16[64,1792]{1,0:T(8,128)(2,1)} %fusion.16), channel_id=1, source_target_pairs={{0,1},{1,0},{2,3},{3,2},{4,5},{5,4},{6,7},{7,6},{8,9},{9,8},{10,11... | collective-permute-start | bytes 688136 | tf_op jit(solution)/shard_map/ppermute | solution.py:417
  (26 other events, 179.6 us)
